TPU v7x, 32 devices: a whole 2x2x4 slice. The times are simulated.
32 devices in a mesh: rep: 4 (over x, core), shard: 8 (over z, y).
Axes of the slice: x: 2, y: 2, z: 4, core: 2. Of those that a mesh axis runs over, the one named last changes fastest.
Arguments:
- tokens: bfloat16 [64, 1024, 768], P(('rep', 'shard')), may hold values from -6 to 6
- cotangent: bfloat16 [64, 1024, 768], P(('rep', 'shard')), may hold values from -6 to 6
- lengths: int32 [64], P(('rep', 'shard')), may hold values from 256 to 1024, as said below
- widen_weight: bfloat16 [768, 3328], P('shard'), may hold values from -0.21875 to 0.21875
- timestep_weight: bfloat16 [768, 48], P('shard'), may hold values from -0.21875 to 0.21875
- narrow_weight: bfloat16 [1536, 768], P('shard'), may hold values from -0.15625 to 0.15625
- filter_weight: bfloat16 [4, 1792], P(None, 'shard'), may hold values from -3 to 3
- filter_offset: bfloat16 [1792], P('shard'), may hold values from -3 to 3
- prenorm_gain: bfloat16 [768], P('shard'), may hold values from 0.099609375 to 1.8984375
- postnorm_gain: bfloat16 [1536], P('shard'), may hold values from 0.099609375 to 1.8984375
- timestep_bias: float32 [48], replicated, may hold values from -7 to -2.3
- decay_log: float32 [24], replicated, may hold values from 0 to 2.77
- skip_gain: float32 [24], replicated, may hold values from 0.5 to 1.5
Outputs:
- result: bfloat16 [64, 1024, 768], P(('rep', 'shard'))
- tokens_gradient: bfloat16 [64, 1024, 768], P(('rep', 'shard'))
- widen_gradient: float32 [768, 3328], P('shard')
- timestep_gradient: float32 [768, 48], P('shard')
- narrow_gradient: float32 [1536, 768], P('shard')
- filter_gradient: float32 [4, 1792], P(None, 'shard')
- offset_gradient: float32 [1792], P('shard')
- prenorm_gradient: float32 [768], P('shard')
- postnorm_gradient: float32 [1536], P('shard')
- bias_gradient: float32 [48], replicated
- decay_gradient: float32 [24], replicated
- skip_gradient: float32 [24], replicated
Inputs may be any that keep to these rules, and one draw needn't show every extreme that they name: `lengths`: each length lies between a quarter of 1024 and 1024; some sequence has exactly 1024.
All inputs are finite; a program needn't handle non-finite values.
Results may differ from a plain program's by a relative error of at most 0.0082.
Values may be sent and summed in bfloat16 or wider, within the bound.
A program may use at most 384 MiB of HBM per device.

v0:
```python
from functools import partial

import jax
import jax.numpy as jnp
from jax import lax
from jax.sharding import PartitionSpec as P

HEADS = 24
HEADDIM = 64
STATE = 64
CONV = 4
SPAN = 256
INNER = 1536


epsilon = 1e-05
precise = lax.Precision.HIGHEST


def normalize(values, gain):
    return values * lax.rsqrt(jnp.mean(values * values, axis=-1, keepdims=True) + epsilon) * gain


def span_scan(values, steps, rate, inputs_b, outputs_c):
    length = values.shape[0]
    count = length // SPAN
    lower = lax.broadcasted_iota(jnp.int32, (SPAN, SPAN), 0) > lax.broadcasted_iota(
        jnp.int32, (SPAN, SPAN), 1
    )

    def advance(state, pieces):
        value_piece, step_piece, input_piece, output_piece = pieces
        cums = jnp.cumsum(step_piece * rate, axis=0).T
        spread = cums[:, :, None] - cums[:, None, :]
        decay = jnp.where(lower, jnp.exp(jnp.where(lower, spread, 0.0)), 0.0)
        scores = jnp.dot(output_piece, input_piece.T, precision=precise)
        weights = decay * scores[None] * step_piece.T[:, None, :]
        inside = jnp.einsum("hts,shp->thp", weights, value_piece, precision=precise)
        carried = (
            jnp.einsum("tn,hnp->thp", output_piece, state, precision=precise)
            * jnp.exp(cums.T)[:, :, None]
        )
        tail = jnp.exp(cums[:, -1:] - cums).T * step_piece
        fresh = jnp.einsum("sh,sn,shp->hnp", tail, input_piece, value_piece, precision=precise)
        state = state * jnp.exp(cums[:, -1])[:, None, None] + fresh
        return (state, inside + carried)

    initial = jnp.zeros((HEADS, STATE, HEADDIM), jnp.float32)
    pieces = (
        values.reshape(count, SPAN, HEADS, HEADDIM),
        steps.reshape(count, SPAN, HEADS),
        inputs_b.reshape(count, SPAN, STATE),
        outputs_c.reshape(count, SPAN, STATE),
    )
    _, outputs = lax.scan(jax.checkpoint(advance), initial, pieces)
    return outputs.reshape(length, HEADS, HEADDIM)


def mixer_block(
    projected,
    raw_steps,
    filter_weight,
    filter_offset,
    timestep_bias,
    decay_log,
    skip_gain,
    postnorm_gain,
    mask,
    scanner,
):
    length = projected.shape[0]
    gate = projected[:, :INNER]
    filter_input = projected[:, INNER:]
    padded = jnp.pad(filter_input, ((CONV - 1, 0), (0, 0)))
    filtered = filter_offset + jnp.zeros_like(filter_input)
    for place in range(CONV):
        filtered = filtered + filter_weight[place] * padded[place : place + length]
    active = jax.nn.silu(filtered)
    values = (active[:, :INNER] * mask).reshape(length, HEADS, HEADDIM)
    forward_in = active[:, INNER : INNER + STATE]
    forward_out = active[:, INNER + STATE : INNER + 2 * STATE]
    reverse_in = active[:, INNER + 2 * STATE : INNER + 3 * STATE]
    reverse_out = active[:, INNER + 3 * STATE :]
    steps = jax.nn.softplus(raw_steps + timestep_bias)
    rate = -jnp.exp(decay_log)
    ahead = scanner(values, steps[:, :HEADS], rate, forward_in, forward_out)
    behind = jnp.flip(
        scanner(
            jnp.flip(values, 0),
            jnp.flip(steps[:, HEADS:], 0),
            rate,
            jnp.flip(reverse_in, 0),
            jnp.flip(reverse_out, 0),
        ),
        0,
    )
    mixed = (ahead + behind + skip_gain[:, None] * values).reshape(length, INNER)
    return normalize(mixed * jax.nn.silu(gate), postnorm_gain)


def contract_rows(left, right):
    return lax.dot_general(
        left, right, (((0,), (0,)), ((), ())), preferred_element_type=jnp.float32
    )


def contract_columns(left, right):
    return lax.dot_general(
        left, right, (((1,), (1,)), ((), ())), preferred_element_type=jnp.float32
    )


def small_sizes(timestep_weight, filter_weight, filter_offset, prenorm_gain, postnorm_gain):
    sizes = [
        timestep_weight.size,
        filter_weight.size,
        filter_offset.size,
        prenorm_gain.size,
        postnorm_gain.size,
    ]
    used = sum(sizes)
    width = (used + 127) // 128 * 128
    return (sizes, used, width)


def pack_own(timestep_weight, filter_weight, filter_offset, prenorm_gain, postnorm_gain, width):
    joined = jnp.concatenate(
        [
            timestep_weight.reshape(-1),
            filter_weight.reshape(-1),
            filter_offset,
            prenorm_gain,
            postnorm_gain,
        ]
    )
    return jnp.pad(joined, (0, width - joined.shape[0]))


def unpack_rows(rows, sizes, conv_taps):
    count = rows.shape[0]
    starts = [0]
    for amount in sizes:
        starts.append(starts[-1] + amount)
    timestep = rows[:, starts[0] : starts[1]].reshape(-1, 2 * HEADS)
    filter_piece = rows[:, starts[1] : starts[2]].reshape(count, conv_taps, -1)
    smoother = jnp.transpose(filter_piece, (1, 0, 2)).reshape(conv_taps, -1)
    shifter = rows[:, starts[2] : starts[3]].reshape(-1)
    prenorm = rows[:, starts[3] : starts[4]].reshape(-1)
    postnorm = rows[:, starts[4] : starts[5]].reshape(-1)
    return (timestep, smoother, shifter, prenorm, postnorm)


def pack_grads(
    timestep_grad, smoother_grad, shifter_grad, prenorm_grad, postnorm_grad, count, width
):
    conv_taps = smoother_grad.shape[0]
    filter_rows = jnp.transpose(smoother_grad.reshape(conv_taps, count, -1), (1, 0, 2)).reshape(
        count, -1
    )
    joined = jnp.concatenate(
        [
            timestep_grad.reshape(count, -1),
            filter_rows,
            shifter_grad.reshape(count, -1),
            prenorm_grad.reshape(count, -1),
            postnorm_grad.reshape(count, -1),
        ],
        axis=1,
    )
    return jnp.pad(joined, ((0, 0), (0, width - joined.shape[1])))


def local(
    tokens,
    cotangent,
    lengths,
    widen_weight,
    timestep_weight,
    narrow_weight,
    filter_weight,
    filter_offset,
    prenorm_gain,
    postnorm_gain,
    timestep_bias,
    decay_log,
    skip_gain,
):
    micro = tokens.shape[0]
    length = tokens.shape[1]
    count = lax.axis_size("shard")
    conv_taps = filter_weight.shape[0]
    positions = lax.iota(jnp.int32, length)
    sizes, used, width = small_sizes(
        timestep_weight, filter_weight, filter_offset, prenorm_gain, postnorm_gain
    )
    own_small = pack_own(
        timestep_weight, filter_weight, filter_offset, prenorm_gain, postnorm_gain, width
    )
    head_totals = (
        jnp.zeros_like(timestep_bias),
        jnp.zeros_like(decay_log),
        jnp.zeros_like(skip_gain),
    )
    shard_totals = None
    outputs = []
    slopes = []
    for index in range(micro):
        gathered = (
            lax.all_gather(widen_weight, "shard", axis=0, tiled=True),
            lax.all_gather(narrow_weight, "shard", axis=0, tiled=True),
            lax.all_gather(own_small, "shard", axis=0, tiled=True),
        )
        widen, narrow = (gathered[0], gathered[1])
        timestep, smoother, shifter, prenorm, postnorm = unpack_rows(
            gathered[2].reshape(count, width), sizes, conv_taps
        )
        mask = (positions < lengths[index]).astype(jnp.float32)[:, None]
        row = tokens[index].astype(jnp.float32)
        normed_full, norm_pull = jax.vjp(normalize, row, prenorm.astype(jnp.float32))
        normed = normed_full.astype(jnp.bfloat16)
        projected = jnp.dot(normed, widen, preferred_element_type=jnp.float32)
        raw_steps = jnp.dot(normed, timestep, preferred_element_type=jnp.float32)
        gnormed_full, mixer_pull = jax.vjp(
            partial(mixer_block, mask=mask, scanner=span_scan),
            projected,
            raw_steps,
            smoother.astype(jnp.float32),
            shifter.astype(jnp.float32),
            timestep_bias,
            decay_log,
            skip_gain,
            postnorm.astype(jnp.float32),
        )
        gnormed = gnormed_full.astype(jnp.bfloat16)
        branch = jnp.dot(gnormed, narrow, preferred_element_type=jnp.float32)
        outputs.append((row + mask * branch).astype(jnp.bfloat16))
        regathered = (
            lax.all_gather(widen_weight, "shard", axis=0, tiled=True),
            lax.all_gather(narrow_weight, "shard", axis=0, tiled=True),
            lax.all_gather(own_small, "shard", axis=0, tiled=True),
        )
        widen_back, narrow_back = (regathered[0], regathered[1])
        timestep_back = unpack_rows(regathered[2].reshape(count, width), sizes, conv_taps)[0]
        slope_full = cotangent[index].astype(jnp.float32)
        slope = (slope_full * mask).astype(jnp.bfloat16)
        narrow_grad = contract_rows(gnormed, slope)
        gnormed_grad = contract_columns(slope, narrow_back)
        (
            projected_grad,
            steps_grad,
            smoother_grad,
            shifter_grad,
            bias_grad,
            decay_grad,
            skip_grad,
            postnorm_grad,
        ) = mixer_pull(gnormed_grad)
        projected_low = projected_grad.astype(jnp.bfloat16)
        steps_low = steps_grad.astype(jnp.bfloat16)
        widen_grad = contract_rows(normed, projected_low)
        timestep_grad = contract_rows(normed, steps_low)
        normed_grad = contract_columns(projected_low, widen_back) + contract_columns(
            steps_low, timestep_back
        )
        row_grad, prenorm_grad = norm_pull(normed_grad)
        slopes.append((slope_full + row_grad).astype(jnp.bfloat16))
        head_totals = (
            head_totals[0] + bias_grad,
            head_totals[1] + decay_grad,
            head_totals[2] + skip_grad,
        )
        small_grad = pack_grads(
            timestep_grad, smoother_grad, shifter_grad, prenorm_grad, postnorm_grad, count, width
        )
        shares = (
            lax.psum_scatter(widen_grad, "shard", scatter_dimension=0, tiled=True),
            lax.psum_scatter(narrow_grad, "shard", scatter_dimension=0, tiled=True),
            lax.psum_scatter(small_grad, "shard", scatter_dimension=0, tiled=True),
        )
        if shard_totals is None:
            shard_totals = shares
        else:
            shard_totals = tuple((total + share for total, share in zip(shard_totals, shares)))
    summed = lax.psum((shard_totals[0], shard_totals[1], shard_totals[2]), "rep")
    heads_summed = lax.psum((head_totals[0], head_totals[1], head_totals[2]), ("rep", "shard"))
    timestep_out, filter_out, offset_out, prenorm_out, postnorm_out = unpack_rows(
        summed[2], sizes, conv_taps
    )
    return (
        jnp.stack(outputs),
        jnp.stack(slopes),
        summed[0],
        timestep_out,
        summed[1],
        filter_out,
        offset_out,
        prenorm_out,
        postnorm_out,
        heads_summed[0],
        heads_summed[1],
        heads_summed[2],
    )


def solution(mesh):
    placed = (
        P(("rep", "shard"), None, None),
        P(("rep", "shard"), None, None),
        P(("rep", "shard")),
        P("shard", None),
        P("shard", None),
        P("shard", None),
        P(None, "shard"),
        P("shard"),
        P("shard"),
        P("shard"),
        P(),
        P(),
        P(),
    )
    return jax.shard_map(
        local,
        mesh=mesh,
        in_specs=placed,
        out_specs=(
            P(("rep", "shard"), None, None),
            P(("rep", "shard"), None, None),
            P("shard", None),
            P("shard", None),
            P("shard", None),
            P(None, "shard"),
            P("shard"),
            P("shard"),
            P("shard"),
            P(),
            P(),
            P(),
        ),
        check_vma=False,
    )
```

profile of v0, /device:TPU:0, one launch (start us, length us, event | category | flops | bytes accessed | tf_op | source)
XLA Modules:
  0.0 3774.7 jit_solution(6437284531543065062)
XLA Ops:
  12.6 33.0 all-gather
  81.1 70.0 %all-gather.4.cloned.1.call-done = bf16[768,3328]{1,0:T(8,128)(2,1)} async-done(((bf16[96,3328]{1,0:T(8,128)(2,1)}), bf16[768,3328]{1,0:T(8,128)(2,1)}) %all-gather.4.cloned.1.call-update) | async-done | bytes 5111824 | tf_op jit(solution)/shard_map/all_gather | solution.py:209
  183.2 28.5 fusion.417
  256.7 229.5 %while.176 = (s32[]{:T(128)}, f32[24,64,64]{2,1,0:T(8,128)S(1)}, f32[4,256,24,64]{1,0,3,2:T(4,128)}, f32[4,24,64,64]{3,2,1,0:T(8,128)}, f32[4,256,24]{1,2,0:T(8,...) while((s32[]{:T(128)}, f32[24,64,64]{2,1,0:T(8,128)S(1)}, ...), condition=%wide.region_4.6_spmd.clone.clone, body=%wide.region_1.5_spmd.clone.clone.sunk | while | flops 1872427008 | bytes 19123836 | solution.py:55
  279.9 34.5 dynamic_update_slice.281
  337.1 34.5 dynamic_update_slice.281
  394.4 34.5 dynamic_update_slice.281
  451.7 34.5 dynamic_update_slice.281
  521.6 229.3 %while.177 = (s32[]{:T(128)}, f32[24,64,64]{2,1,0:T(8,128)S(1)}, f32[4,256,24,64]{1,0,3,2:T(4,128)}, f32[4,24,64,64]{3,2,1,0:T(8,128)}, f32[4,256,24]{1,2,0:T(8,...) while((s32[]{:T(128)}, f32[24,64,64]{2,1,0:T(8,128)S(1)}, ...), condition=%wide.region_8.10_spmd.clone.clone, body=%wide.region_5.9_spmd.clone.clone.sunk | while | flops 1872427008 | bytes 19123836 | solution.py:55
  544.5 34.5 dynamic_update_slice.283
  601.8 34.5 dynamic_update_slice.283
  659.0 34.5 dynamic_update_slice.283
  716.3 34.5 dynamic_update_slice.283
  800.9 229.1 %while.178 = (s32[]{:T(128)}, f32[24,64,64]{2,1,0:T(8,128)S(1)}, f32[4,256,24,64]{1,0,3,2:T(4,128)}, f32[4,24,64,64]{3,2,1,0:T(8,128)}, f32[4,256,24]{1,2,0:T(8,...) while((s32[]{:T(128)}, f32[24,64,64]{2,1,0:T(8,128)S(1)}, ...), condition=%wide.region_14.16_spmd.clone.clone, body=%wide.region_11.15_spmd.clone.clone.sunk | while | flops 1872427008 | bytes 19123836 | solution.py:55
  823.6 34.5 dynamic_update_slice.285
  880.9 34.5 dynamic_update_slice.285
  938.2 34.5 dynamic_update_slice.285
  995.5 34.5 dynamic_update_slice.285
  1066.0 229.2 %while.179 = (s32[]{:T(128)}, f32[24,64,64]{2,1,0:T(8,128)S(1)}, f32[4,256,24,64]{1,0,3,2:T(4,128)}, f32[4,24,64,64]{3,2,1,0:T(8,128)}, f32[4,256,24]{1,2,0:T(8,...) while((s32[]{:T(128)}, f32[24,64,64]{2,1,0:T(8,128)S(1)}, ...), condition=%wide.region_18.20_spmd.clone.clone, body=%wide.region_15.19_spmd.clone.clone.sunk | while | flops 1872427008 | bytes 19123836 | solution.py:55
  1088.7 34.6 dynamic_update_slice.287
  1146.0 34.6 dynamic_update_slice.287
  1203.3 34.6 dynamic_update_slice.287
  1260.7 34.6 dynamic_update_slice.287
  1377.2 28.3 multiply_reduce_fusion.25
  1462.8 399.3 %while.173 = (s32[]{:T(128)}, f32[24]{0:T(128)}, f32[24,64,64]{1,2,0:T(8,128)}, f32[4,256,24,64]{1,0,3,2:T(4,128)}, f32[4,256,24]{1,0,2:T(4,128)}, /*index=5*/f3...) while((s32[]{:T(128)}, f32[24]{0:T(128)}, ...), condition=%wide.region_48.50_spmd.clone, body=%wide.region_35.49_spmd.clone.sunk | while | flops 4114469120 | bytes 52002032 | solution.py:55
  1518.7 34.7 dynamic_update_slice.270
  1619.0 34.7 dynamic_update_slice.270
  1719.2 34.7 dynamic_update_slice.270
  1819.4 34.7 dynamic_update_slice.270
  1897.0 433.5 %while.172 = (s32[]{:T(128)}, f32[24]{0:T(128)}, f32[24,64,64]{1,2,0:T(8,128)}, f32[4,256,24,64]{1,0,3,2:T(4,128)}, f32[4,256,24]{1,0,2:T(4,128)}, /*index=5*/f3...) while((s32[]{:T(128)}, f32[24]{0:T(128)}, ...), condition=%wide.region_34.36_spmd.clone, body=%wide.region_21.35_spmd.clone.sunk | while | flops 4114469120 | bytes 55147764 | solution.py:55
  1975.2 34.7 dynamic_update_slice.266
  2079.4 34.7 dynamic_update_slice.266
  2183.6 34.7 dynamic_update_slice.266
  2287.8 34.7 dynamic_update_slice.266
  2367.2 416.5 %while.175 = (s32[]{:T(128)}, f32[24]{0:T(128)}, f32[24,64,64]{1,2,0:T(8,128)}, f32[4,256,24,64]{1,0,3,2:T(4,128)}, f32[4,256,24]{1,0,2:T(4,128)}, /*index=5*/f3...) while((s32[]{:T(128)}, f32[24]{0:T(128)}, ...), condition=%wide.region_78.80_spmd.clone, body=%wide.region_65.79_spmd.clone.sunk | while | flops 4114469120 | bytes 52002032 | solution.py:55
  2440.2 34.7 dynamic_update_slice.278
  2540.4 34.7 dynamic_update_slice.278
  2640.7 34.7 dynamic_update_slice.278
  2740.9 34.7 dynamic_update_slice.278
  2818.5 432.0 %while.174 = (s32[]{:T(128)}, f32[24]{0:T(128)}, f32[24,64,64]{1,2,0:T(8,128)}, f32[4,256,24,64]{1,0,3,2:T(4,128)}, f32[4,256,24]{1,0,2:T(4,128)}, /*index=5*/f3...) while((s32[]{:T(128)}, f32[24]{0:T(128)}, ...), condition=%wide.region_64.66_spmd.clone, body=%wide.region_51.65_spmd.clone.sunk | while | flops 4114469120 | bytes 55147764 | solution.py:55
  2895.1 34.7 dynamic_update_slice.274
  2999.2 34.7 dynamic_update_slice.274
  3103.3 34.7 dynamic_update_slice.274
  3207.4 34.7 dynamic_update_slice.274
  3537.1 40.4 %all-reduce.45 = (f32[48]{0:T(128)}, f32[24]{0:T(128)}, f32[24]{0:T(128)}) all-reduce(f32[48]{0:T(128)S(1)} %add.432, f32[24]{0:T(128)S(1)} %add_multiply_fusion, f32[24]{0:T(128)S(1)} %add.434), channel_id=1, replica_groups=mesh['rep'=4,'shard'=8] {'rep','shard'}, use_global_device_ids=true, to_apply=%region_105.107 | all-reduce | flops 96 | bytes 768 | tf_op jit(solution)/shard_map/psum | solution.py:285
  3579.4 61.2 %reduce-scatter.3.cloned.1.call-done = f32[96,3328]{1,0:T(8,128)} async-done(((f32[768,3328]{1,0:T(8,128)}), f32[96,3328]{1,0:T(8,128)}) %reduce-scatter.3.cloned.1.call-update) | async-done | bytes 1277968 | tf_op jit(solution)/shard_map/reduce_scatter | solution.py:276
  3640.6 73.3 %all-reduce.50.cloned.1.call-done = f32[8,6016]{1,0:T(8,128)} async-done(((f32[8,6016]{1,0:T(8,128)}), f32[8,6016]{1,0:T(8,128)}) %all-reduce.50.cloned.1.call-update) | async-done | bytes 192528
  3729.6 33.6 all-reduce.52.cloned.1.call-done
  (1705 shorter events, 2226.3 us)
Async XLA Ops:
  7.2 53.6 %copy-start.14 = (bf16[2,1024,768]{2,1,0:T(8,128)(2,1)S(1)}, bf16[2,1024,768]{2,1,0:T(8,128)(2,1)}, u32[]{:S(2)}) copy-start(bf16[2,1024,768]{2,1,0:T(8,128)(2,1)} %param.30) | copy-start | bytes 9437188
  7.2 66.2 %all-gather.6.cloned.1.call-start = ((), (), s32[]{:S(2)}) async-start(), calls=%async_computation.3 | async-start | bytes 2654208 | tf_op jit(solution)/shard_map/all_gather | solution.py:210
  7.9 143.2 %all-gather.4.cloned.1.call-start = ((), (), s32[]{:S(2)}) async-start(), calls=%async_computation.2 | async-start | bytes 5750784 | tf_op jit(solution)/shard_map/all_gather | solution.py:209
  8.7 3570.7 %reduce-scatter.5.cloned.1.call-start = ((), (), s32[]{:S(2)}) async-start(), calls=%async_computation.5 | async-start | bytes 5308416 | tf_op jit(solution)/shard_map/reduce_scatter | solution.py:277
  45.8 117.1 %copy-start.73 = (f32[768]{0:T(1024)}, f32[768]{0:T(1024)S(1)}, u32[]{:S(2)}) copy-start(f32[768]{0:T(1024)S(1)} %reshape.1409) | copy-start | bytes 9220
  46.1 137.2 %copy-start.89 = (f32[1792]{0:T(1024)}, f32[1792]{0:T(1024)S(1)}, u32[]{:S(2)}) copy-start(f32[1792]{0:T(1024)S(1)} %mul.1928) | copy-start | bytes 21508
  49.0 19.2 copy-start.62
  60.8 102.0 %copy-start.75 = (f32[1024]{0:T(1024)}, f32[1024]{0:T(1024)S(1)}, u32[]{:S(2)}) copy-start(f32[1024]{0:T(1024)S(1)} %fusion.508) | copy-start | bytes 12292
  70.9 140.9 %copy-start.97 = (f32[1024]{0:T(1024)}, f32[1024]{0:T(1024)S(1)}, u32[]{:S(2)}) copy-start(f32[1024]{0:T(1024)S(1)} %fusion.505) | copy-start | bytes 12292
  71.5 152.9 %copy-start.81 = (f32[1024]{0:T(1024)}, f32[1024]{0:T(1024)S(1)}, u32[]{:S(2)}) copy-start(f32[1024]{0:T(1024)S(1)} %fusion.504) | copy-start | bytes 12292
  73.4 77.8 %copy-start.118 = (f32[1024]{0:T(1024)S(1)}, f32[1024]{0:T(1024)}, u32[]{:S(2)}) copy-start(f32[1024]{0:T(1024)} %copy-done.117) | copy-start | bytes 12292
  1349.9 27.2 copy-start.101
  1356.5 20.6 slice-start
  1364.3 74.6 %copy-start.104 = (f32[1024]{0:T(1024)}, f32[1024]{0:T(1024)S(1)}, u32[]{:S(2)}) copy-start(f32[1024]{0:T(1024)S(1)} %fusion.507) | copy-start | bytes 12292
  1515.8 40.0 %copy-start.35 = (f32[256,24]{0,1:T(8,128)S(1)}, f32[256,24]{0,1:T(8,128)}, u32[]{:S(2)}) copy-start(f32[256,24]{0,1:T(8,128)} %copy-done.34) | copy-start | bytes 73732 | tf_op jit(solution)/shard_map/transpose(jvp())/while
  1616.1 40.0 %copy-start.35 = (f32[256,24]{0,1:T(8,128)S(1)}, f32[256,24]{0,1:T(8,128)}, u32[]{:S(2)}) copy-start(f32[256,24]{0,1:T(8,128)} %copy-done.34) | copy-start | bytes 73732 | tf_op jit(solution)/shard_map/transpose(jvp())/while
  1716.3 40.0 %copy-start.35 = (f32[256,24]{0,1:T(8,128)S(1)}, f32[256,24]{0,1:T(8,128)}, u32[]{:S(2)}) copy-start(f32[256,24]{0,1:T(8,128)} %copy-done.34) | copy-start | bytes 73732 | tf_op jit(solution)/shard_map/transpose(jvp())/while
  1816.5 40.0 %copy-start.35 = (f32[256,24]{0,1:T(8,128)S(1)}, f32[256,24]{0,1:T(8,128)}, u32[]{:S(2)}) copy-start(f32[256,24]{0,1:T(8,128)} %copy-done.34) | copy-start | bytes 73732 | tf_op jit(solution)/shard_map/transpose(jvp())/while
  1972.3 40.0 %copy-start.37 = (f32[256,24]{0,1:T(8,128)S(1)}, f32[256,24]{0,1:T(8,128)}, u32[]{:S(2)}) copy-start(f32[256,24]{0,1:T(8,128)} %copy-done.36) | copy-start | bytes 73732 | tf_op jit(solution)/shard_map/transpose(jvp())/while
  2076.5 40.0 %copy-start.37 = (f32[256,24]{0,1:T(8,128)S(1)}, f32[256,24]{0,1:T(8,128)}, u32[]{:S(2)}) copy-start(f32[256,24]{0,1:T(8,128)} %copy-done.36) | copy-start | bytes 73732 | tf_op jit(solution)/shard_map/transpose(jvp())/while
  2180.7 40.0 %copy-start.37 = (f32[256,24]{0,1:T(8,128)S(1)}, f32[256,24]{0,1:T(8,128)}, u32[]{:S(2)}) copy-start(f32[256,24]{0,1:T(8,128)} %copy-done.36) | copy-start | bytes 73732 | tf_op jit(solution)/shard_map/transpose(jvp())/while
  2284.9 40.0 %copy-start.37 = (f32[256,24]{0,1:T(8,128)S(1)}, f32[256,24]{0,1:T(8,128)}, u32[]{:S(2)}) copy-start(f32[256,24]{0,1:T(8,128)} %copy-done.36) | copy-start | bytes 73732 | tf_op jit(solution)/shard_map/transpose(jvp())/while
  2437.3 40.0 %copy-start.39 = (f32[256,24]{0,1:T(8,128)S(1)}, f32[256,24]{0,1:T(8,128)}, u32[]{:S(2)}) copy-start(f32[256,24]{0,1:T(8,128)} %copy-done.38) | copy-start | bytes 73732 | tf_op jit(solution)/shard_map/transpose(jvp())/while
  2537.5 40.0 %copy-start.39 = (f32[256,24]{0,1:T(8,128)S(1)}, f32[256,24]{0,1:T(8,128)}, u32[]{:S(2)}) copy-start(f32[256,24]{0,1:T(8,128)} %copy-done.38) | copy-start | bytes 73732 | tf_op jit(solution)/shard_map/transpose(jvp())/while
  2637.8 40.0 %copy-start.39 = (f32[256,24]{0,1:T(8,128)S(1)}, f32[256,24]{0,1:T(8,128)}, u32[]{:S(2)}) copy-start(f32[256,24]{0,1:T(8,128)} %copy-done.38) | copy-start | bytes 73732 | tf_op jit(solution)/shard_map/transpose(jvp())/while
  2738.0 40.0 %copy-start.39 = (f32[256,24]{0,1:T(8,128)S(1)}, f32[256,24]{0,1:T(8,128)}, u32[]{:S(2)}) copy-start(f32[256,24]{0,1:T(8,128)} %copy-done.38) | copy-start | bytes 73732 | tf_op jit(solution)/shard_map/transpose(jvp())/while
  2892.2 40.0 %copy-start.41 = (f32[256,24]{0,1:T(8,128)S(1)}, f32[256,24]{0,1:T(8,128)}, u32[]{:S(2)}) copy-start(f32[256,24]{0,1:T(8,128)} %copy-done.40) | copy-start | bytes 73732 | tf_op jit(solution)/shard_map/transpose(jvp())/while
  2996.3 40.0 %copy-start.41 = (f32[256,24]{0,1:T(8,128)S(1)}, f32[256,24]{0,1:T(8,128)}, u32[]{:S(2)}) copy-start(f32[256,24]{0,1:T(8,128)} %copy-done.40) | copy-start | bytes 73732 | tf_op jit(solution)/shard_map/transpose(jvp())/while
  3100.4 40.0 %copy-start.41 = (f32[256,24]{0,1:T(8,128)S(1)}, f32[256,24]{0,1:T(8,128)}, u32[]{:S(2)}) copy-start(f32[256,24]{0,1:T(8,128)} %copy-done.40) | copy-start | bytes 73732 | tf_op jit(solution)/shard_map/transpose(jvp())/while
  3204.5 40.0 %copy-start.41 = (f32[256,24]{0,1:T(8,128)S(1)}, f32[256,24]{0,1:T(8,128)}, u32[]{:S(2)}) copy-start(f32[256,24]{0,1:T(8,128)} %copy-done.40) | copy-start | bytes 73732 | tf_op jit(solution)/shard_map/transpose(jvp())/while
  3317.8 22.3 copy-start.27
  3317.8 22.3 copy-start.87
  3317.9 22.3 copy-start.102
  3349.6 22.6 slice-start.2
  3349.6 291.0 %reduce-scatter.3.cloned.1.call-start = ((), (), s32[]{:S(2)}) async-start(), calls=%async_computation.4 | async-start | bytes 11501568 | tf_op jit(solution)/shard_map/reduce_scatter | solution.py:276
  3349.6 22.6 slice-start.3
  3349.6 22.5 copy-start.44
  3349.6 22.5 copy-start.45
  3349.7 22.5 copy-start.46
  3349.7 22.5 copy-start.47
  3410.7 16.8 copy-start.9
  3436.4 14.5 copy-start.76
  3465.6 248.2 %all-reduce.50.cloned.1.call-start = ((), (), s32[]{:S(2)}) async-start(), calls=%async_computation.6 | async-start | bytes 385024
  3505.8 14.4 copy-start.107
  3511.4 16.4 slice-start.4
  3520.3 243.0 %all-reduce.52.cloned.1.call-start = ((), (), s32[]{:S(2)}) async-start(), calls=%async_computation.7 | async-start | bytes 3735552 | tf_op jit(solution)/shard_map/psum | solution.py:284
  3534.7 42.7 %copy-start.32 = (bf16[1,1024,768]{2,1,0:T(8,128)(2,1)S(1)}, bf16[1,1024,768]{2,1,0:T(8,128)(2,1)}, u32[]{:S(2)}) copy-start(bf16[1,1024,768]{2,1,0:T(8,128)(2,1)} %get-tuple-element.3203) | copy-start | bytes 4718596
  3534.8 42.7 %copy-start.33 = (bf16[1,1024,768]{2,1,0:T(8,128)(2,1)S(1)}, bf16[1,1024,768]{2,1,0:T(8,128)(2,1)}, u32[]{:S(2)}) copy-start(bf16[1,1024,768]{2,1,0:T(8,128)(2,1)} %get-tuple-element.3204) | copy-start | bytes 4718596
  (202 other events, 1524.6 us)
Sparse Core Ops, SparseCore 0:
  10.2 55.2 all-gather.5
  67.7 83.4 all-gather.3
  3349.7 93.5 reduce-scatter.4
  3465.7 174.7 reduce-scatter.2
  3644.7 69.1 all-reduce.49
  3716.2 46.9 all-reduce.51
where the time goes:
time: 3830 us; the launch traced here: 3770 us
  local copies, waits for them, and re-layouts  1910 us (50%)
  matrix products  895 us (23%)
  other arithmetic  573 us (15%)
  waiting for transfers between devices  240 us (6%)
  blocking collectives  84.2 us (2%)
  loops' own time  57 us (1%)
    dynamic_update_slice x96, local copies, waits for them, and re-layouts, span_scan(): _, outputs = lax.scan(jax.checkpoint(advance), initial, pieces)  1220 us
    dot_general x48, matrix products, advance(): inside = jnp.einsum('hts,shp->thp', weights, value_piece, precision=precise)  447 us
    dot_general x48, matrix products, advance(): jnp.einsum('sh,sn,shp->hnp', tail, input_piece, value_piece, precision=pr...  127 us
    another operation x176, other arithmetic  122 us
    squeeze x64, local copies, waits for them, and re-layouts, span_scan(): _, outputs = lax.scan(jax.checkpoint(advance), initial, pieces)  88.8 us
    dot_general x32, matrix products, advance(): jnp.einsum('tn,hnp->thp', output_piece, state, precision=precise)  83.4 us
  transfers between devices with their start and end apart: 6, of which 4 were waited for; matrix products, arithmetic and copies ran while one was open for 6% of the time, Pallas kernels for 0%

commit v1 on v0

v1 whole, which is shorter than its diff:
```python
from functools import partial

import jax
import jax.numpy as jnp
from jax import lax
from jax.experimental import pallas as pl
from jax.experimental.pallas import tpu as pltpu
from jax.sharding import PartitionSpec as P

HEADS = 24
HEADDIM = 64
STATE = 64
CONV = 4
INNER = 1536
CHANNELS = 1792
D = 768
WIDE = INNER + CHANNELS
SPAN = 128
BLOCK = 256
SUBS = BLOCK // SPAN
EPS = 1e-05
LOG2E = 1.4426950408889634
TINY = 1.2e-38
f32 = jnp.float32
bf16 = jnp.bfloat16
precise = lax.Precision.HIGHEST
VMEM_LIMIT = 60 * 1024 * 1024


def mm(a, b, precision=None):
    return lax.dot_general(
        a, b, (((1,), (0,)), ((), ())), precision=precision, preferred_element_type=f32
    )


def mm_nt(a, b):
    return lax.dot_general(a, b, (((1,), (1,)), ((), ())), preferred_element_type=f32)


def mm_tn(a, b):
    return lax.dot_general(a, b, (((0,), (0,)), ((), ())), preferred_element_type=f32)


def sigmoid(v):
    return 0.5 * jnp.tanh(0.5 * v) + 0.5


def iotas(shape):
    return (
        lax.broadcasted_iota(jnp.int32, shape, 0),
        lax.broadcasted_iota(jnp.int32, shape, 1),
    )


def step_sums(x, rate):
    rows, cols = iotas((SPAN, SPAN))
    steps = jnp.maximum(x, 0.0) + jnp.log1p(jnp.exp(-jnp.abs(x)))
    scaled = steps * rate
    fcum = mm(scaled[:HEADS], (rows <= cols).astype(f32), precise)
    rcum = mm(scaled[HEADS:], (rows >= cols).astype(f32), precise)
    return steps, fcum, rcum


def span_tails(steps, fcum, rcum):
    tail_f = jnp.exp2(fcum[:, SPAN - 1 :] - fcum) * steps[:HEADS]
    tail_r = jnp.exp2(rcum[:, :1] - rcum) * steps[HEADS:]
    return tail_f, tail_r


def enter_kernel(
    len_ref,
    tok_ref,
    wide_ref,
    time_ref,
    pre_ref,
    taps_ref,
    bias_ref,
    rate_ref,
    gate_o,
    fin_o,
    filt_o,
    act_o,
    x_o,
    state_o,
    proj_s,
    run_s,
):
    seq = pl.program_id(0)
    block = pl.program_id(1)
    length = len_ref[seq]

    @pl.when(block == 0)
    def _():
        proj_s[:, BLOCK:] = jnp.zeros((CHANNELS, SPAN), f32)
        run_s[...] = jnp.zeros_like(run_s)

    @pl.when(block * BLOCK < length)
    def _():
        tok = tok_ref[0].astype(f32)
        scale = lax.rsqrt(jnp.mean(tok * tok, axis=-1, keepdims=True) + EPS)
        normed = (tok * scale * pre_ref[...]).astype(bf16)
        x_o[0] = mm_nt(time_ref[...], normed) + bias_ref[...]
        proj_s[:, :SPAN] = proj_s[:, BLOCK:]
        for i in range(INNER // 256):
            gate_o[0, i * 256 : (i + 1) * 256, :] = mm_nt(
                wide_ref[i * 256 : (i + 1) * 256, :], normed
            ).astype(bf16)
        for i in range(CHANNELS // 256):
            proj_s[i * 256 : (i + 1) * 256, SPAN:] = mm_nt(
                wide_ref[INNER + i * 256 : INNER + (i + 1) * 256, :], normed
            )
        place = block * BLOCK + lax.broadcasted_iota(jnp.int32, (1, BLOCK), 1)
        mask = (place < length).astype(f32)

        def filter_rows(i, masked):
            r = pl.ds(pl.multiple_of(i * 32, 32), 32)
            w = proj_s[r, :]
            taps = taps_ref[r, :]
            acc = taps[:, 4:5] + taps[:, 3:4] * w[:, SPAN:]
            for lag in range(1, CONV):
                moved = pltpu.roll(w, lag, 1)[:, SPAN:]
                acc = acc + taps[:, 3 - lag : 4 - lag] * moved
            fin_o[0, r, :] = w[:, SPAN:].astype(bf16)
            filt_o[0, r, :] = acc.astype(bf16)
            act = acc * sigmoid(acc)
            if masked:
                act = act * mask
            act_o[0, r, :] = act.astype(bf16)

        lax.fori_loop(0, INNER // 32, lambda i, _: filter_rows(i, True), None)
        lax.fori_loop(INNER // 32, CHANNELS // 32, lambda i, _: filter_rows(i, False), None)

        lane = lax.broadcasted_iota(jnp.int32, (1, SPAN), 1)

        def span(sub, _):
            cols = pl.ds(pl.multiple_of(sub * SPAN, SPAN), SPAN)
            steps, fcum, rcum = step_sums(x_o[0, :, cols], rate_ref[...])
            tail_f, tail_r = span_tails(steps, fcum, rcum)
            decay = jnp.exp2(fcum[:, SPAN - 1 :])
            ins_f = act_o[0, INNER : INNER + 64, cols].astype(f32)
            ins_r = act_o[0, INNER + 128 : INNER + 192, cols].astype(f32)
            for h in range(HEADS):
                rows = slice(h * 64, (h + 1) * 64)
                weighted = jnp.concatenate(
                    [
                        (ins_f * tail_f[h : h + 1]).astype(bf16),
                        (ins_r * tail_r[h : h + 1]).astype(bf16),
                    ],
                    axis=0,
                )
                fresh = mm_nt(act_o[0, rows, cols], weighted)
                run = run_s[rows, :]
                state_o[0, sub, rows, :] = jnp.where(lane < 64, run, fresh)
                run_s[rows, :] = run * decay[h : h + 1] + fresh
            return None

        lax.fori_loop(0, SUBS, span, None)


def middle_kernel(
    len_ref,
    skip_ref,
    tok_ref,
    cot_ref,
    gate_ref,
    act_ref,
    x_ref,
    state_ref,
    narrow_ref,
    turned_ref,
    post_ref,
    rate_ref,
    result_o,
    dgate_o,
    dval_o,
    dio_o,
    sums_o,
    dstate_o,
    rstate_o,
    narrow_o,
    post_o,
    skip_o,
    run_s,
    grun_s,
    mixed_s,
    gated_s,
    dgn_s,
    spread_s,
    matrix_s,
    held_s,
):
    seq = pl.program_id(0)
    step = pl.program_id(1)
    block = pl.num_programs(1) - 1 - step
    length = len_ref[seq]

    @pl.when((seq == 0) & (step == 0))
    def _():
        narrow_o[...] = jnp.zeros_like(narrow_o)
        post_o[...] = jnp.zeros_like(post_o)
        skip_o[...] = jnp.zeros_like(skip_o)

    @pl.when(step == 0)
    def _():
        run_s[...] = jnp.zeros_like(run_s)
        grun_s[...] = jnp.zeros_like(grun_s)

    @pl.when(block * BLOCK >= length)
    def _():
        result_o[...] = tok_ref[...]

    @pl.when(block * BLOCK < length)
    def _():
        rows_i, cols_i = iotas((SPAN, SPAN))
        lower = rows_i < cols_i
        upper = rows_i > cols_i
        lane = lax.broadcasted_iota(jnp.int32, (1, SPAN), 1)

        def span_scores(cols):
            fi = act_ref[0, INNER : INNER + 64, cols]
            fo = act_ref[0, INNER + 64 : INNER + 128, cols]
            ri = act_ref[0, INNER + 128 : INNER + 192, cols]
            ro = act_ref[0, INNER + 192 : INNER + 256, cols]
            ahead = mm_tn(fi, fo)
            behind = mm_tn(ri, ro)
            scores = jnp.where(lower, ahead, jnp.where(upper, behind, 0.0))
            return fi, fo, ri, ro, scores

        def forward_span(back, _):
            sub = SUBS - 1 - back
            cols = pl.ds(pl.multiple_of(sub * SPAN, SPAN), SPAN)
            steps, fcum, rcum = step_sums(x_ref[0, :, cols], rate_ref[...])
            least = jnp.log2(jnp.maximum(steps, TINY))
            columns = jnp.concatenate(
                [fcum - least[:HEADS], rcum - least[HEADS:], jnp.zeros((SPAN - 48, SPAN), f32)],
                axis=0,
            ).T
            out_f = jnp.exp2(fcum)
            out_r = jnp.exp2(rcum)
            decay = jnp.exp2(rcum[:, :1])
            fi, fo, ri, ro, scores = span_scores(cols)
            fo = fo.astype(f32)
            ro = ro.astype(f32)
            for h in range(HEADS):
                rows = slice(h * 64, (h + 1) * 64)
                power = jnp.where(
                    lower,
                    fcum[h : h + 1] - columns[:, h : h + 1],
                    rcum[h : h + 1] - columns[:, HEADS + h : HEADS + h + 1],
                )
                spread = jnp.exp2(power)
                spread_s[sub, h] = spread.astype(bf16)
                matrix = jnp.concatenate(
                    [
                        (spread * scores).astype(bf16),
                        (fo * out_f[h : h + 1]).astype(bf16),
                        (ro * out_r[h : h + 1]).astype(bf16),
                    ],
                    axis=0,
                )
                matrix_s[sub, h] = matrix
                state = state_ref[0, sub, rows, :]
                run = run_s[rows, :]
                rstate_o[0, sub, rows, :] = run
                held = jnp.where(lane < 64, state, run).astype(bf16)
                held_s[sub, rows, :] = held
                run_s[rows, :] = run * decay[h : h + 1] + state
                values = act_ref[0, rows, cols]
                both = jnp.concatenate([values, held], axis=1)
                mixed_s[rows, cols] = mm(both, matrix) + skip_ref[h] * values.astype(f32)
            return None

        lax.fori_loop(0, SUBS, forward_span, None)

        def gate_rows(i, total):
            r = pl.ds(pl.multiple_of(i * 32, 32), 32)
            gate = gate_ref[0, r, :].astype(f32)
            gated = mixed_s[r, :] * (gate * sigmoid(gate))
            gated_s[r, :] = gated
            return total + jnp.sum((gated * gated).reshape(4, 8, BLOCK), axis=0)

        squares = lax.fori_loop(0, INNER // 32, gate_rows, jnp.zeros((8, BLOCK), f32))
        rs = lax.rsqrt(jnp.sum(squares, axis=0, keepdims=True) * (1.0 / INNER) + EPS)

        def norm_rows(i, _):
            r = pl.ds(pl.multiple_of(i * 32, 32), 32)
            held_gn = gated_s[r, :] * rs * post_ref[r, :1]
            dgate_o[0, r, :] = held_gn.astype(bf16)
            return None

        lax.fori_loop(0, INNER // 32, norm_rows, None)
        gnormed = dgate_o[0]
        place = block * BLOCK + lax.broadcasted_iota(jnp.int32, (BLOCK, 1), 0)
        inside = place < length
        branch = mm(turned_ref[...], gnormed)
        result_o[0] = (tok_ref[0].astype(f32) + jnp.where(inside, branch.T, 0.0)).astype(bf16)
        slope = jnp.where(inside, cot_ref[0].astype(f32), 0.0).astype(bf16)
        for i in range(3):
            rows = slice(i * 512, (i + 1) * 512)
            narrow_o[rows, :] += mm(gnormed[rows], slope)
            dgn_s[rows, :] = mm_nt(narrow_ref[rows, :], slope)

        def dot_rows(i, total):
            r = pl.ds(pl.multiple_of(i * 32, 32), 32)
            product = dgn_s[r, :] * gated_s[r, :]
            kept = product * rs
            post_o[r, :] += kept[:, :SPAN] + kept[:, SPAN:]
            weighted = product * post_ref[r, :1]
            return total + jnp.sum(weighted.reshape(4, 8, BLOCK), axis=0)

        dots = lax.fori_loop(0, INNER // 32, dot_rows, jnp.zeros((8, BLOCK), f32))
        mean = jnp.sum(dots, axis=0, keepdims=True) * (1.0 / INNER)
        pull = rs * rs * rs * mean

        def grad_rows(i, _):
            r = pl.ds(pl.multiple_of(i * 32, 32), 32)
            gate = gate_ref[0, r, :].astype(f32)
            sig = sigmoid(gate)
            dgated = rs * post_ref[r, :1] * dgn_s[r, :] - gated_s[r, :] * pull
            dmixed = dgated * (gate * sig)
            dgate = dgated * mixed_s[r, :] * (sig * (1.0 + gate * (1.0 - sig)))
            dgate_o[0, r, :] = dgate.astype(bf16)
            dgn_s[r, :] = dmixed
            product = dmixed * act_ref[0, r, :].astype(f32)
            skip_o[r, :] += product[:, :SPAN] + product[:, SPAN:]
            return None

        lax.fori_loop(0, INNER // 32, grad_rows, None)

        ones_row = (lax.broadcasted_iota(jnp.int32, (8, 2 * SPAN), 1) // SPAN) == (
            lax.broadcasted_iota(jnp.int32, (8, 2 * SPAN), 0)
        )
        ones_row = ones_row.astype(bf16)
        ones_flat = jnp.ones((8, SPAN), bf16)

        def backward_span(back, _):
            sub = SUBS - 1 - back
            cols = pl.ds(pl.multiple_of(sub * SPAN, SPAN), SPAN)
            steps, fcum, rcum = step_sums(x_ref[0, :, cols], rate_ref[...])
            out_f = jnp.exp2(fcum)
            out_r = jnp.exp2(rcum)
            decay = jnp.exp2(fcum[:, SPAN - 1 :])
            fi, fo, ri, ro, scores = span_scores(cols)
            fo32 = fo.astype(f32)
            ro32 = ro.astype(f32)
            dscores = jnp.zeros((SPAN, SPAN), f32)
            dfo = jnp.zeros((64, SPAN), f32)
            dro = jnp.zeros((64, SPAN), f32)
            for h in range(HEADS):
                rows = slice(h * 64, (h + 1) * 64)
                dmixed = dgn_s[rows, cols]
                dm = dmixed.astype(bf16)
                values = act_ref[0, rows, cols]
                held = held_s[sub, rows, :]
                both = jnp.concatenate([values, held], axis=1)
                grad = mm_tn(both, dm)
                matrix = matrix_s[sub, h]
                first = grad[:SPAN] * spread_s[sub, h].astype(f32)
                dscores = dscores + first
                pairs = first * scores
                pairs_low = jnp.where(lower, pairs, 0.0).astype(bf16)
                stack = jnp.concatenate([pairs_low, pairs.astype(bf16)], axis=0)
                by_row = mm(ones_row, stack)
                by_col = mm_nt(ones_flat, stack)
                part_f = grad[SPAN : SPAN + 64] * out_f[h : h + 1]
                part_r = grad[SPAN + 64 :] * out_r[h : h + 1]
                dfo = dfo + part_f
                dro = dro + part_r
                carried_f = jnp.sum(part_f * fo32, axis=0, keepdims=True)
                carried_r = jnp.sum(part_r * ro32, axis=0, keepdims=True)
                col_f = by_col[:1, :SPAN]
                sums_o[0, h : h + 1, cols] = by_row[:1] + carried_f
                sums_o[0, HEADS + h : HEADS + h + 1, cols] = (
                    by_row[1:2] - by_row[:1] + carried_r
                )
                sums_o[0, 2 * HEADS + h : 2 * HEADS + h + 1, cols] = col_f
                sums_o[0, 3 * HEADS + h : 3 * HEADS + h + 1, cols] = by_col[:1, SPAN:] - col_f
                dboth = mm_nt(dm, matrix)
                dval_o[0, rows, cols] = (dboth[:, :SPAN] + skip_ref[h] * dmixed).astype(bf16)
                dheld = dboth[:, SPAN:]
                run = grun_s[rows, :]
                dstate_o[0, sub, rows, :] = jnp.where(lane < 64, run, dheld)
                sums_o[0, 4 * HEADS + h : 4 * HEADS + h + 1, cols] = decay[h : h + 1] * jnp.sum(
                    jnp.where(lane < 64, run * held.astype(f32), 0.0), axis=0, keepdims=True
                )
                grun_s[rows, :] = run * decay[h : h + 1] + dheld
            low = jnp.where(lower, dscores, 0.0).astype(bf16)
            high = jnp.where(upper, dscores, 0.0).astype(bf16)
            dio_o[0, 0:64, cols] = mm_nt(fo, low)
            dio_o[0, 64:128, cols] = dfo + mm(fi, low)
            dio_o[0, 128:192, cols] = mm_nt(ro, high)
            dio_o[0, 192:256, cols] = dro + mm(ri, high)
            return None

        lax.fori_loop(0, SUBS, backward_span, None)


def leave_kernel(
    len_ref,
    filt_ref,
    act_ref,
    fin_ref,
    x_ref,
    dval_ref,
    dio_ref,
    sums_ref,
    dstate_ref,
    rstate_ref,
    rate_ref,
    dfilt_o,
    draw_o,
    offset_o,
    taps_o,
    bias_o,
    decay_o,
    grun_s,
    near_s,
    dact_s,
    last_s,
):
    seq = pl.program_id(0)
    block = pl.program_id(1)
    length = len_ref[seq]

    @pl.when((seq == 0) & (block == 0))
    def _():
        offset_o[...] = jnp.zeros_like(offset_o)
        taps_o[...] = jnp.zeros_like(taps_o)
        bias_o[...] = jnp.zeros_like(bias_o)
        decay_o[...] = jnp.zeros_like(decay_o)

    @pl.when(block == 0)
    def _():
        grun_s[...] = jnp.zeros_like(grun_s)
        last_s[...] = jnp.zeros_like(last_s)

    @pl.when(block * BLOCK < length)
    def _():
        rows_i, cols_i = iotas((SPAN, SPAN))
        lane = lax.broadcasted_iota(jnp.int32, (1, SPAN), 1)

        def span(sub, _):
            cols = pl.ds(pl.multiple_of(sub * SPAN, SPAN), SPAN)
            x = x_ref[0, :, cols]
            steps, fcum, rcum = step_sums(x, rate_ref[...])
            tail_f, tail_r = span_tails(steps, fcum, rcum)
            decay = jnp.exp2(rcum[:, :1])
            fi = act_ref[0, INNER : INNER + 64, cols].astype(f32)
            ri = act_ref[0, INNER + 128 : INNER + 192, cols].astype(f32)
            dfi = jnp.zeros((64, SPAN), f32)
            dri = jnp.zeros((64, SPAN), f32)
            ends_f = []
            ends_r = []
            for h in range(HEADS):
                rows = slice(h * 64, (h + 1) * 64)
                weighted = jnp.concatenate(
                    [
                        (fi * tail_f[h : h + 1]).astype(bf16),
                        (ri * tail_r[h : h + 1]).astype(bf16),
                    ],
                    axis=0,
                )
                dstate = dstate_ref[0, sub, rows, :]
                run = grun_s[rows, :]
                dfresh = jnp.where(lane < 64, dstate, run).astype(bf16)
                near_s[h : h + 1, :] = decay[h : h + 1] * jnp.sum(
                    jnp.where(lane < 64, 0.0, run * rstate_ref[0, sub, rows, :]),
                    axis=0,
                    keepdims=True,
                )
                grun_s[rows, :] = run * decay[h : h + 1] + dstate
                values = act_ref[0, rows, cols]
                dact_s[rows, cols] = dval_ref[0, rows, cols].astype(f32) + mm(dfresh, weighted)
                dweighted = mm_tn(dfresh, values)
                part_f = dweighted[:64] * tail_f[h : h + 1]
                part_r = dweighted[64:] * tail_r[h : h + 1]
                dfi = dfi + part_f
                dri = dri + part_r
                ends_f.append(jnp.sum(part_f * fi, axis=0, keepdims=True))
                ends_r.append(jnp.sum(part_r * ri, axis=0, keepdims=True))
            dact_s[INNER : INNER + 64, cols] = dio_ref[0, 0:64, cols] + dfi
            dact_s[INNER + 64 : INNER + 128, cols] = dio_ref[0, 64:128, cols]
            dact_s[INNER + 128 : INNER + 192, cols] = dio_ref[0, 128:192, cols] + dri
            dact_s[INNER + 192 : INNER + 256, cols] = dio_ref[0, 192:256, cols]
            ends_f = jnp.concatenate(ends_f, axis=0)
            ends_r = jnp.concatenate(ends_r, axis=0)
            col_f = sums_ref[0, 2 * HEADS : 3 * HEADS, cols]
            col_r = sums_ref[0, 3 * HEADS : 4 * HEADS, cols]
            far_f = jnp.sum(sums_ref[0, 4 * HEADS :, cols], axis=1, keepdims=True)
            far_r = jnp.sum(near_s[...], axis=1, keepdims=True)
            dfa = mm(sums_ref[0, :HEADS, cols] - col_f, (rows_i >= cols_i).astype(f32), precise)
            dra = mm(
                sums_ref[0, HEADS : 2 * HEADS, cols] - col_r,
                (rows_i <= cols_i).astype(f32),
                precise,
            )
            dfa = dfa + far_f + mm(ends_f, (rows_i < cols_i).astype(f32), precise)
            dra = dra + far_r + mm(ends_r, (rows_i > cols_i).astype(f32), precise)
            sig = jax.nn.sigmoid(x)
            rate = rate_ref[...] * (1.0 / LOG2E)
            share = sig / jnp.maximum(steps, TINY)
            span_d = jnp.concatenate([dfa, dra], axis=0)
            draw = jnp.concatenate([col_f + ends_f, col_r + ends_r], axis=0) * share + span_d * (rate * sig)
            draw_o[0, :, cols] = draw.astype(bf16)
            bias_o[...] += draw
            decay_o[...] += span_d * steps * rate
            return None

        lax.fori_loop(0, SUBS, span, None)
        place = block * BLOCK + lax.broadcasted_iota(jnp.int32, (1, BLOCK), 1)
        mask = (place < length).astype(f32)

        def filter_rows(i, masked):
            r = pl.ds(pl.multiple_of(i * 32, 32), 32)
            filt = filt_ref[0, r, :].astype(f32)
            sig = sigmoid(filt)
            dact = dact_s[r, :]
            if masked:
                dact = dact * mask
            dfilt = dact * (sig * (1.0 + filt * (1.0 - sig)))
            dfilt_o[0, r, :] = dfilt.astype(bf16)
            offset_o[r, :] += dfilt[:, :SPAN] + dfilt[:, SPAN:]
            fin = fin_ref[0, r, :].astype(f32)
            w = jnp.concatenate([last_s[r, :], fin], axis=1)
            last_s[r, :] = fin[:, SPAN:]
            product = dfilt * fin
            taps_o[3, r, :] += product[:, :SPAN] + product[:, SPAN:]
            for lag in range(1, CONV):
                product = dfilt * pltpu.roll(w, lag, 1)[:, SPAN:]
                taps_o[3 - lag, r, :] += product[:, :SPAN] + product[:, SPAN:]
            return None

        lax.fori_loop(0, INNER // 32, lambda i, _: filter_rows(i, True), None)
        lax.fori_loop(INNER // 32, CHANNELS // 32, lambda i, _: filter_rows(i, False), None)


def widen_kernel(
    len_ref,
    tok_ref,
    cot_ref,
    dgate_ref,
    dfilt_ref,
    next_ref,
    draw_ref,
    wide_ref,
    time_ref,
    pre_ref,
    taps_ref,
    slope_o,
    wide_o,
    time_o,
    pre_o,
    dproj_s,
):
    seq = pl.program_id(0)
    block = pl.program_id(1)
    length = len_ref[seq]

    @pl.when((seq == 0) & (block == 0))
    def _():
        wide_o[...] = jnp.zeros_like(wide_o)
        time_o[...] = jnp.zeros_like(time_o)
        pre_o[...] = jnp.zeros_like(pre_o)

    @pl.when(block * BLOCK >= length)
    def _():
        slope_o[...] = cot_ref[...]

    @pl.when(block * BLOCK < length)
    def _():
        tok = tok_ref[0].astype(f32)
        scale = lax.rsqrt(jnp.mean(tok * tok, axis=-1, keepdims=True) + EPS)
        normed = (tok * scale * pre_ref[...]).astype(bf16)
        normed_t = normed.T
        dproj_s[:INNER, :] = dgate_ref[0]
        beyond = (block + 1) * BLOCK < length

        def filter_rows(i, _):
            r = pl.ds(pl.multiple_of(i * 32, 32), 32)
            following = jnp.where(beyond, next_ref[0, r, :].astype(f32), 0.0)
            w = jnp.concatenate([dfilt_ref[0, r, :].astype(f32), following], axis=1)
            taps = taps_ref[r, :]
            acc = taps[:, 3:4] * w[:, :BLOCK]
            for lag in range(1, CONV):
                moved = pltpu.roll(w, BLOCK + SPAN - lag, 1)[:, :BLOCK]
                acc = acc + taps[:, 3 - lag : 4 - lag] * moved
            dproj_s[pl.ds(pl.multiple_of(INNER + i * 32, 32), 32), :] = acc.astype(bf16)
            return None

        lax.fori_loop(0, CHANNELS // 32, filter_rows, None)
        for i in range(WIDE // 256):
            rows = slice(i * 256, (i + 1) * 256)
            wide_o[:, rows] += mm_nt(normed_t, dproj_s[rows, :])
        draw = draw_ref[0]
        time_o[...] += mm_nt(normed_t, draw)
        dnormed = (mm(wide_ref[...], dproj_s[...]) + mm(time_ref[...], draw)).T
        product = dnormed * tok
        pre_o[...] += jnp.sum((product * scale).reshape(BLOCK // 8, 8, D), axis=0)
        gain = pre_ref[...]
        mean = jnp.mean(product * gain, axis=-1, keepdims=True)
        grad = scale * (gain * dnormed) - tok * (scale * scale * scale * mean)
        slope_o[0] = (cot_ref[0].astype(f32) + grad).astype(bf16)


def whole(shape):
    return pl.BlockSpec(shape, lambda s, c, *_: (0,) * len(shape))


def layer(
    tokens, cotangent, lengths, wide, time, narrow, taps, offset, prenorm, postnorm,
    timestep_bias, decay_log, skip_gain,
):
    count, length = tokens.shape[:2]
    blocks = length // BLOCK
    spans = length // SPAN
    wide_t = wide.T
    time_t = time.T
    narrow_t = narrow.T
    pre = prenorm.astype(f32)[None]
    post = jnp.pad(postnorm.astype(f32)[:, None], ((0, 0), (0, 7)))
    cols = jnp.concatenate([taps, offset[None], jnp.zeros((3, CHANNELS), bf16)], axis=0).astype(f32).T
    bias = timestep_bias[:, None]
    rate = -jnp.exp(decay_log) * LOG2E
    rate = jnp.concatenate([rate, rate])[:, None]
    grid = (count, blocks)
    sds = jax.ShapeDtypeStruct

    def ahead(rows, width=BLOCK):
        return pl.BlockSpec((1, rows, width), lambda s, c, *_: (s, 0, c))

    def back(rows, width=BLOCK):
        return pl.BlockSpec((1, rows, width), lambda s, c, *_: (s, 0, blocks - 1 - c))

    def tall(reverse):
        if reverse:
            return pl.BlockSpec((1, BLOCK, D), lambda s, c, *_: (s, blocks - 1 - c, 0))
        return pl.BlockSpec((1, BLOCK, D), lambda s, c, *_: (s, c, 0))

    def states(reverse):
        if reverse:
            return pl.BlockSpec((1, SUBS, INNER, SPAN), lambda s, c, *_: (s, blocks - 1 - c, 0, 0))
        return pl.BlockSpec((1, SUBS, INNER, SPAN), lambda s, c, *_: (s, c, 0, 0))

    params = pltpu.CompilerParams(
        dimension_semantics=("arbitrary", "arbitrary"), vmem_limit_bytes=VMEM_LIMIT
    )
    state_shape = sds((count, spans, INNER, SPAN), f32)
    gate, fin, filt, act, x, state = pl.pallas_call(
        enter_kernel,
        grid_spec=pltpu.PrefetchScalarGridSpec(
            num_scalar_prefetch=1,
            grid=grid,
            in_specs=[
                tall(False), whole((WIDE, D)), whole((48, D)), whole((1, D)),
                whole((CHANNELS, 8)), whole((48, 1)), whole((48, 1)),
            ],
            out_specs=[
                ahead(INNER), ahead(CHANNELS), ahead(CHANNELS), ahead(CHANNELS), ahead(48), states(False),
            ],
            scratch_shapes=[
                pltpu.VMEM((CHANNELS, BLOCK + SPAN), f32),
                pltpu.VMEM((INNER, SPAN), f32),
            ],
        ),
        out_shape=[
            sds((count, INNER, length), bf16),
            sds((count, CHANNELS, length), bf16),
            sds((count, CHANNELS, length), bf16),
            sds((count, CHANNELS, length), bf16),
            sds((count, 48, length), f32),
            state_shape,
        ],
        compiler_params=params,
        name="enter",
    )(lengths, tokens, wide_t, time_t, pre, cols, bias, rate)

    result, dgate, dval, dio, sums, dstate, rstate, narrow_grad, post_grad, skip_grad = pl.pallas_call(
        middle_kernel,
        grid_spec=pltpu.PrefetchScalarGridSpec(
            num_scalar_prefetch=1,
            grid=grid,
            in_specs=[
                pl.BlockSpec(memory_space=pltpu.SMEM),
                tall(True), tall(True), back(INNER), back(CHANNELS), back(48), states(True),
                whole((INNER, D)), whole((D, INNER)), whole((INNER, 8)), whole((48, 1)),
            ],
            out_specs=[
                tall(True), back(INNER), back(INNER), back(256), back(120), states(True), states(True),
                whole((INNER, D)), whole((INNER, SPAN)), whole((INNER, SPAN)),
            ],
            scratch_shapes=[
                pltpu.VMEM((INNER, SPAN), f32),
                pltpu.VMEM((INNER, SPAN), f32),
                pltpu.VMEM((INNER, BLOCK), f32),
                pltpu.VMEM((INNER, BLOCK), f32),
                pltpu.VMEM((INNER, BLOCK), f32),
                pltpu.VMEM((SUBS, HEADS, SPAN, SPAN), bf16),
                pltpu.VMEM((SUBS, HEADS, 2 * SPAN, SPAN), bf16),
                pltpu.VMEM((SUBS, INNER, SPAN), bf16),
            ],
        ),
        out_shape=[
            sds((count, length, D), bf16),
            sds((count, INNER, length), bf16),
            sds((count, INNER, length), bf16),
            sds((count, 256, length), f32),
            sds((count, 120, length), f32),
            state_shape,
            state_shape,
            sds((INNER, D), f32),
            sds((INNER, SPAN), f32),
            sds((INNER, SPAN), f32),
        ],
        compiler_params=params,
        name="middle",
    )(lengths, skip_gain, tokens, cotangent, gate, act, x, state, narrow, narrow_t, post, rate)

    dfilt, draw, offset_grad, taps_grad, bias_grad, decay_grad = pl.pallas_call(
        leave_kernel,
        grid_spec=pltpu.PrefetchScalarGridSpec(
            num_scalar_prefetch=1,
            grid=grid,
            in_specs=[
                ahead(CHANNELS), ahead(CHANNELS), ahead(CHANNELS), ahead(48), ahead(INNER), ahead(256), ahead(120),
                states(False), states(False), whole((48, 1)),
            ],
            out_specs=[
                ahead(CHANNELS), ahead(48),
                whole((CHANNELS, SPAN)), whole((CONV, CHANNELS, SPAN)),
                whole((48, SPAN)), whole((48, SPAN)),
            ],
            scratch_shapes=[
                pltpu.VMEM((INNER, SPAN), f32),
                pltpu.VMEM((HEADS, SPAN), f32),
                pltpu.VMEM((CHANNELS, BLOCK), f32),
                pltpu.VMEM((CHANNELS, SPAN), f32),
            ],
        ),
        out_shape=[
            sds((count, CHANNELS, length), bf16),
            sds((count, 48, length), bf16),
            sds((CHANNELS, SPAN), f32),
            sds((CONV, CHANNELS, SPAN), f32),
            sds((48, SPAN), f32),
            sds((48, SPAN), f32),
        ],
        compiler_params=params,
        name="leave",
    )(lengths, filt, act, fin, x, dval, dio, sums, dstate, rstate, rate)

    slope, wide_grad, time_grad, pre_grad = pl.pallas_call(
        widen_kernel,
        grid_spec=pltpu.PrefetchScalarGridSpec(
            num_scalar_prefetch=1,
            grid=grid,
            in_specs=[
                tall(False), tall(False), ahead(INNER), ahead(CHANNELS),
                pl.BlockSpec(
                    (1, CHANNELS, SPAN),
                    lambda s, c, *_: (s, 0, jnp.minimum(SUBS * (c + 1), spans - 1)),
                ),
                ahead(48),
                whole((D, WIDE)), whole((D, 48)), whole((1, D)), whole((CHANNELS, 8)),
            ],
            out_specs=[tall(False), whole((D, WIDE)), whole((D, 48)), whole((8, D))],
            scratch_shapes=[pltpu.VMEM((WIDE, BLOCK), bf16)],
        ),
        out_shape=[
            sds((count, length, D), bf16),
            sds((D, WIDE), f32),
            sds((D, 48), f32),
            sds((8, D), f32),
        ],
        compiler_params=params,
        name="widen",
    )(lengths, tokens, cotangent, dgate, dfilt, dfilt, draw, wide, time, pre, cols)

    decay_rows = jnp.sum(decay_grad, axis=1)
    return (
        result,
        slope,
        wide_grad,
        time_grad,
        narrow_grad,
        jnp.sum(taps_grad, axis=2),
        jnp.sum(offset_grad, axis=1),
        jnp.sum(pre_grad, axis=0),
        jnp.sum(post_grad, axis=1),
        jnp.sum(bias_grad, axis=1),
        decay_rows[:HEADS] + decay_rows[HEADS:],
        jnp.sum(skip_grad.reshape(HEADS, HEADDIM * SPAN), axis=1),
    )


def small_sizes(timestep_weight, filter_weight, filter_offset, prenorm_gain, postnorm_gain):
    sizes = [
        timestep_weight.size,
        filter_weight.size,
        filter_offset.size,
        prenorm_gain.size,
        postnorm_gain.size,
    ]
    used = sum(sizes)
    width = (used + 127) // 128 * 128
    return (sizes, used, width)


def pack_own(timestep_weight, filter_weight, filter_offset, prenorm_gain, postnorm_gain, width):
    joined = jnp.concatenate(
        [
            timestep_weight.reshape(-1),
            filter_weight.reshape(-1),
            filter_offset,
            prenorm_gain,
            postnorm_gain,
        ]
    )
    return jnp.pad(joined, (0, width - joined.shape[0]))


def unpack_rows(rows, sizes, conv_taps):
    count = rows.shape[0]
    starts = [0]
    for amount in sizes:
        starts.append(starts[-1] + amount)
    timestep = rows[:, starts[0] : starts[1]].reshape(-1, 2 * HEADS)
    filter_piece = rows[:, starts[1] : starts[2]].reshape(count, conv_taps, -1)
    smoother = jnp.transpose(filter_piece, (1, 0, 2)).reshape(conv_taps, -1)
    shifter = rows[:, starts[2] : starts[3]].reshape(-1)
    prenorm = rows[:, starts[3] : starts[4]].reshape(-1)
    postnorm = rows[:, starts[4] : starts[5]].reshape(-1)
    return (timestep, smoother, shifter, prenorm, postnorm)


def pack_grads(
    timestep_grad, smoother_grad, shifter_grad, prenorm_grad, postnorm_grad, count, width
):
    conv_taps = smoother_grad.shape[0]
    filter_rows = jnp.transpose(smoother_grad.reshape(conv_taps, count, -1), (1, 0, 2)).reshape(
        count, -1
    )
    joined = jnp.concatenate(
        [
            timestep_grad.reshape(count, -1),
            filter_rows,
            shifter_grad.reshape(count, -1),
            prenorm_grad.reshape(count, -1),
            postnorm_grad.reshape(count, -1),
        ],
        axis=1,
    )
    return jnp.pad(joined, ((0, 0), (0, width - joined.shape[1])))


def local(
    tokens,
    cotangent,
    lengths,
    widen_weight,
    timestep_weight,
    narrow_weight,
    filter_weight,
    filter_offset,
    prenorm_gain,
    postnorm_gain,
    timestep_bias,
    decay_log,
    skip_gain,
):
    count = lax.axis_size("shard")
    sizes, used, width = small_sizes(
        timestep_weight, filter_weight, filter_offset, prenorm_gain, postnorm_gain
    )
    own_small = pack_own(
        timestep_weight, filter_weight, filter_offset, prenorm_gain, postnorm_gain, width
    )
    widen = lax.all_gather(widen_weight, "shard", axis=0, tiled=True)
    narrow = lax.all_gather(narrow_weight, "shard", axis=0, tiled=True)
    small = lax.all_gather(own_small, "shard", axis=0, tiled=True)
    timestep, smoother, shifter, prenorm, postnorm = unpack_rows(
        small.reshape(count, width), sizes, CONV
    )
    (
        result, slope, widen_grad, timestep_grad, narrow_grad, smoother_grad, shifter_grad,
        prenorm_grad, postnorm_grad, bias_grad, decay_grad, skip_grad,
    ) = layer(
        tokens, cotangent, lengths, widen, timestep, narrow, smoother, shifter, prenorm, postnorm,
        timestep_bias, decay_log, skip_gain,
    )
    small_grad = pack_grads(
        timestep_grad, smoother_grad, shifter_grad, prenorm_grad, postnorm_grad, count, width
    )
    shares = (
        lax.psum_scatter(widen_grad, "shard", scatter_dimension=0, tiled=True),
        lax.psum_scatter(narrow_grad, "shard", scatter_dimension=0, tiled=True),
        lax.psum_scatter(small_grad, "shard", scatter_dimension=0, tiled=True),
    )
    summed = lax.psum(shares, "rep")
    heads_summed = lax.psum((bias_grad, decay_grad, skip_grad), ("rep", "shard"))
    timestep_out, filter_out, offset_out, prenorm_out, postnorm_out = unpack_rows(
        summed[2], sizes, CONV
    )
    return (
        result, slope, summed[0], timestep_out, summed[1], filter_out, offset_out, prenorm_out,
        postnorm_out, *heads_summed,
    )


def solution(mesh):
    placed = (
        P(("rep", "shard"), None, None),
        P(("rep", "shard"), None, None),
        P(("rep", "shard")),
        P("shard", None),
        P("shard", None),
        P("shard", None),
        P(None, "shard"),
        P("shard"),
        P("shard"),
        P("shard"),
        P(),
        P(),
        P(),
    )
    return jax.shard_map(
        local,
        mesh=mesh,
        in_specs=placed,
        out_specs=(
            P(("rep", "shard"), None, None),
            P(("rep", "shard"), None, None),
            P("shard", None),
            P("shard", None),
            P("shard", None),
            P(None, "shard"),
            P("shard"),
            P("shard"),
            P("shard"),
            P(),
            P(),
            P(),
        ),
        check_vma=False,
    )
```

time: 3830 us -> 956 us (0.25); the launches traced: 3770 us -> 956 us
  local copies, waits for them, and re-layouts: 1910 us -> 33.7 us
  matrix products: 895 us -> 0 us
  other arithmetic: 573 us -> 6.19 us
  Pallas kernels: 0 us -> 393 us
  blocking collectives: 84.2 us -> 180 us
  waiting for transfers between devices: 240 us -> 327 us
  loops' own time: 57 us -> 0 us
    dynamic_update_slice x96 -> x0, local copies, waits for them, and re-layouts: 1220 us -> none  [span_scan(): _, outputs = lax.scan(jax.checkpoint(advance), initial, pieces)]
    dot_general x210 -> x0, matrix products: 837 us -> none  [the longest x48 447 us: advance(): inside = jnp.einsum('hts,shp->thp', weights, value_piece, precision=precise)]
    pallas_call x0 -> x4, Pallas kernels: none -> 393 us  [the longest x1 176 us: layer(): pl.pallas_call(middle_kernel, grid_spec=pltpu.PrefetchScalarGridSpec(num_...]
    reshape x48 -> x2, local copies, waits for them, and re-layouts: 178 us -> 0.19 us  [the longest x1 0.1 us: unpack_rows(): smoother = jnp.transpose(filter_piece, (1, 0, 2)).reshape(conv_taps, -1)]
    another operation x195 -> x0, other arithmetic: 148 us -> none
    rev x20 -> x0, local copies, waits for them, and re-layouts: 126 us -> none  [the longest x4 49.8 us: mixer_block(): jnp.flip(scanner(jnp.flip(values, 0), jnp.flip(steps[:, HEADS:], 0), rate...]
    mul x38 -> x1, other arithmetic: 114 us -> 0.66 us  [layer(): rate = -jnp.exp(decay_log) * LOG2E]
    reduce_sum x42 -> x8, other arithmetic: 114 us -> 4.27 us  [the longest x1 3.06 us: layer(): jnp.sum(taps_grad, axis=2)]
  transfers between devices with their start and end apart: 6 -> 6, of which waited for: 4 -> 5; matrix products, arithmetic and copies ran while one was open for 6% -> 3% of each run, Pallas kernels for 0% -> 14%
where the time goes in v1:
time: 956 us
  Pallas kernels  393 us (41%)
  waiting for transfers between devices  327 us (34%)
  blocking collectives  180 us (19%)
  local copies, waits for them, and re-layouts  33.7 us (4%)
  between operations  14.4 us (2%)
    pallas_call x1, Pallas kernels, layer(): pl.pallas_call(middle_kernel, grid_spec=pltpu.PrefetchScalarGridSpec(num_...  176 us
    psum x1, blocking collectives, local(): lax.psum((bias_grad, decay_grad, skip_grad), ('rep', 'shard'))  136 us
    reduce_scatter x1, waiting for transfers between devices, local(): lax.psum_scatter(widen_grad, 'shard', scatter_dimension=0, tiled=True)  126 us
    pallas_call x1, Pallas kernels, layer(): pl.pallas_call(enter_kernel, grid_spec=pltpu.PrefetchScalarGridSpec(num_s...  82.7 us
    all_gather x1, waiting for transfers between devices, local(): widen = lax.all_gather(widen_weight, 'shard', axis=0, tiled=True)  81.5 us
    unnamed x7, waiting for transfers between devices  74.6 us
    pallas_call x1, Pallas kernels, layer(): pl.pallas_call(widen_kernel, grid_spec=pltpu.PrefetchScalarGridSpec(num_s...  72.1 us
    pallas_call x1, Pallas kernels, layer(): pl.pallas_call(leave_kernel, grid_spec=pltpu.PrefetchScalarGridSpec(num_s...  62.7 us
  transfers between devices with their start and end apart: 6, of which 5 were waited for; matrix products, arithmetic and copies ran while one was open for 3% of the time, Pallas kernels for 14%

profile of v1, /device:TPU:0, one launch (start us, length us, event | category | flops | bytes accessed | tf_op | source)
XLA Modules:
  0.0 955.7 jit_solution(17966876726256234228)
XLA Ops:
  7.2 0.7 all-gather.6.cloned.1.call-update
  8.0 0.7 all-gather.4.cloned.1.call-update
  8.7 0.8 copy.74
  9.5 0.1 reshape.100
  9.6 0.8 reshape.101
  10.4 2.1 concatenate.12
  12.5 33.0 %all-gather = bf16[8,1,6016]{2,1,0:T(2,128)(2,1)S(1)} all-gather(bf16[1,1,6016]{2,1,0:T(2,128)(2,1)S(1)} %reshape.117), channel_id=1, replica_groups=mesh['rep'=4,'shard'=8] {'shard'}, dimensions={0}, use_global_device_ids=true | all-gather | bytes 108288 | tf_op jit(solution)/shard_map/all_gather | solution.py:879
  46.1 1.2 copy.77
  47.4 0.2 reshape.103.time_ref
  47.6 0.8 copy.75
  48.4 0.7 reshape.116.pre_ref
  49.1 0.7 negate_multiply_fusion
  49.8 0.7 copy.80.rate_ref
  50.5 1.3 copy.79.bias_ref
  51.9 0.7 convert_element_type.31
  52.6 1.0 pad_convert_fusion.post_ref
  53.5 11.9 %all-gather.6.cloned.1.call-done.narrow_ref = bf16[1536,768]{1,0:T(8,128)(2,1)} async-done(((bf16[192,768]{1,0:T(8,128)(2,1)}), bf16[1536,768]{1,0:T(8,128)(2,1)}) %all-gather.6.cloned.1.call-update) | async-done | bytes 2359312 | tf_op jit(solution)/shard_map/all_gather | solution.py:878
  65.5 4.3 copy.81
  69.7 81.5 %all-gather.4.cloned.1.call-done.wide_ref = bf16[768,3328]{1,0:T(8,128)(2,1)} async-done(((bf16[96,3328]{1,0:T(8,128)(2,1)}), bf16[768,3328]{1,0:T(8,128)(2,1)}) %all-gather.4.cloned.1.call-update) | async-done | bytes 5111824 | tf_op jit(solution)/shard_map/all_gather | solution.py:877
  151.3 7.8 copy.78.wide_ref
  159.0 82.7 %enter.1 = (bf16[2,1536,1024]{2,1,0:T(8,128)(2,1)}, bf16[2,1792,1024]{2,1,0:T(8,128)(2,1)}, bf16[2,1792,1024]{2,1,0:T(8,128)(2,1)}, bf16[2,1792,1024]{2,1,0:T(8,...) custom-call(s32[2]{0:T(128)} %len_ref.7, bf16[2,1024,768]{2,1,0:T(8,128)(2,1)} %tok_ref.5, ...), custom_call_target="tpu_custom_call" | custom-call | tf_op jit(solution)/shard_map/enter/pallas_call | solution.py:648
  241.7 176.0 %middle.1 = (bf16[2,1024,768]{2,1,0:T(8,128)(2,1)}, bf16[2,1536,1024]{2,1,0:T(8,128)(2,1)}, bf16[2,1536,1024]{2,1,0:T(8,128)(2,1)}, f32[2,256,1024]{2,1,0:T(8,12...) custom-call(s32[2]{0:T(128)} %len_ref.7, ...), custom_call_target="tpu_custom_call" | custom-call | tf_op jit(solution)/shard_map/middle/pallas_call | solution.py:677
  417.7 0.2 reduce-scatter.3.cloned.1.call-start
  417.9 62.7 %leave.1 = (bf16[2,1792,1024]{2,1,0:T(8,128)(2,1)}, bf16[2,48,1024]{2,1,0:T(8,128)(2,1)}, f32[1792,128]{1,0:T(8,128)}, f32[4,1792,128]{2,1,0:T(8,128)}, f32[48,128]{1,0:T(8,128)}, /*index=5*/f32[48,128]{1,0:T(8,128)}) custom-call(s32[2]{0:T(128)} %len_ref.7, bf16[2,1792,1024]{2,1,0:T(8,128)(2,1)} %get-tuple-element.44.filt_ref, ...), custom_call_target="tpu_custom_call" | custom-call | tf_op jit(solution)/shard_map/leave/pallas_call | solution.py:718
  480.6 72.1 %widen.1 = (bf16[2,1024,768]{2,1,0:T(8,128)(2,1)}, f32[768,3328]{1,0:T(8,128)}, f32[768,48]{1,0:T(8,128)}, f32[8,768]{1,0:T(8,128)}) custom-call(s32[2]{0:T(128)} %len_ref.7, bf16[2,1024,768]{2,1,0:T(8,128)(2,1)} %tok_ref.5, bf16[2,1024,768]{2,1,0:T(8,128)(2,1)} %cot_ref.3, bf16[2,1536,1024]{2,1,0:T(8,128)(2,1)} %get-tuple-element.43.dgate_ref, ...), custom_call_target="tpu_custom_call" | custom-call | tf_op jit(solution)/shard_map/widen/pallas_call | solution.py:751
  552.9 0.5 copy-done.8
  553.4 0.6 dynamic-slice
  554.1 0.1 reduce_sum.74
  554.2 0.3 reduce_sum.76
  554.5 0.1 reduce_sum.78
  554.7 0.2 reshape.106
  555.0 3.1 reduce_sum.70
  558.3 0.3 reduce_sum.71
  558.7 0.3 reduce_sum.73
  559.0 0.7 concatenate.15
  559.9 136.4 %all-reduce.2 = (f32[48]{0:T(128)}, f32[24]{0:T(128)}, f32[24]{0:T(128)}) all-reduce(f32[48]{0:T(128)S(1)} %reduce_sum.74, f32[24]{0:T(128)S(1)} %slice_add_fusion, f32[24]{0:T(128)S(1)} %reduce_sum.78), channel_id=1, replica_groups=mesh['rep'=4,'shard'=8] {'rep','shard'}, use_global_device_ids=true, to_apply=%region_11.12 | all-reduce | flops 96 | bytes 768 | tf_op jit(solution)/shard_map/psum | solution.py:899
  696.3 125.6 %reduce-scatter.3.cloned.1.call-done = f32[96,3328]{1,0:T(8,128)} async-done(((f32[768,3328]{1,0:T(8,128)}), f32[96,3328]{1,0:T(8,128)}) %reduce-scatter.3.cloned.1.call-update) | async-done | bytes 1277968 | tf_op jit(solution)/shard_map/reduce_scatter | solution.py:894
  821.9 73.2 %all-reduce.7.cloned.1.call-done = f32[8,6016]{1,0:T(8,128)} async-done(((f32[8,6016]{1,0:T(8,128)}), f32[8,6016]{1,0:T(8,128)}) %all-reduce.7.cloned.1.call-update) | async-done | bytes 192528
  895.1 1.6 constant_dynamic-slice_fusion
  896.7 10.8 %psum.43 = f32[1,6016]{1,0:T(1,128)S(1)} all-reduce(f32[1,6016]{1,0:T(1,128)S(1)} %constant_dynamic-slice_fusion), channel_id=1, replica_groups=mesh['rep'=4,'shard'=8] {'rep'}, use_global_device_ids=true, to_apply=%region_7.8 | all-reduce | flops 6016 | bytes 48128 | tf_op jit(solution)/shard_map/psum | solution.py:898
  907.6 0.6 slice.57
  908.2 0.6 slice.55
  908.9 0.7 copy.86
  909.6 0.7 reshape_transpose_reshape.3
  910.3 0.6 slice_bitcast_fusion
  910.9 33.6 %all-reduce.9.cloned.1.call-done = (f32[96,3328]{1,0:T(8,128)}, f32[192,768]{1,0:T(8,128)}) async-done(((f32[96,3328]{1,0:T(8,128)}, f32[192,768]{1,0:T(8,128)}), (f32[96,3328]{1,0:T(8,128)}, f32[192,768]{1,0:T(8,128)})) %all-reduce.9.cloned.1.call-update) | async-done | bytes 1867792 | tf_op jit(solution)/shard_map/psum | solution.py:898
  944.5 2.4 copy.93
  946.9 1.9 copy.94
  (55 shorter events, 1.8 us)
Async XLA Ops:
  7.2 58.3 %all-gather.6.cloned.1.call-start = ((), (), s32[]{:S(2)}) async-start(), calls=%async_computation.3 | async-start | bytes 2654208 | tf_op jit(solution)/shard_map/all_gather | solution.py:878
  7.9 143.4 %all-gather.4.cloned.1.call-start = ((), (), s32[]{:S(2)}) async-start(), calls=%async_computation.2 | async-start | bytes 5750784 | tf_op jit(solution)/shard_map/all_gather | solution.py:877
  8.7 687.6 %reduce-scatter.5.cloned.1.call-start = ((), (), s32[]{:S(2)}) async-start(), calls=%async_computation.5 | async-start | bytes 5308416 | tf_op jit(solution)/shard_map/reduce_scatter | solution.py:895
  47.6 111.5 %copy-start = (bf16[768,48]{1,0:T(8,128)(2,1)}, bf16[768,48]{1,0:T(8,128)(2,1)S(1)}, u32[]{:S(2)}) copy-start(bf16[768,48]{1,0:T(8,128)(2,1)S(1)} %reshape.103.time_ref) | copy-start | bytes 221188
  417.7 404.2 %reduce-scatter.3.cloned.1.call-start = ((), (), s32[]{:S(2)}) async-start(), calls=%async_computation.4 | async-start | bytes 11501568 | tf_op jit(solution)/shard_map/reduce_scatter | solution.py:894
  552.7 0.7 copy-start.8
  552.7 1.2 copy-start.6
  552.7 1.3 copy-start.5
  552.7 1.4 copy-start.3
  552.8 1.9 copy-start.4
  552.8 2.1 copy-start.7
  552.8 5.5 copy-start.1
  552.8 5.8 copy-start.2
  552.8 342.3 %all-reduce.7.cloned.1.call-start = ((), (), s32[]{:S(2)}) async-start(), calls=%async_computation.6 | async-start | bytes 385024
  559.8 384.7 %all-reduce.9.cloned.1.call-start = ((), (), s32[]{:S(2)}) async-start(), calls=%async_computation.7 | async-start | bytes 3735552 | tf_op jit(solution)/shard_map/psum | solution.py:898
Sparse Core Ops, SparseCore 0:
  10.2 55.2 all-gather.5
  67.7 83.5 all-gather.3
  417.8 161.5 reduce-scatter.4
  583.0 238.8 reduce-scatter.2
  826.0 69.0 all-reduce.6
  897.5 46.9 all-reduce.8

commit v2 on v1

--- a/solution.py
+++ b/solution.py
@@ -82,16 +82,22 @@
     act_o,
     x_o,
     state_o,
-    proj_s,
+    last_s,
     run_s,
+    taps_s,
 ):
     seq = pl.program_id(0)
     block = pl.program_id(1)
     length = len_ref[seq]
 
+    @pl.when((seq == 0) & (block == 0))
+    def _():
+        for k in range(CONV + 1):
+            taps_s[k] = jnp.broadcast_to(taps_ref[:, k : k + 1], (CHANNELS, SPAN))
+
     @pl.when(block == 0)
     def _():
-        proj_s[:, BLOCK:] = jnp.zeros((CHANNELS, SPAN), f32)
+        last_s[...] = jnp.zeros_like(last_s)
         run_s[...] = jnp.zeros_like(run_s)
 
     @pl.when(block * BLOCK < length)
@@ -100,35 +106,42 @@
         scale = lax.rsqrt(jnp.mean(tok * tok, axis=-1, keepdims=True) + EPS)
         normed = (tok * scale * pre_ref[...]).astype(bf16)
         x_o[0] = mm_nt(time_ref[...], normed) + bias_ref[...]
-        proj_s[:, :SPAN] = proj_s[:, BLOCK:]
+        place = block * BLOCK + lax.broadcasted_iota(jnp.int32, (1, BLOCK), 1)
+        mask = (place < length).astype(f32)
+
+        def project(i):
+            fin_o[0, i * 256 : (i + 1) * 256, :] = mm_nt(
+                wide_ref[INNER + i * 256 : INNER + (i + 1) * 256, :], normed
+            ).astype(bf16)
+
+        def filter_rows(i):
+            r = slice(i * 32, (i + 1) * 32)
+            now = fin_o[0, r, :]
+            w = jnp.concatenate([last_s[r, :], now], axis=1)
+            last_s[r, :] = now[:, SPAN:]
+            twice = lambda k: jnp.concatenate([taps_s[k, r, :]] * 2, axis=1)
+            acc = twice(4) + twice(3) * now.astype(f32)
+            for lag in range(1, CONV):
+                moved = pltpu.roll(w, lag, 1)[:, SPAN:].astype(f32)
+                acc = acc + twice(3 - lag) * moved
+            filt_o[0, r, :] = acc.astype(bf16)
+            act = acc * sigmoid(acc)
+            if i < INNER // 32:
+                act = act * mask
+            act_o[0, r, :] = act.astype(bf16)
+
+        for i in range(CHANNELS // 256):
+            project(i)
+            if i:
+                for j in range(8):
+                    filter_rows((i - 1) * 8 + j)
         for i in range(INNER // 256):
             gate_o[0, i * 256 : (i + 1) * 256, :] = mm_nt(
                 wide_ref[i * 256 : (i + 1) * 256, :], normed
             ).astype(bf16)
-        for i in range(CHANNELS // 256):
-            proj_s[i * 256 : (i + 1) * 256, SPAN:] = mm_nt(
-                wide_ref[INNER + i * 256 : INNER + (i + 1) * 256, :], normed
-            )
-        place = block * BLOCK + lax.broadcasted_iota(jnp.int32, (1, BLOCK), 1)
-        mask = (place < length).astype(f32)
-
-        def filter_rows(i, masked):
-            r = pl.ds(pl.multiple_of(i * 32, 32), 32)
-            w = proj_s[r, :]
-            taps = taps_ref[r, :]
-            acc = taps[:, 4:5] + taps[:, 3:4] * w[:, SPAN:]
-            for lag in range(1, CONV):
-                moved = pltpu.roll(w, lag, 1)[:, SPAN:]
-                acc = acc + taps[:, 3 - lag : 4 - lag] * moved
-            fin_o[0, r, :] = w[:, SPAN:].astype(bf16)
-            filt_o[0, r, :] = acc.astype(bf16)
-            act = acc * sigmoid(acc)
-            if masked:
-                act = act * mask
-            act_o[0, r, :] = act.astype(bf16)
-
-        lax.fori_loop(0, INNER // 32, lambda i, _: filter_rows(i, True), None)
-        lax.fori_loop(INNER // 32, CHANNELS // 32, lambda i, _: filter_rows(i, False), None)
+            if i == 0:
+                for j in range(8):
+                    filter_rows((CHANNELS // 256 - 1) * 8 + j)
 
         lane = lax.broadcasted_iota(jnp.int32, (1, SPAN), 1)
 
@@ -182,12 +195,16 @@
     skip_o,
     run_s,
     grun_s,
-    mixed_s,
+    ahead_s,
+    behind_s,
     gated_s,
     dgn_s,
     spread_s,
     matrix_s,
     held_s,
+    slope_s,
+    norm_s,
+    gain_s,
 ):
     seq = pl.program_id(0)
     step = pl.program_id(1)
@@ -199,6 +216,7 @@
         narrow_o[...] = jnp.zeros_like(narrow_o)
         post_o[...] = jnp.zeros_like(post_o)
         skip_o[...] = jnp.zeros_like(skip_o)
+        gain_s[...] = jnp.broadcast_to(post_ref[:, :1], (INNER, SPAN))
 
     @pl.when(step == 0)
     def _():
@@ -215,16 +233,23 @@
         lower = rows_i < cols_i
         upper = rows_i > cols_i
         lane = lax.broadcasted_iota(jnp.int32, (1, SPAN), 1)
+        place = block * BLOCK + lax.broadcasted_iota(jnp.int32, (BLOCK, 1), 0)
+        inside = place < length
+        slope_s[...] = jnp.where(inside, cot_ref[0].astype(f32), 0.0).astype(bf16)
+        for i in range(3):
+            rows = slice(i * 512, (i + 1) * 512)
+            dgn_s[rows, :] = mm_nt(narrow_ref[rows, :], slope_s[...])
+        zero = jnp.zeros((64, SPAN), bf16)
 
         def span_scores(cols):
             fi = act_ref[0, INNER : INNER + 64, cols]
             fo = act_ref[0, INNER + 64 : INNER + 128, cols]
             ri = act_ref[0, INNER + 128 : INNER + 192, cols]
             ro = act_ref[0, INNER + 192 : INNER + 256, cols]
-            ahead = mm_tn(fi, fo)
-            behind = mm_tn(ri, ro)
-            scores = jnp.where(lower, ahead, jnp.where(upper, behind, 0.0))
-            return fi, fo, ri, ro, scores
+            return fi, fo, ri, ro
+
+        def fold(value):
+            return jnp.sum(value.reshape(8, 8, SPAN), axis=0)
 
         def forward_span(back, _):
             sub = SUBS - 1 - back
@@ -238,9 +263,13 @@
             out_f = jnp.exp2(fcum)
             out_r = jnp.exp2(rcum)
             decay = jnp.exp2(rcum[:, :1])
-            fi, fo, ri, ro, scores = span_scores(cols)
+            fi, fo, ri, ro = span_scores(cols)
+            ahead_scores = jnp.where(lower, mm_tn(fi, fo), 0.0)
+            behind_scores = jnp.where(upper, mm_tn(ri, ro), 0.0)
             fo = fo.astype(f32)
             ro = ro.astype(f32)
+            squares = jnp.zeros((8, SPAN), f32)
+            dots = jnp.zeros((8, SPAN), f32)
             for h in range(HEADS):
                 rows = slice(h * 64, (h + 1) * 64)
                 power = jnp.where(
@@ -250,15 +279,21 @@
                 )
                 spread = jnp.exp2(power)
                 spread_s[sub, h] = spread.astype(bf16)
+                low = (spread * ahead_scores).astype(bf16)
+                high = (spread * behind_scores).astype(bf16)
+                out_low = (fo * out_f[h : h + 1]).astype(bf16)
+                out_high = (ro * out_r[h : h + 1]).astype(bf16)
+                matrix_s[sub, h, :SPAN] = low
+                matrix_s[sub, h, SPAN : 2 * SPAN] = high
+                matrix_s[sub, h, 2 * SPAN : 2 * SPAN + 64] = out_low
+                matrix_s[sub, h, 2 * SPAN + 64 :] = out_high
                 matrix = jnp.concatenate(
                     [
-                        (spread * scores).astype(bf16),
-                        (fo * out_f[h : h + 1]).astype(bf16),
-                        (ro * out_r[h : h + 1]).astype(bf16),
+                        jnp.concatenate([low, out_low, zero], axis=0),
+                        jnp.concatenate([high, zero, out_high], axis=0),
                     ],
-                    axis=0,
+                    axis=1,
                 )
-                matrix_s[sub, h] = matrix
                 state = state_ref[0, sub, rows, :]
                 run = run_s[rows, :]
                 rstate_o[0, sub, rows, :] = run
@@ -266,72 +301,42 @@
                 held_s[sub, rows, :] = held
                 run_s[rows, :] = run * decay[h : h + 1] + state
                 values = act_ref[0, rows, cols]
-                both = jnp.concatenate([values, held], axis=1)
-                mixed_s[rows, cols] = mm(both, matrix) + skip_ref[h] * values.astype(f32)
+                pair = mm(jnp.concatenate([values, held], axis=1), matrix)
+                ahead = pair[:, :SPAN]
+                behind = pair[:, SPAN:]
+                ahead_s[rows, cols] = ahead
+                behind_s[rows, cols] = behind
+                mixed = ahead + behind + skip_ref[h] * values.astype(f32)
+                gate = gate_ref[0, rows, cols].astype(f32)
+                gated = mixed * (gate * sigmoid(gate))
+                gated_s[rows, cols] = gated
+                squares = squares + fold(gated * gated)
+                dots = dots + fold(gated * gain_s[rows, :] * dgn_s[rows, cols])
+            rs = lax.rsqrt(jnp.sum(squares, axis=0, keepdims=True) * (1.0 / INNER) + EPS)
+            pull = rs * rs * rs * (jnp.sum(dots, axis=0, keepdims=True) * (1.0 / INNER))
+            norm_s[:1, cols] = rs
+            norm_s[1:2, cols] = pull
             return None
 
         lax.fori_loop(0, SUBS, forward_span, None)
-
-        def gate_rows(i, total):
-            r = pl.ds(pl.multiple_of(i * 32, 32), 32)
-            gate = gate_ref[0, r, :].astype(f32)
-            gated = mixed_s[r, :] * (gate * sigmoid(gate))
-            gated_s[r, :] = gated
-            return total + jnp.sum((gated * gated).reshape(4, 8, BLOCK), axis=0)
-
-        squares = lax.fori_loop(0, INNER // 32, gate_rows, jnp.zeros((8, BLOCK), f32))
-        rs = lax.rsqrt(jnp.sum(squares, axis=0, keepdims=True) * (1.0 / INNER) + EPS)
+        rs = norm_s[:1, :]
 
         def norm_rows(i, _):
             r = pl.ds(pl.multiple_of(i * 32, 32), 32)
-            held_gn = gated_s[r, :] * rs * post_ref[r, :1]
-            dgate_o[0, r, :] = held_gn.astype(bf16)
+            kept = gated_s[r, :] * rs
+            gain = gain_s[r, :]
+            dgate_o[0, r, :] = (kept * jnp.concatenate([gain, gain], axis=1)).astype(bf16)
+            product = kept * dgn_s[r, :]
+            post_o[r, :] += product[:, :SPAN] + product[:, SPAN:]
             return None
 
-        lax.fori_loop(0, INNER // 32, norm_rows, None)
+        lax.fori_loop(0, INNER // 32, norm_rows, None, unroll=8)
         gnormed = dgate_o[0]
-        place = block * BLOCK + lax.broadcasted_iota(jnp.int32, (BLOCK, 1), 0)
-        inside = place < length
         branch = mm(turned_ref[...], gnormed)
         result_o[0] = (tok_ref[0].astype(f32) + jnp.where(inside, branch.T, 0.0)).astype(bf16)
-        slope = jnp.where(inside, cot_ref[0].astype(f32), 0.0).astype(bf16)
         for i in range(3):
             rows = slice(i * 512, (i + 1) * 512)
-            narrow_o[rows, :] += mm(gnormed[rows], slope)
-            dgn_s[rows, :] = mm_nt(narrow_ref[rows, :], slope)
-
-        def dot_rows(i, total):
-            r = pl.ds(pl.multiple_of(i * 32, 32), 32)
-            product = dgn_s[r, :] * gated_s[r, :]
-            kept = product * rs
-            post_o[r, :] += kept[:, :SPAN] + kept[:, SPAN:]
-            weighted = product * post_ref[r, :1]
-            return total + jnp.sum(weighted.reshape(4, 8, BLOCK), axis=0)
-
-        dots = lax.fori_loop(0, INNER // 32, dot_rows, jnp.zeros((8, BLOCK), f32))
-        mean = jnp.sum(dots, axis=0, keepdims=True) * (1.0 / INNER)
-        pull = rs * rs * rs * mean
-
-        def grad_rows(i, _):
-            r = pl.ds(pl.multiple_of(i * 32, 32), 32)
-            gate = gate_ref[0, r, :].astype(f32)
-            sig = sigmoid(gate)
-            dgated = rs * post_ref[r, :1] * dgn_s[r, :] - gated_s[r, :] * pull
-            dmixed = dgated * (gate * sig)
-            dgate = dgated * mixed_s[r, :] * (sig * (1.0 + gate * (1.0 - sig)))
-            dgate_o[0, r, :] = dgate.astype(bf16)
-            dgn_s[r, :] = dmixed
-            product = dmixed * act_ref[0, r, :].astype(f32)
-            skip_o[r, :] += product[:, :SPAN] + product[:, SPAN:]
-            return None
-
-        lax.fori_loop(0, INNER // 32, grad_rows, None)
-
-        ones_row = (lax.broadcasted_iota(jnp.int32, (8, 2 * SPAN), 1) // SPAN) == (
-            lax.broadcasted_iota(jnp.int32, (8, 2 * SPAN), 0)
-        )
-        ones_row = ones_row.astype(bf16)
-        ones_flat = jnp.ones((8, SPAN), bf16)
+            narrow_o[rows, :] += mm(gnormed[rows], slope_s[...])
 
         def backward_span(back, _):
             sub = SUBS - 1 - back
@@ -340,50 +345,52 @@
             out_f = jnp.exp2(fcum)
             out_r = jnp.exp2(rcum)
             decay = jnp.exp2(fcum[:, SPAN - 1 :])
-            fi, fo, ri, ro, scores = span_scores(cols)
-            fo32 = fo.astype(f32)
-            ro32 = ro.astype(f32)
+            fi, fo, ri, ro = span_scores(cols)
+            rs = norm_s[:1, cols]
+            pull = norm_s[1:2, cols]
             dscores = jnp.zeros((SPAN, SPAN), f32)
             dfo = jnp.zeros((64, SPAN), f32)
             dro = jnp.zeros((64, SPAN), f32)
+
+            def down(value):
+                return jnp.sum(value, axis=0, keepdims=True)
+
             for h in range(HEADS):
                 rows = slice(h * 64, (h + 1) * 64)
-                dmixed = dgn_s[rows, cols]
+                gate = gate_ref[0, rows, cols].astype(f32)
+                sig = sigmoid(gate)
+                values = act_ref[0, rows, cols]
+                values32 = values.astype(f32)
+                ahead = ahead_s[rows, cols]
+                behind = behind_s[rows, cols]
+                mixed = ahead + behind + skip_ref[h] * values32
+                dgated = rs * (gain_s[rows, :] * dgn_s[rows, cols]) - gated_s[rows, cols] * pull
+                dmixed = dgated * (gate * sig)
+                dgate = dgated * mixed * (sig * (1.0 + gate * (1.0 - sig)))
+                dgate_o[0, rows, cols] = dgate.astype(bf16)
+                skip_o[h * 8 : h * 8 + 8, :] += fold(dmixed * values32)
                 dm = dmixed.astype(bf16)
-                values = act_ref[0, rows, cols]
+                dm32 = dm.astype(f32)
                 held = held_s[sub, rows, :]
-                both = jnp.concatenate([values, held], axis=1)
-                grad = mm_tn(both, dm)
-                matrix = matrix_s[sub, h]
-                first = grad[:SPAN] * spread_s[sub, h].astype(f32)
-                dscores = dscores + first
-                pairs = first * scores
-                pairs_low = jnp.where(lower, pairs, 0.0).astype(bf16)
-                stack = jnp.concatenate([pairs_low, pairs.astype(bf16)], axis=0)
-                by_row = mm(ones_row, stack)
-                by_col = mm_nt(ones_flat, stack)
-                part_f = grad[SPAN : SPAN + 64] * out_f[h : h + 1]
-                part_r = grad[SPAN + 64 :] * out_r[h : h + 1]
-                dfo = dfo + part_f
-                dro = dro + part_r
-                carried_f = jnp.sum(part_f * fo32, axis=0, keepdims=True)
-                carried_r = jnp.sum(part_r * ro32, axis=0, keepdims=True)
-                col_f = by_col[:1, :SPAN]
-                sums_o[0, h : h + 1, cols] = by_row[:1] + carried_f
-                sums_o[0, HEADS + h : HEADS + h + 1, cols] = (
-                    by_row[1:2] - by_row[:1] + carried_r
-                )
-                sums_o[0, 2 * HEADS + h : 2 * HEADS + h + 1, cols] = col_f
-                sums_o[0, 3 * HEADS + h : 3 * HEADS + h + 1, cols] = by_col[:1, SPAN:] - col_f
-                dboth = mm_nt(dm, matrix)
-                dval_o[0, rows, cols] = (dboth[:, :SPAN] + skip_ref[h] * dmixed).astype(bf16)
-                dheld = dboth[:, SPAN:]
+                grad = mm_tn(jnp.concatenate([values, held], axis=1), dm)
+                dscores = dscores + grad[:SPAN] * spread_s[sub, h].astype(f32)
+                dfo = dfo + grad[SPAN : SPAN + 64] * out_f[h : h + 1]
+                dro = dro + grad[SPAN + 64 :] * out_r[h : h + 1]
+                dall = mm_nt(dm, matrix_s[sub, h])
+                dlow = dall[:, :SPAN]
+                dhigh = dall[:, SPAN : 2 * SPAN]
+                dheld = dall[:, 2 * SPAN :]
+                dval_o[0, rows, cols] = (dlow + dhigh + skip_ref[h] * dmixed).astype(bf16)
                 run = grun_s[rows, :]
                 dstate_o[0, sub, rows, :] = jnp.where(lane < 64, run, dheld)
-                sums_o[0, 4 * HEADS + h : 4 * HEADS + h + 1, cols] = decay[h : h + 1] * jnp.sum(
-                    jnp.where(lane < 64, run * held.astype(f32), 0.0), axis=0, keepdims=True
+                grun_s[rows, :] = run * decay[h : h + 1] + dheld
+                sums_o[0, h : h + 1, cols] = down(dm32 * ahead)
+                sums_o[0, HEADS + h : HEADS + h + 1, cols] = down(dm32 * behind)
+                sums_o[0, 2 * HEADS + h : 2 * HEADS + h + 1, cols] = down(values32 * dlow)
+                sums_o[0, 3 * HEADS + h : 3 * HEADS + h + 1, cols] = down(values32 * dhigh)
+                sums_o[0, 4 * HEADS + h : 4 * HEADS + h + 1, cols] = decay[h : h + 1] * down(
+                    jnp.where(lane < 64, run * held.astype(f32), 0.0)
                 )
-                grun_s[rows, :] = run * decay[h : h + 1] + dheld
             low = jnp.where(lower, dscores, 0.0).astype(bf16)
             high = jnp.where(upper, dscores, 0.0).astype(bf16)
             dio_o[0, 0:64, cols] = mm_nt(fo, low)
@@ -520,18 +527,18 @@
             dfilt = dact * (sig * (1.0 + filt * (1.0 - sig)))
             dfilt_o[0, r, :] = dfilt.astype(bf16)
             offset_o[r, :] += dfilt[:, :SPAN] + dfilt[:, SPAN:]
-            fin = fin_ref[0, r, :].astype(f32)
+            fin = fin_ref[0, r, :]
             w = jnp.concatenate([last_s[r, :], fin], axis=1)
             last_s[r, :] = fin[:, SPAN:]
-            product = dfilt * fin
+            product = dfilt * fin.astype(f32)
             taps_o[3, r, :] += product[:, :SPAN] + product[:, SPAN:]
             for lag in range(1, CONV):
-                product = dfilt * pltpu.roll(w, lag, 1)[:, SPAN:]
+                product = dfilt * pltpu.roll(w, lag, 1)[:, SPAN:].astype(f32)
                 taps_o[3 - lag, r, :] += product[:, :SPAN] + product[:, SPAN:]
             return None
 
-        lax.fori_loop(0, INNER // 32, lambda i, _: filter_rows(i, True), None)
-        lax.fori_loop(INNER // 32, CHANNELS // 32, lambda i, _: filter_rows(i, False), None)
+        lax.fori_loop(0, INNER // 32, lambda i, _: filter_rows(i, True), None, unroll=8)
+        lax.fori_loop(INNER // 32, CHANNELS // 32, lambda i, _: filter_rows(i, False), None, unroll=8)
 
 
 def widen_kernel(
@@ -551,6 +558,7 @@
     time_o,
     pre_o,
     dproj_s,
+    taps_s,
 ):
     seq = pl.program_id(0)
     block = pl.program_id(1)
@@ -561,6 +569,8 @@
         wide_o[...] = jnp.zeros_like(wide_o)
         time_o[...] = jnp.zeros_like(time_o)
         pre_o[...] = jnp.zeros_like(pre_o)
+        for k in range(CONV):
+            taps_s[k] = jnp.broadcast_to(taps_ref[:, k : k + 1], (CHANNELS, SPAN))
 
     @pl.when(block * BLOCK >= length)
     def _():
@@ -577,17 +587,18 @@
 
         def filter_rows(i, _):
             r = pl.ds(pl.multiple_of(i * 32, 32), 32)
-            following = jnp.where(beyond, next_ref[0, r, :].astype(f32), 0.0)
-            w = jnp.concatenate([dfilt_ref[0, r, :].astype(f32), following], axis=1)
-            taps = taps_ref[r, :]
-            acc = taps[:, 3:4] * w[:, :BLOCK]
+            following = jnp.where(beyond, next_ref[0, r, :].astype(f32), 0.0).astype(bf16)
+            now = dfilt_ref[0, r, :]
+            w = jnp.concatenate([now, following], axis=1)
+            twice = lambda k: jnp.concatenate([taps_s[k, r, :]] * 2, axis=1)
+            acc = twice(3) * now.astype(f32)
             for lag in range(1, CONV):
-                moved = pltpu.roll(w, BLOCK + SPAN - lag, 1)[:, :BLOCK]
-                acc = acc + taps[:, 3 - lag : 4 - lag] * moved
+                moved = pltpu.roll(w, BLOCK + SPAN - lag, 1)[:, :BLOCK].astype(f32)
+                acc = acc + twice(3 - lag) * moved
             dproj_s[pl.ds(pl.multiple_of(INNER + i * 32, 32), 32), :] = acc.astype(bf16)
             return None
 
-        lax.fori_loop(0, CHANNELS // 32, filter_rows, None)
+        lax.fori_loop(0, CHANNELS // 32, filter_rows, None, unroll=8)
         for i in range(WIDE // 256):
             rows = slice(i * 256, (i + 1) * 256)
             wide_o[:, rows] += mm_nt(normed_t, dproj_s[rows, :])
@@ -658,8 +669,9 @@
                 ahead(INNER), ahead(CHANNELS), ahead(CHANNELS), ahead(CHANNELS), ahead(48), states(False),
             ],
             scratch_shapes=[
-                pltpu.VMEM((CHANNELS, BLOCK + SPAN), f32),
+                pltpu.VMEM((CHANNELS, SPAN), bf16),
                 pltpu.VMEM((INNER, SPAN), f32),
+                pltpu.VMEM((CONV + 1, CHANNELS, SPAN), f32),
             ],
         ),
         out_shape=[
@@ -686,7 +698,7 @@
             ],
             out_specs=[
                 tall(True), back(INNER), back(INNER), back(256), back(120), states(True), states(True),
-                whole((INNER, D)), whole((INNER, SPAN)), whole((INNER, SPAN)),
+                whole((INNER, D)), whole((INNER, SPAN)), whole((8 * HEADS, SPAN)),
             ],
             scratch_shapes=[
                 pltpu.VMEM((INNER, SPAN), f32),
@@ -694,9 +706,13 @@
                 pltpu.VMEM((INNER, BLOCK), f32),
                 pltpu.VMEM((INNER, BLOCK), f32),
                 pltpu.VMEM((INNER, BLOCK), f32),
+                pltpu.VMEM((INNER, BLOCK), f32),
                 pltpu.VMEM((SUBS, HEADS, SPAN, SPAN), bf16),
-                pltpu.VMEM((SUBS, HEADS, 2 * SPAN, SPAN), bf16),
+                pltpu.VMEM((SUBS, HEADS, 3 * SPAN, SPAN), bf16),
                 pltpu.VMEM((SUBS, INNER, SPAN), bf16),
+                pltpu.VMEM((BLOCK, D), bf16),
+                pltpu.VMEM((8, BLOCK), f32),
+                pltpu.VMEM((INNER, SPAN), f32),
             ],
         ),
         out_shape=[
@@ -709,7 +725,7 @@
             state_shape,
             sds((INNER, D), f32),
             sds((INNER, SPAN), f32),
-            sds((INNER, SPAN), f32),
+            sds((8 * HEADS, SPAN), f32),
         ],
         compiler_params=params,
         name="middle",
@@ -733,7 +749,7 @@
                 pltpu.VMEM((INNER, SPAN), f32),
                 pltpu.VMEM((HEADS, SPAN), f32),
                 pltpu.VMEM((CHANNELS, BLOCK), f32),
-                pltpu.VMEM((CHANNELS, SPAN), f32),
+                pltpu.VMEM((CHANNELS, SPAN), bf16),
             ],
         ),
         out_shape=[
@@ -763,7 +779,10 @@
                 whole((D, WIDE)), whole((D, 48)), whole((1, D)), whole((CHANNELS, 8)),
             ],
             out_specs=[tall(False), whole((D, WIDE)), whole((D, 48)), whole((8, D))],
-            scratch_shapes=[pltpu.VMEM((WIDE, BLOCK), bf16)],
+            scratch_shapes=[
+                pltpu.VMEM((WIDE, BLOCK), bf16),
+                pltpu.VMEM((CONV, CHANNELS, SPAN), f32),
+            ],
         ),
         out_shape=[
             sds((count, length, D), bf16),
@@ -788,68 +807,415 @@
         jnp.sum(post_grad, axis=1),
         jnp.sum(bias_grad, axis=1),
         decay_rows[:HEADS] + decay_rows[HEADS:],
-        jnp.sum(skip_grad.reshape(HEADS, HEADDIM * SPAN), axis=1),
+        jnp.sum(skip_grad.reshape(HEADS, 8 * SPAN), axis=1),
     )
 
 
-def small_sizes(timestep_weight, filter_weight, filter_offset, prenorm_gain, postnorm_gain):
-    sizes = [
-        timestep_weight.size,
-        filter_weight.size,
-        filter_offset.size,
-        prenorm_gain.size,
-        postnorm_gain.size,
+def peer(rep, shard):
+    return {"rep": rep, "shard": shard}
+
+
+def remote(src, dst, send, recv, device):
+    return pltpu.make_async_remote_copy(
+        src_ref=src, dst_ref=dst, send_sem=send, recv_sem=recv,
+        device_id=device, device_id_type=pl.DeviceIdType.MESH,
+    )
+
+
+def greet(devices):
+    barrier = pltpu.get_barrier_semaphore()
+    for device in devices:
+        pl.semaphore_signal(barrier, inc=1, device_id=device, device_id_type=pl.DeviceIdType.MESH)
+    pl.semaphore_wait(barrier, len(devices))
+
+
+def reduce_kernel(
+    lines, wide,
+    wide_ref, narrow_ref, small_ref, heads_ref, out_ref, heads_out_ref,
+    grads_s, near_s, sum_s, p1_s, q1_s, t0_s, t1_s, p2_s, q2_s, r_s, z_s,
+    hc_s, hx_s, hy_s, hz_s,
+    send_sem, recv_sem, hsend_sem, hrecv_sem,
+):
+    piece, rows = grads_s.shape[-3:-1]
+    shards = 2 * lines
+    tiles_wide = wide_ref.shape[1] // 128
+    tiles_narrow = narrow_ref.shape[1] // 128
+    rep = lax.axis_index("rep")
+    shard = lax.axis_index("shard")
+    core, x = lax.rem(rep, 2), lax.div(rep, 2)
+    y, z = lax.rem(shard, 2), lax.div(shard, 2)
+    sibling = peer(rep + 1 - 2 * core, shard)
+    partner = peer(rep, shard + 1 - 2 * y)
+    across = [peer(lax.rem(x + k, wide) * 2 + core, shard) for k in range(1, wide)]
+    along = [peer(rep, lax.rem(z + k, lines) * 2 + y) for k in range(1, lines)]
+    greet([sibling, partner, *across, *along])
+    started = []
+    used = [0]
+
+    def launch(src, dst, device):
+        i = used[0]
+        used[0] += 1
+        copy = remote(src, dst, send_sem.at[i], recv_sem.at[i], device)
+        copy.start()
+        started.append(copy)
+        return copy
+
+    hused = [0]
+
+    def launch_small(src, dst, device):
+        i = hused[0]
+        hused[0] += 1
+        copy = remote(src, dst, hsend_sem.at[i], hrecv_sem.at[i], device)
+        copy.start()
+        started.append(copy)
+        return copy
+
+    def add(dst, *srcs):
+        flat = 1
+        for extent in dst.shape[:-3]:
+            flat *= extent
+        shape = dst.shape[:-3]
+
+        def body(i, _):
+            where = []
+            rest = i
+            for extent in reversed(shape):
+                where.append(lax.rem(rest, extent))
+                rest = lax.div(rest, extent)
+            where = tuple(reversed(where))
+            for unit in range(dst.shape[-3]):
+                place = (*where, unit)
+                total = srcs[0][place].astype(f32)
+                for src in srcs[1:]:
+                    total = total + src[place].astype(f32)
+                dst[place] = total.astype(dst.dtype)
+            return None
+
+        lax.fori_loop(0, flat, body, None)
+
+    def pack(half, order):
+        def body(index, _):
+            start = pl.multiple_of(index * rows, 8)
+            for position in range(wide):
+                for i in range(piece):
+                    unit = ((half * wide + position) * 2 + order) * piece + i
+                    if unit < tiles_wide:
+                        value = wide_ref[pl.ds(start, rows), unit * 128 : unit * 128 + 128]
+                    elif unit < tiles_wide + 2 * tiles_narrow:
+                        lower, tile = divmod(unit - tiles_wide, tiles_narrow)
+                        begin = pl.multiple_of(2 * start + lower * rows, 8)
+                        value = narrow_ref[pl.ds(begin, rows), tile * 128 : tile * 128 + 128]
+                    elif unit == tiles_wide + 2 * tiles_narrow:
+                        value = small_ref[index]
+                    else:
+                        value = jnp.zeros((rows, 128), f32)
+                    where = (half, order, position, lax.rem(index, 2), lax.div(index, 2), i)
+                    grads_s[where] = value.astype(bf16)
+            return None
+
+        lax.fori_loop(0, shards, body, None)
+
+    def pack_half(mine, order):
+        pl.when(core == (0 if mine else 1))(lambda: pack(0, order))
+        pl.when(core == (1 if mine else 0))(lambda: pack(1, order))
+
+    hc_s[core] = heads_ref[...]
+    head = launch_small(hc_s.at[core], hc_s.at[core], sibling)
+    near = []
+    for order in range(2):
+        pack_half(False, order)
+        near.append(launch(grads_s.at[1 - core, order], near_s.at[order], sibling))
+    for order in range(2):
+        pack_half(True, order)
+    near[0].wait_recv()
+    add(sum_s.at[0], grads_s.at[core, 0], near_s.at[0])
+    p1 = [
+        launch(sum_s.at[0, lax.rem(x + k, wide)], p1_s.at[k - 1], across[k - 1])
+        for k in range(1, wide)
     ]
-    used = sum(sizes)
-    width = (used + 127) // 128 * 128
-    return (sizes, used, width)
-
-
-def pack_own(timestep_weight, filter_weight, filter_offset, prenorm_gain, postnorm_gain, width):
-    joined = jnp.concatenate(
-        [
-            timestep_weight.reshape(-1),
-            filter_weight.reshape(-1),
-            filter_offset,
-            prenorm_gain,
-            postnorm_gain,
-        ]
-    )
-    return jnp.pad(joined, (0, width - joined.shape[0]))
-
-
-def unpack_rows(rows, sizes, conv_taps):
-    count = rows.shape[0]
+    near[1].wait_recv()
+    add(sum_s.at[1], grads_s.at[core, 1], near_s.at[1])
+    q1 = launch(sum_s.at[1, :, 1 - y], q1_s, partner)
+    head.wait_recv()
+    hx_s[x] = hc_s[0] + hc_s[1]
+    heads = [launch_small(hx_s.at[x], hx_s.at[x], device) for device in across]
+    for copy in p1:
+        copy.wait_recv()
+    add(t0_s, sum_s.at[0, x], *[p1_s.at[k] for k in range(wide - 1)])
+    p2 = launch(t0_s.at[1 - y], p2_s, partner)
+    q1.wait_recv()
+    add(t1_s, sum_s.at[1, :, y], q1_s)
+    q2 = [
+        launch(t1_s.at[lax.rem(x + k, wide)], q2_s.at[k - 1], across[k - 1])
+        for k in range(1, wide)
+    ]
+    for copy in heads:
+        copy.wait_recv()
+    total = hx_s[0]
+    for k in range(1, wide):
+        total = total + hx_s[k]
+    hy_s[y] = total
+    head = launch_small(hy_s.at[y], hy_s.at[y], partner)
+    p2.wait_recv()
+    add(r_s.at[0], t0_s.at[y], p2_s)
+    z0 = [launch(r_s.at[0, lax.rem(z + k, lines)], z_s.at[0, k - 1], along[k - 1]) for k in range(1, lines)]
+    for copy in q2:
+        copy.wait_recv()
+    add(r_s.at[1], t1_s.at[x], *[q2_s.at[k] for k in range(wide - 1)])
+    z1 = [launch(r_s.at[1, lax.rem(z + k, lines)], z_s.at[1, k - 1], along[k - 1]) for k in range(1, lines)]
+    head.wait_recv()
+    hz_s[z] = hy_s[0] + hy_s[1]
+    heads = [launch_small(hz_s.at[z], hz_s.at[z], device) for device in along]
+    for order, copies in ((0, z0), (1, z1)):
+        for copy in copies:
+            copy.wait_recv()
+        add(out_ref.at[core, x, order], r_s.at[order, z], *[z_s.at[order, k] for k in range(lines - 1)])
+    shares = [launch(out_ref.at[core, x], out_ref.at[core, x], device) for device in across]
+    for copy in heads:
+        copy.wait_recv()
+    total = hz_s[0]
+    for k in range(1, lines):
+        total = total + hz_s[k]
+    heads_out_ref[...] = total
+    for copy in shares:
+        copy.wait_recv()
+    last = launch(out_ref.at[core], out_ref.at[core], sibling)
+    last.wait_recv()
+    for copy in started:
+        copy.wait_send()
+
+
+def unit_count(wide_columns, narrow_columns, wide):
+    used = wide_columns // 128 + 2 * (narrow_columns // 128) + 1
+    return -(-used // (4 * wide)) * 4 * wide
+
+
+def reduce_units(wide_grad, narrow_grad, small_grad, heads, wide, lines):
+    rows = small_grad.shape[1]
+    unit = unit_count(wide_grad.shape[1], narrow_grad.shape[1], wide) // (4 * wide)
+    piece = (unit, rows, 128)
+    copies = 2 + (wide - 1) * 3 + 2 + 2 * (lines - 1) + 1
+    small = 1 + (wide - 1) + 1 + (lines - 1)
+    vmem = pl.BlockSpec(memory_space=pltpu.VMEM)
+    return pl.pallas_call(
+        partial(reduce_kernel, lines, wide),
+        in_specs=[vmem] * 4,
+        out_specs=[vmem, vmem],
+        out_shape=[
+            jax.ShapeDtypeStruct((2, wide, 2, *piece), bf16),
+            jax.ShapeDtypeStruct((8, 128), f32),
+        ],
+        scratch_shapes=[
+            pltpu.VMEM((2, 2, wide, 2, lines, *piece), bf16),
+            pltpu.VMEM((2, wide, 2, lines, *piece), bf16),
+            pltpu.VMEM((2, wide, 2, lines, *piece), bf16),
+            pltpu.VMEM((max(wide - 1, 1), 2, lines, *piece), bf16),
+            pltpu.VMEM((wide, lines, *piece), bf16),
+            pltpu.VMEM((2, lines, *piece), bf16),
+            pltpu.VMEM((wide, lines, *piece), bf16),
+            pltpu.VMEM((lines, *piece), bf16),
+            pltpu.VMEM((max(wide - 1, 1), lines, *piece), bf16),
+            pltpu.VMEM((2, lines, *piece), bf16),
+            pltpu.VMEM((2, lines - 1, *piece), bf16),
+            pltpu.VMEM((2, 8, 128), f32),
+            pltpu.VMEM((wide, 8, 128), f32),
+            pltpu.VMEM((2, 8, 128), f32),
+            pltpu.VMEM((lines, 8, 128), f32),
+            pltpu.SemaphoreType.DMA((copies,)),
+            pltpu.SemaphoreType.DMA((copies,)),
+            pltpu.SemaphoreType.DMA((small,)),
+            pltpu.SemaphoreType.DMA((small,)),
+        ],
+        compiler_params=pltpu.CompilerParams(
+            collective_id=1, has_side_effects=True, vmem_limit_bytes=VMEM_LIMIT
+        ),
+        name="reduce",
+    )(wide_grad, narrow_grad, small_grad, heads)
+
+
+def gather_kernel(lines, cuts, wide_ref, small_ref, wide_o, small_o, send_sem, recv_sem, own_sem):
+    rep = lax.axis_index("rep")
+    shard = lax.axis_index("shard")
+    core = lax.rem(rep, 2)
+    y, z = lax.rem(shard, 2), lax.div(shard, 2)
+    half = sum(cuts)
+    sibling = peer(rep + 1 - 2 * core, shard)
+    partner = peer(rep, shard + 1 - 2 * y)
+    has_up, has_down = z < lines - 1, z > 0
+    up = peer(rep, jnp.minimum(z + 1, lines - 1) * 2 + y)
+    down = peer(rep, jnp.maximum(z - 1, 0) * 2 + y)
+    barrier = pltpu.get_barrier_semaphore()
+
+    def hello(device):
+        pl.semaphore_signal(barrier, inc=1, device_id=device, device_id_type=pl.DeviceIdType.MESH)
+
+    hello(sibling)
+    hello(partner)
+    pl.when(has_up)(lambda: hello(up))
+    pl.when(has_down)(lambda: hello(down))
+    pl.semaphore_wait(barrier, 2 + has_up.astype(jnp.int32) + has_down.astype(jnp.int32))
+
+    own = [
+        pltpu.make_async_copy(wide_ref, wide_o.at[shard], own_sem.at[0]),
+        pltpu.make_async_copy(small_ref, small_o.at[shard], own_sem.at[1]),
+    ]
+    for copy in own:
+        copy.start()
+
+    def place(order, part, ref, index, side):
+        if part:
+            return ref.at[side] if index is None else ref.at[index, side]
+        start = pl.multiple_of(side * half + (cuts[0] if order else 0), 128)
+        columns = pl.ds(start, cuts[order])
+        return ref.at[:, columns] if index is None else ref.at[index, :, columns]
+
+    def parts(order):
+        return (0, 1) if order == 0 else (0,)
+
+    def copies(way, order, index, device, mine=False, side=None):
+        side = core if side is None else side
+        made = []
+        for part in parts(order):
+            out = (wide_o, small_o)[part]
+            src = (wide_ref, small_ref)[part] if mine else out
+            made.append(
+                remote(
+                    place(order, part, src, None if mine else index, side),
+                    place(order, part, out, index, side),
+                    send_sem.at[way, order, part, index],
+                    recv_sem.at[way, order, part, index],
+                    device,
+                )
+            )
+        return made
+
+    def start(*args, **kw):
+        for copy in copies(*args, **kw):
+            copy.start()
+
+    def arrive(*args, **kw):
+        for copy in copies(*args, **kw):
+            copy.wait_recv()
+
+    def sent(*args, **kw):
+        for copy in copies(*args, **kw):
+            copy.wait_send()
+
+    other = shard + 1 - 2 * y
+
+    def index_of(line, side):
+        return line * 2 + side
+
+    start(0, 1, shard, partner, mine=True)
+    pl.when(has_up)(lambda: start(1, 0, shard, up, mine=True))
+    pl.when(has_down)(lambda: start(2, 0, shard, down, mine=True))
+    pl.when(has_up)(lambda: start(1, 1, shard, up, mine=True))
+    pl.when(has_down)(lambda: start(2, 1, shard, down, mine=True))
+    start(0, 0, shard, partner, mine=True)
+    arrive(0, 1, other, partner)
+    pl.when(has_up)(lambda: start(1, 1, other, up))
+    pl.when(has_down)(lambda: start(2, 1, other, down))
+    start(3, 1, other, sibling)
+
+    def line_step(k, order, side):
+        def from_below():
+            index = index_of(z - k, side)
+            arrive(1, order, index, down)
+            pl.when(has_up)(lambda: start(1, order, index, up))
+            start(3, order, index, sibling)
+            if order == 0:
+                start(0, 0, index, partner)
+
+        def from_above():
+            index = index_of(z + k, side)
+            arrive(2, order, index, up)
+            pl.when(has_down)(lambda: start(2, order, index, down))
+            start(3, order, index, sibling)
+            if order == 0:
+                start(0, 0, index, partner)
+
+        pl.when(z - k >= 0)(from_below)
+        pl.when(z + k < lines)(from_above)
+
+    for k in range(1, lines):
+        line_step(k, 0, y)
+        line_step(k, 1, y)
+        line_step(k, 1, 1 - y)
+    for k in range(lines):
+        def below(k=k):
+            index = index_of(z - k, 1 - y)
+            arrive(0, 0, index, partner)
+            start(3, 0, index, sibling)
+
+        def above(k=k):
+            index = index_of(z + k, 1 - y)
+            arrive(0, 0, index, partner)
+            start(3, 0, index, sibling)
+
+        pl.when(z - k >= 0)(below)
+        if k:
+            pl.when(z + k < lines)(above)
+    for line in range(lines):
+        for side in range(2):
+            index = line * 2 + side
+
+            @pl.when(index != shard)
+            def _(index=index):
+                for order in range(2):
+                    arrive(3, order, index, sibling, side=1 - core)
+                    sent(3, order, index, sibling)
+
+    for line in range(lines):
+        index = index_of(line, y)
+        sent(0, 0, index, partner)
+    sent(0, 1, shard, partner)
+    for line in range(lines):
+        for order, side in ((0, y), (1, y), (1, 1 - y)):
+            index = index_of(line, side)
+
+            @pl.when((line <= z) & has_up)
+            def _(order=order, index=index):
+                sent(1, order, index, up)
+
+            @pl.when((line >= z) & has_down)
+            def _(order=order, index=index):
+                sent(2, order, index, down)
+
+    for copy in own:
+        copy.wait()
+
+
+def gather_weights(wide, small, lines, cuts):
+    shards = 2 * lines
+    hbm = pl.BlockSpec(memory_space=pl.ANY)
+    return pl.pallas_call(
+        partial(gather_kernel, lines, cuts),
+        in_specs=[hbm, hbm],
+        out_specs=[hbm, hbm],
+        out_shape=[
+            jax.ShapeDtypeStruct((shards, *wide.shape), wide.dtype),
+            jax.ShapeDtypeStruct((shards, *small.shape), small.dtype),
+        ],
+        scratch_shapes=[
+            pltpu.SemaphoreType.DMA((4, 2, 2, shards)),
+            pltpu.SemaphoreType.DMA((4, 2, 2, shards)),
+            pltpu.SemaphoreType.DMA((2,)),
+        ],
+        compiler_params=pltpu.CompilerParams(collective_id=0, has_side_effects=True),
+        name="gather",
+    )(wide, small)
+
+
+def pack_rows(pieces, width):
+    joined = jnp.concatenate(pieces, axis=1)
+    return jnp.pad(joined, ((0, 0), (0, width - joined.shape[1])))
+
+
+def split_rows(rows, sizes):
     starts = [0]
     for amount in sizes:
         starts.append(starts[-1] + amount)
-    timestep = rows[:, starts[0] : starts[1]].reshape(-1, 2 * HEADS)
-    filter_piece = rows[:, starts[1] : starts[2]].reshape(count, conv_taps, -1)
-    smoother = jnp.transpose(filter_piece, (1, 0, 2)).reshape(conv_taps, -1)
-    shifter = rows[:, starts[2] : starts[3]].reshape(-1)
-    prenorm = rows[:, starts[3] : starts[4]].reshape(-1)
-    postnorm = rows[:, starts[4] : starts[5]].reshape(-1)
-    return (timestep, smoother, shifter, prenorm, postnorm)
-
-
-def pack_grads(
-    timestep_grad, smoother_grad, shifter_grad, prenorm_grad, postnorm_grad, count, width
-):
-    conv_taps = smoother_grad.shape[0]
-    filter_rows = jnp.transpose(smoother_grad.reshape(conv_taps, count, -1), (1, 0, 2)).reshape(
-        count, -1
-    )
-    joined = jnp.concatenate(
-        [
-            timestep_grad.reshape(count, -1),
-            filter_rows,
-            shifter_grad.reshape(count, -1),
-            prenorm_grad.reshape(count, -1),
-            postnorm_grad.reshape(count, -1),
-        ],
-        axis=1,
-    )
-    return jnp.pad(joined, ((0, 0), (0, width - joined.shape[1])))
+    return [rows[:, starts[i] : starts[i + 1]] for i in range(len(sizes))]
 
 
 def local(
@@ -868,41 +1234,67 @@
     skip_gain,
 ):
     count = lax.axis_size("shard")
-    sizes, used, width = small_sizes(
-        timestep_weight, filter_weight, filter_offset, prenorm_gain, postnorm_gain
+    lines = count // 2
+    wide = lax.axis_size("rep") // 2
+    rows = widen_weight.shape[0]
+    own = [timestep_weight, filter_weight, filter_offset, prenorm_gain, postnorm_gain]
+    sizes = [piece.size for piece in own]
+    width = -(-sum(sizes) // 4096) * 4096
+    own_small = pack_rows([piece.reshape(1, -1) for piece in own], width)
+    half = WIDE // 2
+    first = half * 5 // 8 // 128 * 128
+    widen, small = gather_weights(
+        widen_weight, own_small.reshape(2, -1, 128), lines, (first, half - first)
     )
-    own_small = pack_own(
-        timestep_weight, filter_weight, filter_offset, prenorm_gain, postnorm_gain, width
-    )
-    widen = lax.all_gather(widen_weight, "shard", axis=0, tiled=True)
+    widen = widen.reshape(D, WIDE)
+    narrow_weight, small = lax.optimization_barrier((narrow_weight, small))
     narrow = lax.all_gather(narrow_weight, "shard", axis=0, tiled=True)
-    small = lax.all_gather(own_small, "shard", axis=0, tiled=True)
-    timestep, smoother, shifter, prenorm, postnorm = unpack_rows(
-        small.reshape(count, width), sizes, CONV
-    )
+    timestep, smoother, shifter, prenorm, postnorm = split_rows(small.reshape(count, width), sizes)
     (
         result, slope, widen_grad, timestep_grad, narrow_grad, smoother_grad, shifter_grad,
         prenorm_grad, postnorm_grad, bias_grad, decay_grad, skip_grad,
     ) = layer(
-        tokens, cotangent, lengths, widen, timestep, narrow, smoother, shifter, prenorm, postnorm,
+        tokens, cotangent, lengths, widen, timestep.reshape(D, 2 * HEADS), narrow,
+        jnp.transpose(smoother.reshape(count, CONV, -1), (1, 0, 2)).reshape(CONV, CHANNELS),
+        shifter.reshape(-1), prenorm.reshape(-1), postnorm.reshape(-1),
         timestep_bias, decay_log, skip_gain,
     )
-    small_grad = pack_grads(
-        timestep_grad, smoother_grad, shifter_grad, prenorm_grad, postnorm_grad, count, width
+    small_grad = pack_rows(
+        [
+            timestep_grad.reshape(count, -1),
+            jnp.transpose(smoother_grad.reshape(CONV, count, -1), (1, 0, 2)).reshape(count, -1),
+            shifter_grad.reshape(count, -1),
+            prenorm_grad.reshape(count, -1),
+            postnorm_grad.reshape(count, -1),
+        ],
+        rows * 128,
+    ).reshape(count, rows, 128)
+    heads = pack_rows([bias_grad[None], decay_grad[None], skip_grad[None]], 1024).reshape(8, 128)
+    summed, heads_summed = reduce_units(widen_grad, narrow_grad, small_grad, heads, wide, lines)
+    summed = summed.reshape(-1, rows, 128)
+    tiles = WIDE // 128
+    across = D // 128
+    widen_out = jnp.transpose(summed[:tiles], (1, 0, 2)).reshape(rows, WIDE)
+    narrow_out = jnp.transpose(
+        summed[tiles : tiles + 2 * across].reshape(2, across, rows, 128), (0, 2, 1, 3)
+    ).reshape(2 * rows, D)
+    timestep_out, filter_out, offset_out, prenorm_out, postnorm_out = split_rows(
+        summed[tiles + 2 * across].reshape(1, -1).astype(f32), sizes
     )
-    shares = (
-        lax.psum_scatter(widen_grad, "shard", scatter_dimension=0, tiled=True),
-        lax.psum_scatter(narrow_grad, "shard", scatter_dimension=0, tiled=True),
-        lax.psum_scatter(small_grad, "shard", scatter_dimension=0, tiled=True),
-    )
-    summed = lax.psum(shares, "rep")
-    heads_summed = lax.psum((bias_grad, decay_grad, skip_grad), ("rep", "shard"))
-    timestep_out, filter_out, offset_out, prenorm_out, postnorm_out = unpack_rows(
-        summed[2], sizes, CONV
-    )
+    heads_row = heads_summed.reshape(-1)
     return (
-        result, slope, summed[0], timestep_out, summed[1], filter_out, offset_out, prenorm_out,
-        postnorm_out, *heads_summed,
+        result,
+        slope,
+        widen_out.astype(f32),
+        timestep_out.reshape(rows, -1),
+        narrow_out.astype(f32),
+        filter_out.reshape(CONV, -1),
+        offset_out.reshape(-1),
+        prenorm_out.reshape(-1),
+        postnorm_out.reshape(-1),
+        heads_row[: 2 * HEADS],
+        heads_row[2 * HEADS : 3 * HEADS],
+        heads_row[3 * HEADS : 4 * HEADS],
     )
 
 

time: 956 us -> 415 us (0.43)
  waiting for transfers between devices: 327 us -> 3.71 us
  blocking collectives: 180 us -> 0 us
  Pallas kernels: 393 us -> 345 us
    pallas_call x0 -> x2, Pallas kernels: none -> 171 us  [the longest x1 132 us: reduce_units(): pl.pallas_call(partial(reduce_kernel, lines, wide), in_specs=[vmem] * 4,...]
    psum x2 -> x0, blocking collectives: 147 us -> none  [the longest x1 136 us: local(): lax.psum((bias_grad, decay_grad, skip_grad), ('rep', 'shard'))]
    reduce_scatter x2 -> x0, waiting for transfers between devices: 126 us -> none  [the longest x1 126 us: local(): lax.psum_scatter(widen_grad, 'shard', scatter_dimension=0, tiled=True)]
    pallas_call x1, Pallas kernels: 176 us -> 69.2 us  [layer(): pl.pallas_call(middle_kernel, grid_spec=pltpu.PrefetchScalarGridSpec(num_...]
    all_gather x1 -> x0, waiting for transfers between devices: 81.5 us -> none  [local(): widen = lax.all_gather(widen_weight, 'shard', axis=0, tiled=True)]
    unnamed x7 -> x1, waiting for transfers between devices: 74.6 us -> 0.02 us
    pallas_call x1, Pallas kernels: 82.7 us -> 31.8 us  [layer(): pl.pallas_call(enter_kernel, grid_spec=pltpu.PrefetchScalarGridSpec(num_s...]
    pallas_call x1, Pallas kernels: 72.1 us -> 36.7 us  [layer(): pl.pallas_call(widen_kernel, grid_spec=pltpu.PrefetchScalarGridSpec(num_s...]
  transfers between devices with their start and end apart: 6 -> 1, of which waited for: 5 -> 1; matrix products, arithmetic and copies ran while one was open for 3% -> 4% of each run, Pallas kernels for 14% -> 8%
where the time goes in v2:
time: 415 us; the launch traced here: 411 us
  Pallas kernels  345 us (83%)
  local copies, waits for them, and re-layouts  34.3 us (8%)
  between operations  14.2 us (3%)
  other arithmetic  13.1 us (3%)
    pallas_call x1, Pallas kernels, reduce_units(): pl.pallas_call(partial(reduce_kernel, lines, wide), in_specs=[vmem] * 4,...  132 us
    pallas_call x1, Pallas kernels, layer(): pl.pallas_call(middle_kernel, grid_spec=pltpu.PrefetchScalarGridSpec(num_...  69.2 us
    pallas_call x1, Pallas kernels, gather_weights(): pl.pallas_call(partial(gather_kernel, lines, cuts), in_specs=[hbm, hbm],...  39.6 us
    pallas_call x1, Pallas kernels, layer(): pl.pallas_call(widen_kernel, grid_spec=pltpu.PrefetchScalarGridSpec(num_s...  36.7 us
    pallas_call x1, Pallas kernels, layer(): pl.pallas_call(leave_kernel, grid_spec=pltpu.PrefetchScalarGridSpec(num_s...  36.2 us
    pallas_call x1, Pallas kernels, layer(): pl.pallas_call(enter_kernel, grid_spec=pltpu.PrefetchScalarGridSpec(num_s...  31.8 us
  transfers between devices with their start and end apart: 1, of which 1 were waited for; matrix products, arithmetic and copies ran while one was open for 4% of the time, Pallas kernels for 8%

profile of v2, /device:TPU:0, one launch (start us, length us, event | category | flops | bytes accessed | tf_op | source)
XLA Modules:
  0.0 410.6 jit_solution(18114668176994219704)
XLA Ops:
  7.2 0.7 reshape.155
  7.9 0.7 reshape.157
  8.5 0.8 reshape.154
  9.3 0.8 copy.67
  10.2 0.8 concatenate.15
  11.0 0.7 pad_reduce_fusion
  11.7 39.6 %gather.1 = (bf16[8,96,3328]{2,1,0:T(8,128)(2,1)}, bf16[8,2,32,128]{3,2,1,0:T(8,128)(2,1)}) custom-call(bf16[96,3328]{1,0:T(8,128)(2,1)} %wide_ref.1, bf16[2,32,128]{2,1,0:T(8,128)(2,1)} %bitcast.77), custom_call_target="tpu_custom_call" | custom-call | tf_op jit(solution)/shard_map/gather/pallas_call | solution.py:1191
  51.3 1.0 copy.93
  52.4 0.7 negate_multiply_fusion
  53.1 0.7 copy.73.rate_ref
  53.8 1.3 copy.72.bias_ref
  55.3 0.7 reshape.179.pre_ref
  56.2 0.2 reshape.161.time_ref
  56.4 0.8 copy.68
  57.2 0.7 convert_element_type.87
  58.0 1.2 copy.70
  59.3 7.8 %copy.71.wide_ref = bf16[3328,768]{1,0:T(8,128)(2,1)} copy(bf16[3328,768]{0,1:T(8,128)(2,1)} %bitcast.52) | data formatting | bytes 10223616 | tf_op jit(solution)/shard_map/transpose | solution.py:627
  67.1 31.8 %enter.1 = (bf16[2,1536,1024]{2,1,0:T(8,128)(2,1)}, bf16[2,1792,1024]{2,1,0:T(8,128)(2,1)}, bf16[2,1792,1024]{2,1,0:T(8,128)(2,1)}, bf16[2,1792,1024]{2,1,0:T(8,...) custom-call(s32[2]{0:T(128)} %len_ref.7, bf16[2,1024,768]{2,1,0:T(8,128)(2,1)} %tok_ref.5, ...), custom_call_target="tpu_custom_call" | custom-call | tf_op jit(solution)/shard_map/enter/pallas_call | solution.py:659
  98.9 0.9 pad_convert_fusion.post_ref
  99.8 3.7 all-gather.2.cloned.1.call-done.narrow_ref
  103.5 4.3 %copy.74 = bf16[1536,768]{0,1:T(8,128)(2,1)} copy(bf16[1536,768]{1,0:T(8,128)(2,1)} %all-gather.2.cloned.1.call-done.narrow_ref) | data formatting | bytes 4718592 | tf_op jit(solution)/shard_map/all_gather | solution.py:1251
  107.8 69.2 %middle.1 = (bf16[2,1024,768]{2,1,0:T(8,128)(2,1)}, bf16[2,1536,1024]{2,1,0:T(8,128)(2,1)}, bf16[2,1536,1024]{2,1,0:T(8,128)(2,1)}, f32[2,256,1024]{2,1,0:T(8,12...) custom-call(s32[2]{0:T(128)} %len_ref.7, ...), custom_call_target="tpu_custom_call" | custom-call | tf_op jit(solution)/shard_map/middle/pallas_call | solution.py:689
  177.0 36.2 %leave.1 = (bf16[2,1792,1024]{2,1,0:T(8,128)(2,1)}, bf16[2,48,1024]{2,1,0:T(8,128)(2,1)}, f32[1792,128]{1,0:T(8,128)}, f32[4,1792,128]{2,1,0:T(8,128)}, f32[48,128]{1,0:T(8,128)}, /*index=5*/f32[48,128]{1,0:T(8,128)}) custom-call(s32[2]{0:T(128)} %len_ref.7, bf16[2,1792,1024]{2,1,0:T(8,128)(2,1)} %get-tuple-element.54.filt_ref, ...), custom_call_target="tpu_custom_call" | custom-call | tf_op jit(solution)/shard_map/leave/pallas_call | solution.py:734
  213.2 0.8 reduce_sum.74
  214.1 0.9 reduce_sum.75
  215.0 0.1 reduce_sum.76
  215.1 1.5 reduce_sum.71
  216.7 0.3 reduce_sum.73
  217.1 0.1 reduce_sum.78
  217.3 36.7 %widen.1 = (bf16[2,1024,768]{2,1,0:T(8,128)(2,1)}, f32[768,3328]{1,0:T(8,128)}, f32[768,48]{1,0:T(8,128)}, f32[8,768]{1,0:T(8,128)}) custom-call(s32[2]{0:T(128)} %len_ref.7, bf16[2,1024,768]{2,1,0:T(8,128)(2,1)} %tok_ref.5, bf16[2,1024,768]{2,1,0:T(8,128)(2,1)} %cot_ref.3, bf16[2,1536,1024]{2,1,0:T(8,128)(2,1)} %get-tuple-element.53.dgate_ref, ...), custom_call_target="tpu_custom_call" | custom-call | tf_op jit(solution)/shard_map/widen/pallas_call | solution.py:767
  254.0 0.8 reduce_sum.72
  254.7 3.1 reduce_sum.70
  258.1 1.2 reshape.164
  259.4 0.8 copy.92
  260.2 0.7 select_maximum_fusion
  260.9 131.7 %reduce.9 = (bf16[2,2,2,5,96,128]{5,4,3,2,1,0:T(8,128)(2,1)}, f32[8,128]{1,0:T(8,128)}) custom-call(f32[768,3328]{1,0:T(8,128)} %get-tuple-element.64.wide_ref, f32[1536,768]{1,0:T(8,128)} %get-tuple-element.65.narrow_ref, f32[8,96,128]{2,1,0:T(8,128)} %bitcast.58, f32[8,128]{1,0:T(8,128)} %bitcast.79), custom_call_target="tpu_custom_call" | custom-call | tf_op jit(solution)/shard_map/reduce/pallas_call | solution.py:1000
  392.6 1.2 slice.69
  393.8 1.3 fusion
  395.2 0.7 slice_convert_fusion
  395.9 0.6 slice_bitcast_fusion
  396.5 0.6 slice.84
  397.1 0.6 slice.82
  397.8 1.0 slice.80
  398.8 2.2 copy_bitcast_fusion
  401.0 0.7 reshape.174
  401.7 0.7 copy.81
  402.5 0.4 copy.80
  402.8 0.9 copy.91
  (36 shorter events, 1.7 us)
Async XLA Ops:
  7.2 96.3 %all-gather.2.cloned.1.call-start = ((), (), s32[]{:S(2)}) async-start(), calls=%async_computation | async-start | bytes 2654208 | tf_op jit(solution)/shard_map/all_gather | solution.py:1251
  56.4 10.7 %copy-start = (bf16[768,48]{1,0:T(8,128)(2,1)}, bf16[768,48]{1,0:T(8,128)(2,1)S(1)}, u32[]{:S(2)}) copy-start(bf16[768,48]{1,0:T(8,128)(2,1)S(1)} %reshape.161.time_ref) | copy-start | bytes 221188
  177.0 38.0 %copy-start.2 = (f32[192,128]{1,0:T(8,128)S(1)}, f32[192,128]{1,0:T(8,128)}, u32[]{:S(2)}) copy-start(f32[192,128]{1,0:T(8,128)} %get-tuple-element.73) | copy-start | bytes 294916
  177.0 39.7 %copy-start.1 = (f32[1536,128]{1,0:T(8,128)S(1)}, f32[1536,128]{1,0:T(8,128)}, u32[]{:S(2)}) copy-start(f32[1536,128]{1,0:T(8,128)} %get-tuple-element.70) | copy-start | bytes 2359300
Sparse Core Ops, SparseCore 0:
  51.4 52.0 all-gather.1

commit v3 on v2

--- a/solution.py
+++ b/solution.py
@@ -41,6 +41,12 @@
     return lax.dot_general(a, b, (((0,), (0,)), ((), ())), preferred_element_type=f32)
 
 
+def mm_tn_precise(a, b):
+    return lax.dot_general(
+        a, b, (((0,), (0,)), ((), ())), precision=precise, preferred_element_type=f32
+    )
+
+
 def sigmoid(v):
     return 0.5 * jnp.tanh(0.5 * v) + 0.5
 
@@ -50,6 +56,39 @@
         lax.broadcasted_iota(jnp.int32, shape, 0),
         lax.broadcasted_iota(jnp.int32, shape, 1),
     )
+
+
+def column(row, lanes=SPAN):
+    return mm_tn_precise(row, jnp.ones((1, lanes), f32))
+
+
+def rate_columns(decay_ref):
+    half = column(-jnp.exp(decay_ref[...]) * LOG2E)
+    return jnp.concatenate([half, half], axis=0)
+
+
+def spread_taps(taps_s, taps_ref, offset_ref):
+    shards, taps, width = taps_ref.shape
+    ones = jnp.ones((1, SPAN), bf16)
+    for s in range(shards):
+        rows = slice(s * width, (s + 1) * width)
+        for k in range(taps):
+            taps_s[k, rows, :] = mm_tn(taps_ref[s, k : k + 1, :], ones)
+        if offset_ref is not None:
+            taps_s[taps, rows, :] = mm_tn(offset_ref[s], ones)
+
+
+def join_row(row_s, ref):
+    shards, _, width = ref.shape
+    for s in range(shards):
+        row_s[:, s * width : (s + 1) * width] = ref[s].astype(f32)
+
+
+def lane_sums(value):
+    return lax.dot_general(
+        jnp.ones((8, value.shape[1]), f32), value, (((1,), (1,)), ((), ())),
+        precision=precise, preferred_element_type=f32,
+    )[:1]
 
 
 def step_sums(x, rate):
@@ -74,8 +113,9 @@
     time_ref,
     pre_ref,
     taps_ref,
+    offset_ref,
     bias_ref,
-    rate_ref,
+    decay_ref,
     gate_o,
     fin_o,
     filt_o,
@@ -85,6 +125,11 @@
     last_s,
     run_s,
     taps_s,
+    wide_s,
+    time_s,
+    pre_s,
+    rate_s,
+    bias_s,
 ):
     seq = pl.program_id(0)
     block = pl.program_id(1)
@@ -92,8 +137,14 @@
 
     @pl.when((seq == 0) & (block == 0))
     def _():
-        for k in range(CONV + 1):
-            taps_s[k] = jnp.broadcast_to(taps_ref[:, k : k + 1], (CHANNELS, SPAN))
+        spread_taps(taps_s, taps_ref, offset_ref)
+        join_row(pre_s, pre_ref)
+        rate_s[...] = rate_columns(decay_ref)
+        bias_s[...] = column(bias_ref[...], BLOCK)
+        rows_d, cols_d = iotas((D, D))
+        time_s[...] = mm_tn(time_ref[...], (rows_d == cols_d).astype(bf16)).astype(bf16)
+        for i in range(WIDE // 256):
+            wide_s[i * 256 : (i + 1) * 256, :] = wide_ref[:, i * 256 : (i + 1) * 256].T
 
     @pl.when(block == 0)
     def _():
@@ -104,14 +155,14 @@
     def _():
         tok = tok_ref[0].astype(f32)
         scale = lax.rsqrt(jnp.mean(tok * tok, axis=-1, keepdims=True) + EPS)
-        normed = (tok * scale * pre_ref[...]).astype(bf16)
-        x_o[0] = mm_nt(time_ref[...], normed) + bias_ref[...]
+        normed = (tok * scale * pre_s[...]).astype(bf16)
+        x_o[0] = mm_nt(time_s[...], normed) + bias_s[...]
         place = block * BLOCK + lax.broadcasted_iota(jnp.int32, (1, BLOCK), 1)
         mask = (place < length).astype(f32)
 
         def project(i):
             fin_o[0, i * 256 : (i + 1) * 256, :] = mm_nt(
-                wide_ref[INNER + i * 256 : INNER + (i + 1) * 256, :], normed
+                wide_s[INNER + i * 256 : INNER + (i + 1) * 256, :], normed
             ).astype(bf16)
 
         def filter_rows(i):
@@ -137,7 +188,7 @@
                     filter_rows((i - 1) * 8 + j)
         for i in range(INNER // 256):
             gate_o[0, i * 256 : (i + 1) * 256, :] = mm_nt(
-                wide_ref[i * 256 : (i + 1) * 256, :], normed
+                wide_s[i * 256 : (i + 1) * 256, :], normed
             ).astype(bf16)
             if i == 0:
                 for j in range(8):
@@ -147,7 +198,7 @@
 
         def span(sub, _):
             cols = pl.ds(pl.multiple_of(sub * SPAN, SPAN), SPAN)
-            steps, fcum, rcum = step_sums(x_o[0, :, cols], rate_ref[...])
+            steps, fcum, rcum = step_sums(x_o[0, :, cols], rate_s[:, :1])
             tail_f, tail_r = span_tails(steps, fcum, rcum)
             decay = jnp.exp2(fcum[:, SPAN - 1 :])
             ins_f = act_o[0, INNER : INNER + 64, cols].astype(f32)
@@ -163,7 +214,7 @@
                 )
                 fresh = mm_nt(act_o[0, rows, cols], weighted)
                 run = run_s[rows, :]
-                state_o[0, sub, rows, :] = jnp.where(lane < 64, run, fresh)
+                state_o[0, sub, rows, :] = jnp.where(lane < 64, run, fresh).astype(bf16)
                 run_s[rows, :] = run * decay[h : h + 1] + fresh
             return None
 
@@ -180,9 +231,8 @@
     x_ref,
     state_ref,
     narrow_ref,
-    turned_ref,
     post_ref,
-    rate_ref,
+    decay_ref,
     result_o,
     dgate_o,
     dval_o,
@@ -205,6 +255,9 @@
     slope_s,
     norm_s,
     gain_s,
+    rate_s,
+    narrow_s,
+    post_s,
 ):
     seq = pl.program_id(0)
     step = pl.program_id(1)
@@ -213,10 +266,13 @@
 
     @pl.when((seq == 0) & (step == 0))
     def _():
-        narrow_o[...] = jnp.zeros_like(narrow_o)
-        post_o[...] = jnp.zeros_like(post_o)
+        narrow_s[...] = jnp.zeros_like(narrow_s)
+        post_s[...] = jnp.zeros_like(post_s)
         skip_o[...] = jnp.zeros_like(skip_o)
-        gain_s[...] = jnp.broadcast_to(post_ref[:, :1], (INNER, SPAN))
+        shards, _, width = post_ref.shape
+        for s in range(shards):
+            gain_s[s * width : (s + 1) * width, :] = mm_tn(post_ref[s], jnp.ones((1, SPAN), bf16))
+        rate_s[...] = rate_columns(decay_ref)
 
     @pl.when(step == 0)
     def _():
@@ -254,7 +310,7 @@
         def forward_span(back, _):
             sub = SUBS - 1 - back
             cols = pl.ds(pl.multiple_of(sub * SPAN, SPAN), SPAN)
-            steps, fcum, rcum = step_sums(x_ref[0, :, cols], rate_ref[...])
+            steps, fcum, rcum = step_sums(x_ref[0, :, cols], rate_s[:, :1])
             least = jnp.log2(jnp.maximum(steps, TINY))
             columns = jnp.concatenate(
                 [fcum - least[:HEADS], rcum - least[HEADS:], jnp.zeros((SPAN - 48, SPAN), f32)],
@@ -294,9 +350,9 @@
                     ],
                     axis=1,
                 )
-                state = state_ref[0, sub, rows, :]
+                state = state_ref[0, sub, rows, :].astype(f32)
                 run = run_s[rows, :]
-                rstate_o[0, sub, rows, :] = run
+                rstate_o[0, sub, rows, :] = run.astype(bf16)
                 held = jnp.where(lane < 64, state, run).astype(bf16)
                 held_s[sub, rows, :] = held
                 run_s[rows, :] = run * decay[h : h + 1] + state
@@ -327,21 +383,21 @@
             gain = gain_s[r, :]
             dgate_o[0, r, :] = (kept * jnp.concatenate([gain, gain], axis=1)).astype(bf16)
             product = kept * dgn_s[r, :]
-            post_o[r, :] += product[:, :SPAN] + product[:, SPAN:]
+            post_s[r, :] += product[:, :SPAN] + product[:, SPAN:]
             return None
 
         lax.fori_loop(0, INNER // 32, norm_rows, None, unroll=8)
         gnormed = dgate_o[0]
-        branch = mm(turned_ref[...], gnormed)
-        result_o[0] = (tok_ref[0].astype(f32) + jnp.where(inside, branch.T, 0.0)).astype(bf16)
+        branch = mm_tn(gnormed, narrow_ref[...])
+        result_o[0] = (tok_ref[0].astype(f32) + jnp.where(inside, branch, 0.0)).astype(bf16)
         for i in range(3):
             rows = slice(i * 512, (i + 1) * 512)
-            narrow_o[rows, :] += mm(gnormed[rows], slope_s[...])
+            narrow_s[rows, :] += mm(gnormed[rows], slope_s[...])
 
         def backward_span(back, _):
             sub = SUBS - 1 - back
             cols = pl.ds(pl.multiple_of(sub * SPAN, SPAN), SPAN)
-            steps, fcum, rcum = step_sums(x_ref[0, :, cols], rate_ref[...])
+            steps, fcum, rcum = step_sums(x_ref[0, :, cols], rate_s[:, :1])
             out_f = jnp.exp2(fcum)
             out_r = jnp.exp2(rcum)
             decay = jnp.exp2(fcum[:, SPAN - 1 :])
@@ -368,7 +424,7 @@
                 dmixed = dgated * (gate * sig)
                 dgate = dgated * mixed * (sig * (1.0 + gate * (1.0 - sig)))
                 dgate_o[0, rows, cols] = dgate.astype(bf16)
-                skip_o[h * 8 : h * 8 + 8, :] += fold(dmixed * values32)
+                skip_o[h : h + 1, :] += down(dmixed * values32)
                 dm = dmixed.astype(bf16)
                 dm32 = dm.astype(f32)
                 held = held_s[sub, rows, :]
@@ -382,7 +438,7 @@
                 dheld = dall[:, 2 * SPAN :]
                 dval_o[0, rows, cols] = (dlow + dhigh + skip_ref[h] * dmixed).astype(bf16)
                 run = grun_s[rows, :]
-                dstate_o[0, sub, rows, :] = jnp.where(lane < 64, run, dheld)
+                dstate_o[0, sub, rows, :] = jnp.where(lane < 64, run, dheld).astype(bf16)
                 grun_s[rows, :] = run * decay[h : h + 1] + dheld
                 sums_o[0, h : h + 1, cols] = down(dm32 * ahead)
                 sums_o[0, HEADS + h : HEADS + h + 1, cols] = down(dm32 * behind)
@@ -401,6 +457,18 @@
 
         lax.fori_loop(0, SUBS, backward_span, None)
 
+    @pl.when((seq == pl.num_programs(0) - 1) & (step == pl.num_programs(1) - 1))
+    def _():
+        post_o[...] = lane_sums(post_s[...])
+        halves, shards, rows = narrow_o.shape[0] * SPAN // D, *narrow_o.shape[1:3]
+        for unit in range(narrow_o.shape[0]):
+            half, tile = divmod(unit, D // SPAN)
+            for s in range(shards):
+                start = (s * halves + half) * rows
+                narrow_o[unit, s] = narrow_s[
+                    start : start + rows, tile * SPAN : (tile + 1) * SPAN
+                ].astype(bf16)
+
 
 def leave_kernel(
     len_ref,
@@ -413,17 +481,21 @@
     sums_ref,
     dstate_ref,
     rstate_ref,
-    rate_ref,
+    decay_ref,
+    skip_ref,
     dfilt_o,
     draw_o,
-    offset_o,
-    taps_o,
-    bias_o,
-    decay_o,
+    lines_o,
+    heads_o,
     grun_s,
     near_s,
     dact_s,
     last_s,
+    offset_s,
+    taps_s,
+    bias_s,
+    decay_s,
+    rate_s,
 ):
     seq = pl.program_id(0)
     block = pl.program_id(1)
@@ -431,10 +503,11 @@
 
     @pl.when((seq == 0) & (block == 0))
     def _():
-        offset_o[...] = jnp.zeros_like(offset_o)
-        taps_o[...] = jnp.zeros_like(taps_o)
-        bias_o[...] = jnp.zeros_like(bias_o)
-        decay_o[...] = jnp.zeros_like(decay_o)
+        offset_s[...] = jnp.zeros_like(offset_s)
+        taps_s[...] = jnp.zeros_like(taps_s)
+        bias_s[...] = jnp.zeros_like(bias_s)
+        decay_s[...] = jnp.zeros_like(decay_s)
+        rate_s[...] = rate_columns(decay_ref)
 
     @pl.when(block == 0)
     def _():
@@ -449,7 +522,7 @@
         def span(sub, _):
             cols = pl.ds(pl.multiple_of(sub * SPAN, SPAN), SPAN)
             x = x_ref[0, :, cols]
-            steps, fcum, rcum = step_sums(x, rate_ref[...])
+            steps, fcum, rcum = step_sums(x, rate_s[:, :1])
             tail_f, tail_r = span_tails(steps, fcum, rcum)
             decay = jnp.exp2(rcum[:, :1])
             fi = act_ref[0, INNER : INNER + 64, cols].astype(f32)
@@ -467,11 +540,11 @@
                     ],
                     axis=0,
                 )
-                dstate = dstate_ref[0, sub, rows, :]
+                dstate = dstate_ref[0, sub, rows, :].astype(f32)
                 run = grun_s[rows, :]
                 dfresh = jnp.where(lane < 64, dstate, run).astype(bf16)
                 near_s[h : h + 1, :] = decay[h : h + 1] * jnp.sum(
-                    jnp.where(lane < 64, 0.0, run * rstate_ref[0, sub, rows, :]),
+                    jnp.where(lane < 64, 0.0, run * rstate_ref[0, sub, rows, :].astype(f32)),
                     axis=0,
                     keepdims=True,
                 )
@@ -504,13 +577,13 @@
             dfa = dfa + far_f + mm(ends_f, (rows_i < cols_i).astype(f32), precise)
             dra = dra + far_r + mm(ends_r, (rows_i > cols_i).astype(f32), precise)
             sig = jax.nn.sigmoid(x)
-            rate = rate_ref[...] * (1.0 / LOG2E)
+            rate = rate_s[:, :1] * (1.0 / LOG2E)
             share = sig / jnp.maximum(steps, TINY)
             span_d = jnp.concatenate([dfa, dra], axis=0)
             draw = jnp.concatenate([col_f + ends_f, col_r + ends_r], axis=0) * share + span_d * (rate * sig)
             draw_o[0, :, cols] = draw.astype(bf16)
-            bias_o[...] += draw
-            decay_o[...] += span_d * steps * rate
+            bias_s[...] += draw
+            decay_s[...] += span_d * steps * rate
             return None
 
         lax.fori_loop(0, SUBS, span, None)
@@ -526,19 +599,30 @@
                 dact = dact * mask
             dfilt = dact * (sig * (1.0 + filt * (1.0 - sig)))
             dfilt_o[0, r, :] = dfilt.astype(bf16)
-            offset_o[r, :] += dfilt[:, :SPAN] + dfilt[:, SPAN:]
+            offset_s[r, :] += dfilt[:, :SPAN] + dfilt[:, SPAN:]
             fin = fin_ref[0, r, :]
             w = jnp.concatenate([last_s[r, :], fin], axis=1)
             last_s[r, :] = fin[:, SPAN:]
             product = dfilt * fin.astype(f32)
-            taps_o[3, r, :] += product[:, :SPAN] + product[:, SPAN:]
+            taps_s[3, r, :] += product[:, :SPAN] + product[:, SPAN:]
             for lag in range(1, CONV):
                 product = dfilt * pltpu.roll(w, lag, 1)[:, SPAN:].astype(f32)
-                taps_o[3 - lag, r, :] += product[:, :SPAN] + product[:, SPAN:]
+                taps_s[3 - lag, r, :] += product[:, :SPAN] + product[:, SPAN:]
             return None
 
         lax.fori_loop(0, INNER // 32, lambda i, _: filter_rows(i, True), None, unroll=8)
         lax.fori_loop(INNER // 32, CHANNELS // 32, lambda i, _: filter_rows(i, False), None, unroll=8)
+
+    @pl.when((seq == pl.num_programs(0) - 1) & (block == pl.num_programs(1) - 1))
+    def _():
+        lines_o[...] = jnp.zeros_like(lines_o)
+        heads_o[...] = jnp.zeros_like(heads_o)
+        for k in range(CONV):
+            lines_o[k : k + 1, :] = lane_sums(taps_s[k])
+        lines_o[CONV : CONV + 1, :] = lane_sums(offset_s[...])
+        heads_o[:1, : 2 * HEADS] = lane_sums(bias_s[...])
+        heads_o[1:2, :HEADS] = lane_sums(decay_s[:HEADS] + decay_s[HEADS:])
+        heads_o[2:3, :HEADS] = lane_sums(skip_ref[...])
 
 
 def widen_kernel(
@@ -553,12 +637,18 @@
     time_ref,
     pre_ref,
     taps_ref,
+    lines_ref,
+    post_ref,
     slope_o,
     wide_o,
-    time_o,
-    pre_o,
+    small_o,
     dproj_s,
     taps_s,
+    wide_s,
+    time_s,
+    total_s,
+    pre_s,
+    lines_s,
 ):
     seq = pl.program_id(0)
     block = pl.program_id(1)
@@ -566,11 +656,11 @@
 
     @pl.when((seq == 0) & (block == 0))
     def _():
-        wide_o[...] = jnp.zeros_like(wide_o)
-        time_o[...] = jnp.zeros_like(time_o)
-        pre_o[...] = jnp.zeros_like(pre_o)
-        for k in range(CONV):
-            taps_s[k] = jnp.broadcast_to(taps_ref[:, k : k + 1], (CHANNELS, SPAN))
+        wide_s[...] = jnp.zeros_like(wide_s)
+        time_s[...] = jnp.zeros_like(time_s)
+        total_s[...] = jnp.zeros_like(total_s)
+        spread_taps(taps_s, taps_ref, None)
+        join_row(pre_s, pre_ref)
 
     @pl.when(block * BLOCK >= length)
     def _():
@@ -580,7 +670,7 @@
     def _():
         tok = tok_ref[0].astype(f32)
         scale = lax.rsqrt(jnp.mean(tok * tok, axis=-1, keepdims=True) + EPS)
-        normed = (tok * scale * pre_ref[...]).astype(bf16)
+        normed = (tok * scale * pre_s[...]).astype(bf16)
         normed_t = normed.T
         dproj_s[:INNER, :] = dgate_ref[0]
         beyond = (block + 1) * BLOCK < length
@@ -601,20 +691,44 @@
         lax.fori_loop(0, CHANNELS // 32, filter_rows, None, unroll=8)
         for i in range(WIDE // 256):
             rows = slice(i * 256, (i + 1) * 256)
-            wide_o[:, rows] += mm_nt(normed_t, dproj_s[rows, :])
+            wide_s[:, rows] += mm_nt(normed_t, dproj_s[rows, :])
         draw = draw_ref[0]
-        time_o[...] += mm_nt(normed_t, draw)
+        time_s[:, : 2 * HEADS] += mm_nt(normed_t, draw)
         dnormed = (mm(wide_ref[...], dproj_s[...]) + mm(time_ref[...], draw)).T
         product = dnormed * tok
-        pre_o[...] += jnp.sum((product * scale).reshape(BLOCK // 8, 8, D), axis=0)
-        gain = pre_ref[...]
+        total_s[...] += jnp.sum((product * scale).reshape(BLOCK // 8, 8, D), axis=0)
+        gain = pre_s[...]
         mean = jnp.mean(product * gain, axis=-1, keepdims=True)
         grad = scale * (gain * dnormed) - tok * (scale * scale * scale * mean)
         slope_o[0] = (cot_ref[0].astype(f32) + grad).astype(bf16)
 
+    @pl.when((seq == pl.num_programs(0) - 1) & (block == pl.num_programs(1) - 1))
+    def _():
+        tiles, shards, rows = wide_o.shape[:3]
+        for s in range(shards):
+            own = slice(s * rows, (s + 1) * rows)
+            for unit in range(tiles):
+                wide_o[unit, s] = wide_s[own, unit * SPAN : (unit + 1) * SPAN].astype(bf16)
+            small_o[0, s] = time_s[own, :].astype(bf16)
+        pre_sum = jnp.sum(total_s[...], axis=0, keepdims=True)
+        vectors = [(lines_ref[k : k + 1, :], CHANNELS // shards) for k in range(CONV + 1)]
+        vectors += [(pre_sum, rows), (post_ref[...], INNER // shards)]
+        lines_s[...] = jnp.zeros_like(lines_s)
+        for s in range(shards):
+            line = 0
+            for vector, width in vectors:
+                for start in range(0, width, SPAN):
+                    size = min(SPAN, width - start)
+                    begin = s * width + start
+                    lines_s[line : line + 1, :size] = vector[:, begin : begin + size]
+                    line += 1
+            small_o[1, s] = lines_s[...].astype(bf16)
+
 
 def whole(shape):
-    return pl.BlockSpec(shape, lambda s, c, *_: (0,) * len(shape))
+    return pl.BlockSpec(
+        shape, lambda s, c, *_: (0,) * len(shape), pipeline_mode=pl.Buffered(1)
+    )
 
 
 def layer(
@@ -622,17 +736,12 @@
     timestep_bias, decay_log, skip_gain,
 ):
     count, length = tokens.shape[:2]
+    shards = taps.shape[0]
+    rows = D // shards
     blocks = length // BLOCK
     spans = length // SPAN
-    wide_t = wide.T
-    time_t = time.T
-    narrow_t = narrow.T
-    pre = prenorm.astype(f32)[None]
-    post = jnp.pad(postnorm.astype(f32)[:, None], ((0, 0), (0, 7)))
-    cols = jnp.concatenate([taps, offset[None], jnp.zeros((3, CHANNELS), bf16)], axis=0).astype(f32).T
-    bias = timestep_bias[:, None]
-    rate = -jnp.exp(decay_log) * LOG2E
-    rate = jnp.concatenate([rate, rate])[:, None]
+    bias = timestep_bias[None]
+    decay = decay_log[None]
     grid = (count, blocks)
     sds = jax.ShapeDtypeStruct
 
@@ -655,15 +764,15 @@
     params = pltpu.CompilerParams(
         dimension_semantics=("arbitrary", "arbitrary"), vmem_limit_bytes=VMEM_LIMIT
     )
-    state_shape = sds((count, spans, INNER, SPAN), f32)
+    state_shape = sds((count, spans, INNER, SPAN), bf16)
     gate, fin, filt, act, x, state = pl.pallas_call(
         enter_kernel,
         grid_spec=pltpu.PrefetchScalarGridSpec(
             num_scalar_prefetch=1,
             grid=grid,
             in_specs=[
-                tall(False), whole((WIDE, D)), whole((48, D)), whole((1, D)),
-                whole((CHANNELS, 8)), whole((48, 1)), whole((48, 1)),
+                tall(False), whole((D, WIDE)), whole((D, 48)), whole(prenorm.shape),
+                whole(taps.shape), whole(offset.shape), whole((1, 48)), whole((1, HEADS)),
             ],
             out_specs=[
                 ahead(INNER), ahead(CHANNELS), ahead(CHANNELS), ahead(CHANNELS), ahead(48), states(False),
@@ -672,6 +781,11 @@
                 pltpu.VMEM((CHANNELS, SPAN), bf16),
                 pltpu.VMEM((INNER, SPAN), f32),
                 pltpu.VMEM((CONV + 1, CHANNELS, SPAN), f32),
+                pltpu.VMEM((WIDE, D), bf16),
+                pltpu.VMEM((48, D), bf16),
+                pltpu.VMEM((1, D), f32),
+                pltpu.VMEM((48, SPAN), f32),
+                pltpu.VMEM((48, BLOCK), f32),
             ],
         ),
         out_shape=[
@@ -684,8 +798,9 @@
         ],
         compiler_params=params,
         name="enter",
-    )(lengths, tokens, wide_t, time_t, pre, cols, bias, rate)
-
+    )(lengths, tokens, wide, time, prenorm, taps, offset, bias, decay)
+
+    across = 2 * D // SPAN
     result, dgate, dval, dio, sums, dstate, rstate, narrow_grad, post_grad, skip_grad = pl.pallas_call(
         middle_kernel,
         grid_spec=pltpu.PrefetchScalarGridSpec(
@@ -694,11 +809,11 @@
             in_specs=[
                 pl.BlockSpec(memory_space=pltpu.SMEM),
                 tall(True), tall(True), back(INNER), back(CHANNELS), back(48), states(True),
-                whole((INNER, D)), whole((D, INNER)), whole((INNER, 8)), whole((48, 1)),
+                whole((INNER, D)), whole(postnorm.shape), whole((1, HEADS)),
             ],
             out_specs=[
                 tall(True), back(INNER), back(INNER), back(256), back(120), states(True), states(True),
-                whole((INNER, D)), whole((INNER, SPAN)), whole((8 * HEADS, SPAN)),
+                whole((across, shards, rows, SPAN)), whole((1, INNER)), whole((HEADS, SPAN)),
             ],
             scratch_shapes=[
                 pltpu.VMEM((INNER, SPAN), f32),
@@ -713,6 +828,9 @@
                 pltpu.VMEM((BLOCK, D), bf16),
                 pltpu.VMEM((8, BLOCK), f32),
                 pltpu.VMEM((INNER, SPAN), f32),
+                pltpu.VMEM((48, SPAN), f32),
+                pltpu.VMEM((INNER, D), f32),
+                pltpu.VMEM((INNER, SPAN), f32),
             ],
         ),
         out_shape=[
@@ -723,48 +841,49 @@
             sds((count, 120, length), f32),
             state_shape,
             state_shape,
-            sds((INNER, D), f32),
-            sds((INNER, SPAN), f32),
-            sds((8 * HEADS, SPAN), f32),
+            sds((across, shards, rows, SPAN), bf16),
+            sds((1, INNER), f32),
+            sds((HEADS, SPAN), f32),
         ],
         compiler_params=params,
         name="middle",
-    )(lengths, skip_gain, tokens, cotangent, gate, act, x, state, narrow, narrow_t, post, rate)
-
-    dfilt, draw, offset_grad, taps_grad, bias_grad, decay_grad = pl.pallas_call(
+    )(lengths, skip_gain, tokens, cotangent, gate, act, x, state, narrow, postnorm, decay)
+
+    dfilt, draw, lines, heads = pl.pallas_call(
         leave_kernel,
         grid_spec=pltpu.PrefetchScalarGridSpec(
             num_scalar_prefetch=1,
             grid=grid,
             in_specs=[
                 ahead(CHANNELS), ahead(CHANNELS), ahead(CHANNELS), ahead(48), ahead(INNER), ahead(256), ahead(120),
-                states(False), states(False), whole((48, 1)),
+                states(False), states(False), whole((1, HEADS)), whole((HEADS, SPAN)),
             ],
             out_specs=[
-                ahead(CHANNELS), ahead(48),
-                whole((CHANNELS, SPAN)), whole((CONV, CHANNELS, SPAN)),
-                whole((48, SPAN)), whole((48, SPAN)),
+                ahead(CHANNELS), ahead(48), whole((8, CHANNELS)), whole((8, SPAN)),
             ],
             scratch_shapes=[
                 pltpu.VMEM((INNER, SPAN), f32),
                 pltpu.VMEM((HEADS, SPAN), f32),
                 pltpu.VMEM((CHANNELS, BLOCK), f32),
                 pltpu.VMEM((CHANNELS, SPAN), bf16),
+                pltpu.VMEM((CHANNELS, SPAN), f32),
+                pltpu.VMEM((CONV, CHANNELS, SPAN), f32),
+                pltpu.VMEM((48, SPAN), f32),
+                pltpu.VMEM((48, SPAN), f32),
+                pltpu.VMEM((48, SPAN), f32),
             ],
         ),
         out_shape=[
             sds((count, CHANNELS, length), bf16),
             sds((count, 48, length), bf16),
-            sds((CHANNELS, SPAN), f32),
-            sds((CONV, CHANNELS, SPAN), f32),
-            sds((48, SPAN), f32),
-            sds((48, SPAN), f32),
+            sds((8, CHANNELS), f32),
+            sds((8, SPAN), f32),
         ],
         compiler_params=params,
         name="leave",
-    )(lengths, filt, act, fin, x, dval, dio, sums, dstate, rstate, rate)
-
-    slope, wide_grad, time_grad, pre_grad = pl.pallas_call(
+    )(lengths, filt, act, fin, x, dval, dio, sums, dstate, rstate, decay, skip_grad)
+
+    slope, wide_grad, small_grad = pl.pallas_call(
         widen_kernel,
         grid_spec=pltpu.PrefetchScalarGridSpec(
             num_scalar_prefetch=1,
@@ -776,39 +895,31 @@
                     lambda s, c, *_: (s, 0, jnp.minimum(SUBS * (c + 1), spans - 1)),
                 ),
                 ahead(48),
-                whole((D, WIDE)), whole((D, 48)), whole((1, D)), whole((CHANNELS, 8)),
+                whole((D, WIDE)), whole((D, 48)), whole(prenorm.shape), whole(taps.shape),
+                whole((8, CHANNELS)), whole((1, INNER)),
             ],
-            out_specs=[tall(False), whole((D, WIDE)), whole((D, 48)), whole((8, D))],
+            out_specs=[
+                tall(False), whole((WIDE // SPAN, shards, rows, SPAN)), whole((2, shards, rows, SPAN)),
+            ],
             scratch_shapes=[
                 pltpu.VMEM((WIDE, BLOCK), bf16),
                 pltpu.VMEM((CONV, CHANNELS, SPAN), f32),
+                pltpu.VMEM((D, WIDE), f32),
+                pltpu.VMEM((D, SPAN), f32),
+                pltpu.VMEM((8, D), f32),
+                pltpu.VMEM((1, D), f32),
+                pltpu.VMEM((rows, SPAN), f32),
             ],
         ),
         out_shape=[
             sds((count, length, D), bf16),
-            sds((D, WIDE), f32),
-            sds((D, 48), f32),
-            sds((8, D), f32),
+            sds((WIDE // SPAN, shards, rows, SPAN), bf16),
+            sds((2, shards, rows, SPAN), bf16),
         ],
         compiler_params=params,
         name="widen",
-    )(lengths, tokens, cotangent, dgate, dfilt, dfilt, draw, wide, time, pre, cols)
-
-    decay_rows = jnp.sum(decay_grad, axis=1)
-    return (
-        result,
-        slope,
-        wide_grad,
-        time_grad,
-        narrow_grad,
-        jnp.sum(taps_grad, axis=2),
-        jnp.sum(offset_grad, axis=1),
-        jnp.sum(pre_grad, axis=0),
-        jnp.sum(post_grad, axis=1),
-        jnp.sum(bias_grad, axis=1),
-        decay_rows[:HEADS] + decay_rows[HEADS:],
-        jnp.sum(skip_grad.reshape(HEADS, 8 * SPAN), axis=1),
-    )
+    )(lengths, tokens, cotangent, dgate, dfilt, dfilt, draw, wide, time, prenorm, taps, lines, post_grad)
+    return result, slope, wide_grad, narrow_grad, small_grad, heads
 
 
 def peer(rep, shard):
@@ -829,17 +940,18 @@
     pl.semaphore_wait(barrier, len(devices))
 
 
+STRIDE = 2
+
+
 def reduce_kernel(
     lines, wide,
     wide_ref, narrow_ref, small_ref, heads_ref, out_ref, heads_out_ref,
-    grads_s, near_s, sum_s, p1_s, q1_s, t0_s, t1_s, p2_s, q2_s, r_s, z_s,
+    own_s, near_s, sum_s, p1_s, q1_s, t0_s, t1_s, p2_s, q2_s, r_s, z_s,
     hc_s, hx_s, hy_s, hz_s,
-    send_sem, recv_sem, hsend_sem, hrecv_sem,
+    send_sem, recv_sem, hsend_sem, hrecv_sem, near_sem, arrive_sem, own_sem,
 ):
-    piece, rows = grads_s.shape[-3:-1]
-    shards = 2 * lines
-    tiles_wide = wide_ref.shape[1] // 128
-    tiles_narrow = narrow_ref.shape[1] // 128
+    piece, rows = out_ref.shape[3:5]
+    sources = (wide_ref, narrow_ref, small_ref)
     rep = lax.axis_index("rep")
     shard = lax.axis_index("shard")
     core, x = lax.rem(rep, 2), lax.div(rep, 2)
@@ -850,190 +962,294 @@
     along = [peer(rep, lax.rem(z + k, lines) * 2 + y) for k in range(1, lines)]
     greet([sibling, partner, *across, *along])
     started = []
-    used = [0]
-
-    def launch(src, dst, device):
-        i = used[0]
-        used[0] += 1
-        copy = remote(src, dst, send_sem.at[i], recv_sem.at[i], device)
+    used = [0, 0]
+
+    def launch(src, dst, device, small=False):
+        i = used[small]
+        used[small] += 1
+        pair = (hsend_sem, hrecv_sem) if small else (send_sem, recv_sem)
+        copy = remote(src, dst, pair[0].at[i], pair[1].at[i], device)
         copy.start()
         started.append(copy)
         return copy
 
-    hused = [0]
-
-    def launch_small(src, dst, device):
-        i = hused[0]
-        hused[0] += 1
-        copy = remote(src, dst, hsend_sem.at[i], hrecv_sem.at[i], device)
-        copy.start()
-        started.append(copy)
-        return copy
-
-    def add(dst, *srcs):
+    def add(where, extents, dst, *srcs):
         flat = 1
-        for extent in dst.shape[:-3]:
+        for extent in extents:
             flat *= extent
-        shape = dst.shape[:-3]
-
-        def body(i, _):
-            where = []
-            rest = i
-            for extent in reversed(shape):
-                where.append(lax.rem(rest, extent))
-                rest = lax.div(rest, extent)
-            where = tuple(reversed(where))
-            for unit in range(dst.shape[-3]):
-                place = (*where, unit)
-                total = srcs[0][place].astype(f32)
-                for src in srcs[1:]:
-                    total = total + src[place].astype(f32)
-                dst[place] = total.astype(dst.dtype)
-            return None
-
-        lax.fori_loop(0, flat, body, None)
-
-    def pack(half, order):
-        def body(index, _):
-            start = pl.multiple_of(index * rows, 8)
+        for unit in range(*where):
+
+            def body(i, _, unit=unit):
+                place = []
+                rest = i
+                for extent in reversed(extents):
+                    place.append(lax.rem(rest, extent))
+                    rest = lax.div(rest, extent)
+                place = tuple(reversed(place))
+                total = None
+                for ref, index in srcs:
+                    term = ref[index(unit, *place)].astype(f32)
+                    total = term if total is None else total + term
+                ref, index = dst
+                ref[index(unit, *place)] = total.astype(ref.dtype)
+                return None
+
+            lax.fori_loop(0, flat, body, None)
+
+    def source(position, order, unit):
+        j = (position * 2 + order) * piece + unit
+        for ref in sources:
+            if j < ref.shape[1]:
+                return ref, j
+            j -= ref.shape[1]
+        return None, None
+
+    def chunk(*where):
+        units = pl.ds(where[0], where[1] - where[0])
+        near = []
+        own = []
+        for position in range(wide):
+            for order in range(2):
+                for unit in range(*where):
+                    ref, j = source(position, order, unit)
+                    if ref is None:
+                        continue
+                    place = (position, order, unit)
+                    i = (position * 2 + order) * piece + unit
+                    copy = remote(
+                        ref.at[1 - core, j], near_s.at[place], near_sem.at[i], arrive_sem.at[i], sibling
+                    )
+                    copy.start()
+                    started.append(copy)
+                    near.append((order, place, copy))
+                    copy = pltpu.make_async_copy(ref.at[core, j], own_s.at[place], own_sem.at[i])
+                    copy.start()
+                    own.append((order, place, copy))
+        yield
+        for order in range(2):
             for position in range(wide):
-                for i in range(piece):
-                    unit = ((half * wide + position) * 2 + order) * piece + i
-                    if unit < tiles_wide:
-                        value = wide_ref[pl.ds(start, rows), unit * 128 : unit * 128 + 128]
-                    elif unit < tiles_wide + 2 * tiles_narrow:
-                        lower, tile = divmod(unit - tiles_wide, tiles_narrow)
-                        begin = pl.multiple_of(2 * start + lower * rows, 8)
-                        value = narrow_ref[pl.ds(begin, rows), tile * 128 : tile * 128 + 128]
-                    elif unit == tiles_wide + 2 * tiles_narrow:
-                        value = small_ref[index]
-                    else:
-                        value = jnp.zeros((rows, 128), f32)
-                    where = (half, order, position, lax.rem(index, 2), lax.div(index, 2), i)
-                    grads_s[where] = value.astype(bf16)
-            return None
-
-        lax.fori_loop(0, shards, body, None)
-
-    def pack_half(mine, order):
-        pl.when(core == (0 if mine else 1))(lambda: pack(0, order))
-        pl.when(core == (1 if mine else 0))(lambda: pack(1, order))
-
-    hc_s[core] = heads_ref[...]
-    head = launch_small(hc_s.at[core], hc_s.at[core], sibling)
-    near = []
-    for order in range(2):
-        pack_half(False, order)
-        near.append(launch(grads_s.at[1 - core, order], near_s.at[order], sibling))
-    for order in range(2):
-        pack_half(True, order)
-    near[0].wait_recv()
-    add(sum_s.at[0], grads_s.at[core, 0], near_s.at[0])
-    p1 = [
-        launch(sum_s.at[0, lax.rem(x + k, wide)], p1_s.at[k - 1], across[k - 1])
-        for k in range(1, wide)
-    ]
-    near[1].wait_recv()
-    add(sum_s.at[1], grads_s.at[core, 1], near_s.at[1])
-    q1 = launch(sum_s.at[1, :, 1 - y], q1_s, partner)
-    head.wait_recv()
-    hx_s[x] = hc_s[0] + hc_s[1]
-    heads = [launch_small(hx_s.at[x], hx_s.at[x], device) for device in across]
-    for copy in p1:
-        copy.wait_recv()
-    add(t0_s, sum_s.at[0, x], *[p1_s.at[k] for k in range(wide - 1)])
-    p2 = launch(t0_s.at[1 - y], p2_s, partner)
-    q1.wait_recv()
-    add(t1_s, sum_s.at[1, :, y], q1_s)
-    q2 = [
-        launch(t1_s.at[lax.rem(x + k, wide)], q2_s.at[k - 1], across[k - 1])
-        for k in range(1, wide)
-    ]
-    for copy in heads:
-        copy.wait_recv()
-    total = hx_s[0]
-    for k in range(1, wide):
-        total = total + hx_s[k]
-    hy_s[y] = total
-    head = launch_small(hy_s.at[y], hy_s.at[y], partner)
-    p2.wait_recv()
-    add(r_s.at[0], t0_s.at[y], p2_s)
-    z0 = [launch(r_s.at[0, lax.rem(z + k, lines)], z_s.at[0, k - 1], along[k - 1]) for k in range(1, lines)]
-    for copy in q2:
-        copy.wait_recv()
-    add(r_s.at[1], t1_s.at[x], *[q2_s.at[k] for k in range(wide - 1)])
-    z1 = [launch(r_s.at[1, lax.rem(z + k, lines)], z_s.at[1, k - 1], along[k - 1]) for k in range(1, lines)]
-    head.wait_recv()
-    hz_s[z] = hy_s[0] + hy_s[1]
-    heads = [launch_small(hz_s.at[z], hz_s.at[z], device) for device in along]
-    for order, copies in ((0, z0), (1, z1)):
-        for copy in copies:
+                for unit in range(*where):
+                    if source(position, order, unit)[0] is None:
+                        sum_s[position, order, unit] = jnp.zeros(sum_s.shape[3:], bf16)
+            for mine, theirs in zip(own, near):
+                if mine[0] != order:
+                    continue
+                place = mine[1]
+                mine[2].wait()
+                theirs[2].wait_recv()
+                add(
+                    (place[2], place[2] + 1), (lines, 2),
+                    (sum_s, lambda u, a, b, p=place: (*p, a, b)),
+                    (own_s, lambda u, a, b, p=place: (*p, a, b)),
+                    (near_s, lambda u, a, b, p=place: (*p, a, b)),
+                )
+            if order == 0:
+                p1 = [
+                    launch(sum_s.at[lax.rem(x + k, wide), 0, units], p1_s.at[k - 1, units], across[k - 1])
+                    for k in range(1, wide)
+                ]
+            else:
+                q1 = launch(sum_s.at[:, 1, units, :, 1 - y], q1_s.at[:, units], partner)
+        yield
+        for copy in p1:
             copy.wait_recv()
-        add(out_ref.at[core, x, order], r_s.at[order, z], *[z_s.at[order, k] for k in range(lines - 1)])
-    shares = [launch(out_ref.at[core, x], out_ref.at[core, x], device) for device in across]
-    for copy in heads:
-        copy.wait_recv()
-    total = hz_s[0]
-    for k in range(1, lines):
-        total = total + hz_s[k]
-    heads_out_ref[...] = total
-    for copy in shares:
-        copy.wait_recv()
-    last = launch(out_ref.at[core], out_ref.at[core], sibling)
-    last.wait_recv()
+        add(
+            where, (lines, 2),
+            (t0_s, lambda u, a, b: (u, a, b)),
+            (sum_s, lambda u, a, b: (x, 0, u, a, b)),
+            *[(p1_s, lambda u, a, b, k=k: (k, u, a, b)) for k in range(wide - 1)],
+        )
+        p2 = launch(t0_s.at[units, :, 1 - y], p2_s.at[units], partner)
+        q1.wait_recv()
+        add(
+            where, (wide, lines),
+            (t1_s, lambda u, p, a: (p, u, a)),
+            (sum_s, lambda u, p, a: (p, 1, u, a, y)),
+            (q1_s, lambda u, p, a: (p, u, a)),
+        )
+        q2 = [
+            launch(t1_s.at[lax.rem(x + k, wide), units], q2_s.at[k - 1, units], across[k - 1])
+            for k in range(1, wide)
+        ]
+        yield
+        p2.wait_recv()
+        add(
+            where, (lines,),
+            (r_s, lambda u, a: (0, u, a)), (t0_s, lambda u, a: (u, a, y)), (p2_s, lambda u, a: (u, a)),
+        )
+        for copy in q2:
+            copy.wait_recv()
+        add(
+            where, (lines,),
+            (r_s, lambda u, a: (1, u, a)), (t1_s, lambda u, a: (x, u, a)),
+            *[(q2_s, lambda u, a, k=k: (k, u, a)) for k in range(wide - 1)],
+        )
+        last = [
+            launch(r_s.at[:, units, lax.rem(z + k, lines)], z_s.at[k - 1, :, units], along[k - 1])
+            for k in range(1, lines)
+        ]
+        yield
+        for copy in last:
+            copy.wait_recv()
+        add(
+            where, (2,),
+            (out_ref, lambda u, o: (core, x, o, u)), (r_s, lambda u, o: (o, u, z)),
+            *[(z_s, lambda u, o, k=k: (k, o, u)) for k in range(lines - 1)],
+        )
+        mine = out_ref.at[core, x, :, units]
+        shares = [launch(mine, mine, device) for device in across]
+        yield
+        for copy in shares:
+            copy.wait_recv()
+        half = out_ref.at[core, :, :, units]
+        swap = launch(half, half, sibling)
+        yield
+        swap.wait_recv()
+        yield
+
+    def sum_heads():
+        hc_s[core] = heads_ref[...]
+        head = launch(hc_s.at[core], hc_s.at[core], sibling, True)
+        yield
+        head.wait_recv()
+        hx_s[x] = hc_s[0] + hc_s[1]
+        heads = [launch(hx_s.at[x], hx_s.at[x], device, True) for device in across]
+        yield
+        for copy in heads:
+            copy.wait_recv()
+        total = hx_s[0]
+        for k in range(1, wide):
+            total = total + hx_s[k]
+        hy_s[y] = total
+        head = launch(hy_s.at[y], hy_s.at[y], partner, True)
+        yield
+        head.wait_recv()
+        hz_s[z] = hy_s[0] + hy_s[1]
+        heads = [launch(hz_s.at[z], hz_s.at[z], device, True) for device in along]
+        yield
+        for copy in heads:
+            copy.wait_recv()
+        total = hz_s[0]
+        for k in range(1, lines):
+            total = total + hz_s[k]
+        heads_out_ref[...] = total
+        yield
+
+    works = [chunk(i, min(i + STRIDE, piece)) for i in range(0, piece, STRIDE)]
+    stages = 7
+    small_work = sum_heads()
+    for slot in range(len(works) + stages - 1):
+        for g in range(len(works)):
+            if 0 <= slot - g < stages:
+                next(works[g])
+        if slot < 5:
+            next(small_work)
     for copy in started:
         copy.wait_send()
 
 
-def unit_count(wide_columns, narrow_columns, wide):
-    used = wide_columns // 128 + 2 * (narrow_columns // 128) + 1
-    return -(-used // (4 * wide)) * 4 * wide
-
-
-def reduce_units(wide_grad, narrow_grad, small_grad, heads, wide, lines):
-    rows = small_grad.shape[1]
-    unit = unit_count(wide_grad.shape[1], narrow_grad.shape[1], wide) // (4 * wide)
-    piece = (unit, rows, 128)
-    copies = 2 + (wide - 1) * 3 + 2 + 2 * (lines - 1) + 1
+def reduce_units(wide_units, narrow_units, small_units, heads, wide, lines):
+    rows = wide_units.shape[2]
+    halves = [a.reshape(2, -1, lines, 2, rows, SPAN) for a in (wide_units, narrow_units, small_units)]
+    used = sum(a.shape[1] for a in halves)
+    unit = -(-used // (2 * wide))
+    piece = (rows, SPAN)
+    chunks = -(-unit // STRIDE)
+    copies = (3 * (wide - 1) + 3 + lines - 1) * chunks
     small = 1 + (wide - 1) + 1 + (lines - 1)
+    others = max(wide - 1, 1)
     vmem = pl.BlockSpec(memory_space=pltpu.VMEM)
+    hbm = pl.BlockSpec(memory_space=pl.ANY)
     return pl.pallas_call(
         partial(reduce_kernel, lines, wide),
-        in_specs=[vmem] * 4,
+        in_specs=[hbm, hbm, hbm, vmem],
         out_specs=[vmem, vmem],
         out_shape=[
-            jax.ShapeDtypeStruct((2, wide, 2, *piece), bf16),
-            jax.ShapeDtypeStruct((8, 128), f32),
+            jax.ShapeDtypeStruct((2, wide, 2, unit, *piece), bf16),
+            jax.ShapeDtypeStruct((8, SPAN), f32),
         ],
         scratch_shapes=[
-            pltpu.VMEM((2, 2, wide, 2, lines, *piece), bf16),
-            pltpu.VMEM((2, wide, 2, lines, *piece), bf16),
-            pltpu.VMEM((2, wide, 2, lines, *piece), bf16),
-            pltpu.VMEM((max(wide - 1, 1), 2, lines, *piece), bf16),
-            pltpu.VMEM((wide, lines, *piece), bf16),
-            pltpu.VMEM((2, lines, *piece), bf16),
-            pltpu.VMEM((wide, lines, *piece), bf16),
-            pltpu.VMEM((lines, *piece), bf16),
-            pltpu.VMEM((max(wide - 1, 1), lines, *piece), bf16),
-            pltpu.VMEM((2, lines, *piece), bf16),
-            pltpu.VMEM((2, lines - 1, *piece), bf16),
-            pltpu.VMEM((2, 8, 128), f32),
-            pltpu.VMEM((wide, 8, 128), f32),
-            pltpu.VMEM((2, 8, 128), f32),
-            pltpu.VMEM((lines, 8, 128), f32),
+            pltpu.VMEM((wide, 2, unit, lines, 2, *piece), bf16),
+            pltpu.VMEM((wide, 2, unit, lines, 2, *piece), bf16),
+            pltpu.VMEM((wide, 2, unit, lines, 2, *piece), bf16),
+            pltpu.VMEM((others, unit, lines, 2, *piece), bf16),
+            pltpu.VMEM((wide, unit, lines, *piece), bf16),
+            pltpu.VMEM((unit, lines, 2, *piece), bf16),
+            pltpu.VMEM((wide, unit, lines, *piece), bf16),
+            pltpu.VMEM((unit, lines, *piece), bf16),
+            pltpu.VMEM((others, unit, lines, *piece), bf16),
+            pltpu.VMEM((2, unit, lines, *piece), bf16),
+            pltpu.VMEM((lines - 1, 2, unit, *piece), bf16),
+            pltpu.VMEM((2, 8, SPAN), f32),
+            pltpu.VMEM((wide, 8, SPAN), f32),
+            pltpu.VMEM((2, 8, SPAN), f32),
+            pltpu.VMEM((lines, 8, SPAN), f32),
             pltpu.SemaphoreType.DMA((copies,)),
             pltpu.SemaphoreType.DMA((copies,)),
             pltpu.SemaphoreType.DMA((small,)),
             pltpu.SemaphoreType.DMA((small,)),
+            pltpu.SemaphoreType.DMA((2 * wide * unit,)),
+            pltpu.SemaphoreType.DMA((2 * wide * unit,)),
+            pltpu.SemaphoreType.DMA((2 * wide * unit,)),
         ],
         compiler_params=pltpu.CompilerParams(
             collective_id=1, has_side_effects=True, vmem_limit_bytes=VMEM_LIMIT
         ),
         name="reduce",
-    )(wide_grad, narrow_grad, small_grad, heads)
-
-
-def gather_kernel(lines, cuts, wide_ref, small_ref, wide_o, small_o, send_sem, recv_sem, own_sem):
+    )(*halves, heads)
+
+
+def finish_kernel(
+    wide, summed_ref, heads_ref,
+    wide_o, time_o, narrow_o, taps_o, offset_o, pre_o, post_o, bias_o, decay_o, skip_o,
+):
+    unit, rows = summed_ref.shape[3:5]
+    tiles_wide = wide_o.shape[1] // SPAN // 2
+    tiles_narrow = narrow_o.shape[1] // SPAN
+
+    def read(core, j):
+        block, i = divmod(j, unit)
+        return summed_ref[core, block // 2, block % 2, i].astype(f32)
+
+    for core in range(2):
+        for j in range(tiles_wide):
+            column = (core * tiles_wide + j) * SPAN
+            wide_o[:, column : column + SPAN] = read(core, j)
+        for j in range(tiles_narrow):
+            narrow_o[core * rows : (core + 1) * rows, j * SPAN : (j + 1) * SPAN] = read(
+                core, tiles_wide + j
+            )
+    time_o[...] = read(0, tiles_wide + tiles_narrow)[:, : 2 * HEADS]
+    vectors = read(1, tiles_wide + tiles_narrow)
+    line = 0
+    outs = [(taps_o, k) for k in range(CONV)] + [(offset_o, 0), (pre_o, 0), (post_o, 0)]
+    for out, k in outs:
+        width = out.shape[1]
+        for start in range(0, width, SPAN):
+            size = min(SPAN, width - start)
+            out[k : k + 1, start : start + size] = vectors[line : line + 1, :size]
+            line += 1
+    bias_o[...] = heads_ref[:1, : 2 * HEADS]
+    decay_o[...] = heads_ref[1:2, :HEADS]
+    skip_o[...] = heads_ref[2:3, :HEADS]
+
+
+def finish(summed, heads, wide, rows, width):
+    shapes = [
+        (rows, WIDE), (rows, 2 * HEADS), (2 * rows, D), (CONV, width), (1, width), (1, rows), (1, 2 * rows),
+        (1, 2 * HEADS), (1, HEADS), (1, HEADS),
+    ]
+    return pl.pallas_call(
+        partial(finish_kernel, wide),
+        out_shape=[jax.ShapeDtypeStruct(shape, f32) for shape in shapes],
+        compiler_params=pltpu.CompilerParams(vmem_limit_bytes=VMEM_LIMIT),
+        name="finish",
+    )(summed, heads)
+
+
+def gather_kernel(lines, cuts, kinds, *refs):
+    ins, outs = refs[:kinds], refs[kinds : 2 * kinds]
+    send_sem, recv_sem, own_sem = refs[2 * kinds :]
     rep = lax.axis_index("rep")
     shard = lax.axis_index("shard")
     core = lax.rem(rep, 2)
@@ -1056,32 +1272,28 @@
     pl.semaphore_wait(barrier, 2 + has_up.astype(jnp.int32) + has_down.astype(jnp.int32))
 
     own = [
-        pltpu.make_async_copy(wide_ref, wide_o.at[shard], own_sem.at[0]),
-        pltpu.make_async_copy(small_ref, small_o.at[shard], own_sem.at[1]),
+        pltpu.make_async_copy(src, dst.at[shard], own_sem.at[i])
+        for i, (src, dst) in enumerate(zip(ins, outs))
     ]
     for copy in own:
         copy.start()
 
     def place(order, part, ref, index, side):
         if part:
-            return ref.at[side] if index is None else ref.at[index, side]
+            return ref if index is None else ref.at[index]
         start = pl.multiple_of(side * half + (cuts[0] if order else 0), 128)
         columns = pl.ds(start, cuts[order])
         return ref.at[:, columns] if index is None else ref.at[index, :, columns]
 
-    def parts(order):
-        return (0, 1) if order == 0 else (0,)
-
     def copies(way, order, index, device, mine=False, side=None):
         side = core if side is None else side
+        parts = range(kinds) if order == 0 and way != 3 else (0,)
         made = []
-        for part in parts(order):
-            out = (wide_o, small_o)[part]
-            src = (wide_ref, small_ref)[part] if mine else out
+        for part in parts:
             made.append(
                 remote(
-                    place(order, part, src, None if mine else index, side),
-                    place(order, part, out, index, side),
+                    place(order, part, ins[part] if mine else outs[part], None if mine else index, side),
+                    place(order, part, outs[part], index, side),
                     send_sem.at[way, order, part, index],
                     recv_sem.at[way, order, part, index],
                     device,
@@ -1142,32 +1354,24 @@
         line_step(k, 1, y)
         line_step(k, 1, 1 - y)
     for k in range(lines):
-        def below(k=k):
-            index = index_of(z - k, 1 - y)
+
+        def take(index):
             arrive(0, 0, index, partner)
             start(3, 0, index, sibling)
 
-        def above(k=k):
-            index = index_of(z + k, 1 - y)
-            arrive(0, 0, index, partner)
-            start(3, 0, index, sibling)
-
-        pl.when(z - k >= 0)(below)
+        pl.when(z - k >= 0)(lambda k=k: take(index_of(z - k, 1 - y)))
         if k:
-            pl.when(z + k < lines)(above)
+            pl.when(z + k < lines)(lambda k=k: take(index_of(z + k, 1 - y)))
+    for index in range(2 * lines):
+
+        @pl.when(index != shard)
+        def _(index=index):
+            for order in range(2):
+                arrive(3, order, index, sibling, side=1 - core)
+                sent(3, order, index, sibling)
+
     for line in range(lines):
-        for side in range(2):
-            index = line * 2 + side
-
-            @pl.when(index != shard)
-            def _(index=index):
-                for order in range(2):
-                    arrive(3, order, index, sibling, side=1 - core)
-                    sent(3, order, index, sibling)
-
-    for line in range(lines):
-        index = index_of(line, y)
-        sent(0, 0, index, partner)
+        sent(0, 0, index_of(line, y), partner)
     sent(0, 1, shard, partner)
     for line in range(lines):
         for order, side in ((0, y), (1, y), (1, 1 - y)):
@@ -1185,37 +1389,25 @@
         copy.wait()
 
 
-def gather_weights(wide, small, lines, cuts):
+def gather_weights(arrays, lines):
     shards = 2 * lines
+    half = arrays[0].shape[1] // 2
+    first = half * 5 // 8 // 128 * 128
     hbm = pl.BlockSpec(memory_space=pl.ANY)
+    kinds = len(arrays)
     return pl.pallas_call(
-        partial(gather_kernel, lines, cuts),
-        in_specs=[hbm, hbm],
-        out_specs=[hbm, hbm],
-        out_shape=[
-            jax.ShapeDtypeStruct((shards, *wide.shape), wide.dtype),
-            jax.ShapeDtypeStruct((shards, *small.shape), small.dtype),
-        ],
+        partial(gather_kernel, lines, (first, half - first), kinds),
+        in_specs=[hbm] * kinds,
+        out_specs=[hbm] * kinds,
+        out_shape=[jax.ShapeDtypeStruct((shards, *a.shape), a.dtype) for a in arrays],
         scratch_shapes=[
-            pltpu.SemaphoreType.DMA((4, 2, 2, shards)),
-            pltpu.SemaphoreType.DMA((4, 2, 2, shards)),
-            pltpu.SemaphoreType.DMA((2,)),
+            pltpu.SemaphoreType.DMA((4, 2, kinds, shards)),
+            pltpu.SemaphoreType.DMA((4, 2, kinds, shards)),
+            pltpu.SemaphoreType.DMA((kinds,)),
         ],
         compiler_params=pltpu.CompilerParams(collective_id=0, has_side_effects=True),
         name="gather",
-    )(wide, small)
-
-
-def pack_rows(pieces, width):
-    joined = jnp.concatenate(pieces, axis=1)
-    return jnp.pad(joined, ((0, 0), (0, width - joined.shape[1])))
-
-
-def split_rows(rows, sizes):
-    starts = [0]
-    for amount in sizes:
-        starts.append(starts[-1] + amount)
-    return [rows[:, starts[i] : starts[i + 1]] for i in range(len(sizes))]
+    )(*arrays)
 
 
 def local(
@@ -1233,68 +1425,31 @@
     decay_log,
     skip_gain,
 ):
-    count = lax.axis_size("shard")
-    lines = count // 2
+    lines = lax.axis_size("shard") // 2
     wide = lax.axis_size("rep") // 2
     rows = widen_weight.shape[0]
-    own = [timestep_weight, filter_weight, filter_offset, prenorm_gain, postnorm_gain]
-    sizes = [piece.size for piece in own]
-    width = -(-sum(sizes) // 4096) * 4096
-    own_small = pack_rows([piece.reshape(1, -1) for piece in own], width)
-    half = WIDE // 2
-    first = half * 5 // 8 // 128 * 128
-    widen, small = gather_weights(
-        widen_weight, own_small.reshape(2, -1, 128), lines, (first, half - first)
+    width = filter_weight.shape[1]
+    widen, timestep, taps, offset, prenorm, postnorm = gather_weights(
+        [
+            widen_weight, timestep_weight, filter_weight,
+            filter_offset[None], prenorm_gain[None], postnorm_gain[None],
+        ],
+        lines,
     )
-    widen = widen.reshape(D, WIDE)
-    narrow_weight, small = lax.optimization_barrier((narrow_weight, small))
+    narrow_weight, taps = lax.optimization_barrier((narrow_weight, taps))
     narrow = lax.all_gather(narrow_weight, "shard", axis=0, tiled=True)
-    timestep, smoother, shifter, prenorm, postnorm = split_rows(small.reshape(count, width), sizes)
+    result, slope, wide_grad, narrow_grad, small_grad, heads = layer(
+        tokens, cotangent, lengths, widen.reshape(D, WIDE), timestep.reshape(D, 2 * HEADS), narrow,
+        taps, offset, prenorm, postnorm, timestep_bias, decay_log, skip_gain,
+    )
+    summed, heads = reduce_units(wide_grad, narrow_grad, small_grad, heads, wide, lines)
     (
-        result, slope, widen_grad, timestep_grad, narrow_grad, smoother_grad, shifter_grad,
-        prenorm_grad, postnorm_grad, bias_grad, decay_grad, skip_grad,
-    ) = layer(
-        tokens, cotangent, lengths, widen, timestep.reshape(D, 2 * HEADS), narrow,
-        jnp.transpose(smoother.reshape(count, CONV, -1), (1, 0, 2)).reshape(CONV, CHANNELS),
-        shifter.reshape(-1), prenorm.reshape(-1), postnorm.reshape(-1),
-        timestep_bias, decay_log, skip_gain,
-    )
-    small_grad = pack_rows(
-        [
-            timestep_grad.reshape(count, -1),
-            jnp.transpose(smoother_grad.reshape(CONV, count, -1), (1, 0, 2)).reshape(count, -1),
-            shifter_grad.reshape(count, -1),
-            prenorm_grad.reshape(count, -1),
-            postnorm_grad.reshape(count, -1),
-        ],
-        rows * 128,
-    ).reshape(count, rows, 128)
-    heads = pack_rows([bias_grad[None], decay_grad[None], skip_grad[None]], 1024).reshape(8, 128)
-    summed, heads_summed = reduce_units(widen_grad, narrow_grad, small_grad, heads, wide, lines)
-    summed = summed.reshape(-1, rows, 128)
-    tiles = WIDE // 128
-    across = D // 128
-    widen_out = jnp.transpose(summed[:tiles], (1, 0, 2)).reshape(rows, WIDE)
-    narrow_out = jnp.transpose(
-        summed[tiles : tiles + 2 * across].reshape(2, across, rows, 128), (0, 2, 1, 3)
-    ).reshape(2 * rows, D)
-    timestep_out, filter_out, offset_out, prenorm_out, postnorm_out = split_rows(
-        summed[tiles + 2 * across].reshape(1, -1).astype(f32), sizes
-    )
-    heads_row = heads_summed.reshape(-1)
+        widen_out, timestep_out, narrow_out, filter_out, offset_out, prenorm_out, postnorm_out,
+        bias_out, decay_out, skip_out,
+    ) = finish(summed, heads, wide, rows, width)
     return (
-        result,
-        slope,
-        widen_out.astype(f32),
-        timestep_out.reshape(rows, -1),
-        narrow_out.astype(f32),
-        filter_out.reshape(CONV, -1),
-        offset_out.reshape(-1),
-        prenorm_out.reshape(-1),
-        postnorm_out.reshape(-1),
-        heads_row[: 2 * HEADS],
-        heads_row[2 * HEADS : 3 * HEADS],
-        heads_row[3 * HEADS : 4 * HEADS],
+        result, slope, widen_out, timestep_out, narrow_out, filter_out,
+        *[row.reshape(-1) for row in (offset_out, prenorm_out, postnorm_out, bias_out, decay_out, skip_out)],
     )
 
 

time: 415 us -> 371 us (0.89); the launches traced: 411 us -> 371 us
  local copies, waits for them, and re-layouts: 34.3 us -> 5.33 us
  waiting for transfers between devices: 3.71 us -> 17.4 us
  other arithmetic: 13.1 us -> 0 us
  Pallas kernels: 345 us -> 334 us
    pallas_call x2 -> x3, Pallas kernels: 171 us -> 151 us  [the longest x1 103 us: reduce_units(): pl.pallas_call(partial(reduce_kernel, lines, wide), in_specs=[hbm, hbm, h...]
    all_gather x1, waiting for transfers between devices: 3.69 us -> 17.4 us  [local(): narrow = lax.all_gather(narrow_weight, 'shard', axis=0, tiled=True)]
    transpose x3 -> x0, local copies, waits for them, and re-layouts: 9.07 us -> none  [the longest x1 7.82 us: layer(): wide_t = wide.T]
    reduce_sum x8 -> x0, other arithmetic: 7.51 us -> none  [the longest x1 3.06 us: layer(): jnp.sum(taps_grad, axis=2)]
    reshape x18 -> x0, local copies, waits for them, and re-layouts: 6.29 us -> none  [the longest x4 2.2 us: local(): own_small = pack_rows([piece.reshape(1, -1) for piece in own], width)]
    slice x11 -> x0, local copies, waits for them, and re-layouts: 4.87 us -> none  [the longest x8 1.35 us: split_rows(): return [rows[:, starts[i]:starts[i + 1]] for i in range(len(sizes))]]
    all_gather x1 -> x0, local copies, waits for them, and re-layouts: 4.27 us -> none  [local(): narrow = lax.all_gather(narrow_weight, 'shard', axis=0, tiled=True)]
  transfers between devices with their start and end apart: 1 -> 1, of which waited for: 1 -> 1; matrix products, arithmetic and copies ran while one was open for 4% -> 0% of each run, Pallas kernels for 8% -> 9%
where the time goes in v3:
time: 371 us
  Pallas kernels  334 us (90%)
  waiting for transfers between devices  17.4 us (5%)
  between operations  14.1 us (4%)
  local copies, waits for them, and re-layouts  5.33 us (1%)
    pallas_call x1, Pallas kernels, reduce_units(): pl.pallas_call(partial(reduce_kernel, lines, wide), in_specs=[hbm, hbm, h...  103 us
    pallas_call x1, Pallas kernels, layer(): pl.pallas_call(middle_kernel, grid_spec=pltpu.PrefetchScalarGridSpec(num_...  69.8 us
    pallas_call x1, Pallas kernels, gather_weights(): pl.pallas_call(partial(gather_kernel, lines, (first, half - first), kinds...  45.9 us
    pallas_call x1, Pallas kernels, layer(): pl.pallas_call(widen_kernel, grid_spec=pltpu.PrefetchScalarGridSpec(num_s...  39.7 us
    pallas_call x1, Pallas kernels, layer(): pl.pallas_call(leave_kernel, grid_spec=pltpu.PrefetchScalarGridSpec(num_s...  39 us
    pallas_call x1, Pallas kernels, layer(): pl.pallas_call(enter_kernel, grid_spec=pltpu.PrefetchScalarGridSpec(num_s...  34.3 us
    all_gather x1, waiting for transfers between devices, local(): narrow = lax.all_gather(narrow_weight, 'shard', axis=0, tiled=True)  17.4 us
  transfers between devices with their start and end apart: 1, of which 1 were waited for; matrix products, arithmetic and copies ran while one was open for 0% of the time, Pallas kernels for 9%

profile of v3, /device:TPU:0, one launch (start us, length us, event | category | flops | bytes accessed | tf_op | source)
XLA Modules:
  0.0 371.1 jit_solution(16751031103172908052)
XLA Ops:
  7.2 0.0 all-gather.2.cloned.1.call-start
  7.2 1.2 broadcast_in_dim.15.refs_3_
  8.4 1.2 broadcast_in_dim.17.refs_5_
  9.7 1.4 copy.25.refs_1_
  11.1 45.9 %gather.1 = (bf16[8,96,3328]{2,1,0:T(8,128)(2,1)}, bf16[8,96,48]{2,1,0:T(8,128)(2,1)}, bf16[8,4,224]{2,1,0:T(4,128)(2,1)}, bf16[8,1,224]{2,1,0:T(2,128)(2,1)}, b...) custom-call(bf16[96,3328]{1,0:T(8,128)(2,1)} %refs_0_.1, bf16[96,48]{1,0:T(8,128)(2,1)} %copy.25.refs_1_, ...), custom_call_target="tpu_custom_call" | custom-call | tf_op jit(solution)/shard_map/gather/pallas_call | solution.py:1398
  57.0 0.0 all-gather.2.cloned.1.call-update
  57.0 34.3 %enter.1 = (bf16[2,1536,1024]{2,1,0:T(8,128)(2,1)}, bf16[2,1792,1024]{2,1,0:T(8,128)(2,1)}, bf16[2,1792,1024]{2,1,0:T(8,128)(2,1)}, bf16[2,1792,1024]{2,1,0:T(8,...) custom-call(s32[2]{0:T(128)} %len_ref.7, bf16[2,1024,768]{2,1,0:T(8,128)(2,1)} %tok_ref.5, ...), custom_call_target="tpu_custom_call" | custom-call | tf_op jit(solution)/shard_map/enter/pallas_call | solution.py:768
  91.3 17.4 %all-gather.2.cloned.1.call-done.narrow_ref = bf16[1536,768]{1,0:T(8,128)(2,1)} async-done(((bf16[192,768]{1,0:T(8,128)(2,1)}), bf16[1536,768]{1,0:T(8,128)(2,1)}) %all-gather.2.cloned.1.call-update) | async-done | bytes 2359312 | tf_op jit(solution)/shard_map/all_gather | solution.py:1440
  108.6 69.8 %middle.1 = (bf16[2,1024,768]{2,1,0:T(8,128)(2,1)}, bf16[2,1536,1024]{2,1,0:T(8,128)(2,1)}, bf16[2,1536,1024]{2,1,0:T(8,128)(2,1)}, f32[2,256,1024]{2,1,0:T(8,12...) custom-call(s32[2]{0:T(128)} %len_ref.7, ...), custom_call_target="tpu_custom_call" | custom-call | tf_op jit(solution)/shard_map/middle/pallas_call | solution.py:804
  178.5 39.0 %leave.1 = (bf16[2,1792,1024]{2,1,0:T(8,128)(2,1)}, bf16[2,48,1024]{2,1,0:T(8,128)(2,1)}, f32[8,1792]{1,0:T(8,128)}, f32[8,128]{1,0:T(8,128)}) custom-call(s32[2]{0:T(128)} %len_ref.7, bf16[2,1792,1024]{2,1,0:T(8,128)(2,1)} %get-tuple-element.69.filt_ref, bf16[2,1792,1024]{2,1,0:T(8,128)(2,1)} %get-tuple-element.62.act_ref, ...), custom_call_target="tpu_custom_call" | custom-call | tf_op jit(solution)/shard_map/leave/pallas_call | solution.py:852
  217.5 39.7 %widen.1 = (bf16[2,1024,768]{2,1,0:T(8,128)(2,1)}, bf16[26,8,96,128]{3,2,1,0:T(8,128)(2,1)}, bf16[2,8,96,128]{3,2,1,0:T(8,128)(2,1)}) custom-call(s32[2]{0:T(128)} %len_ref.7, bf16[2,1024,768]{2,1,0:T(8,128)(2,1)} %tok_ref.5, bf16[2,1024,768]{2,1,0:T(8,128)(2,1)} %cot_ref.3, bf16[2,1536,1024]{2,1,0:T(8,128)(2,1)} %get-tuple-element.68.dgate_ref, ...), custom_call_target="tpu_custom_call" | custom-call | tf_op jit(solution)/shard_map/widen/pallas_call | solution.py:886
  257.2 103.0 %reduce.1 = (bf16[2,2,2,5,96,128]{5,4,3,2,1,0:T(8,128)(2,1)}, f32[8,128]{1,0:T(8,128)}) custom-call(bf16[2,13,4,2,96,128]{5,4,3,2,1,0:T(8,128)(2,1)} %bitcast.16, bf16[2,6,4,2,96,128]{5,4,3,2,1,0:T(8,128)(2,1)} %bitcast.17, bf16[2,1,4,2,96,128]{5,4,3,2,1,0:T(8,128)(2,1)} %bitcast.20, f32[8,128]{1,0:T(8,128)} %get-tuple-element.85.heads_ref), custom_call_target="tpu_custom_call" | custom-call | tf_op jit(solution)/shard_map/reduce/pallas_call | solution.py:1163
  360.2 2.6 finish.1
  362.8 1.5 copy.26
Async XLA Ops:
  7.2 101.5 %all-gather.2.cloned.1.call-start = ((), (), s32[]{:S(2)}) async-start(), calls=%async_computation | async-start | bytes 2654208 | tf_op jit(solution)/shard_map/all_gather | solution.py:1440
Sparse Core Ops, SparseCore 0:
  57.1 51.4 all-gather.1

commit v4 on v3

--- a/solution.py
+++ b/solution.py
@@ -67,21 +67,27 @@
     return jnp.concatenate([half, half], axis=0)
 
 
-def spread_taps(taps_s, taps_ref, offset_ref):
-    shards, taps, width = taps_ref.shape
-    ones = jnp.ones((1, SPAN), bf16)
-    for s in range(shards):
-        rows = slice(s * width, (s + 1) * width)
-        for k in range(taps):
-            taps_s[k, rows, :] = mm_tn(taps_ref[s, k : k + 1, :], ones)
-        if offset_ref is not None:
-            taps_s[taps, rows, :] = mm_tn(offset_ref[s], ones)
-
-
-def join_row(row_s, ref):
-    shards, _, width = ref.shape
-    for s in range(shards):
-        row_s[:, s * width : (s + 1) * width] = ref[s].astype(f32)
+def vector_parts(vectors_ref):
+    shards = vectors_ref.shape[0]
+    sizes = [CHANNELS // shards] * (CONV + 1) + [D // shards, INNER // shards]
+    starts = [sum(sizes[:i]) for i in range(len(sizes))]
+    return [slice(start, start + size) for start, size in zip(starts, sizes)]
+
+
+def spread_vectors(out_s, vectors_ref, which):
+    part = vector_parts(vectors_ref)[which]
+    width = part.stop - part.start
+    for s in range(vectors_ref.shape[0]):
+        out_s[s * width : (s + 1) * width, :] = mm_tn(
+            vectors_ref[s, :, part], jnp.ones((1, SPAN), bf16)
+        )
+
+
+def join_row(row_s, vectors_ref, which):
+    part = vector_parts(vectors_ref)[which]
+    width = part.stop - part.start
+    for s in range(vectors_ref.shape[0]):
+        row_s[:, s * width : (s + 1) * width] = vectors_ref[s, :, part].astype(f32)
 
 
 def lane_sums(value):
@@ -91,19 +97,23 @@
     )[:1]
 
 
-def step_sums(x, rate):
-    rows, cols = iotas((SPAN, SPAN))
-    steps = jnp.maximum(x, 0.0) + jnp.log1p(jnp.exp(-jnp.abs(x)))
-    scaled = steps * rate
-    fcum = mm(scaled[:HEADS], (rows <= cols).astype(f32), precise)
-    rcum = mm(scaled[HEADS:], (rows >= cols).astype(f32), precise)
-    return steps, fcum, rcum
-
-
-def span_tails(steps, fcum, rcum):
-    tail_f = jnp.exp2(fcum[:, SPAN - 1 :] - fcum) * steps[:HEADS]
-    tail_r = jnp.exp2(rcum[:, :1] - rcum) * steps[HEADS:]
-    return tail_f, tail_r
+def split_rows(value):
+    high = value.astype(bf16)
+    rest = value - high.astype(f32)
+    middle = rest.astype(bf16)
+    low = (rest - middle.astype(f32)).astype(bf16)
+    return jnp.concatenate([high, middle, low], axis=0)
+
+
+def exact_mm(value, ones):
+    m = value.shape[0]
+    parts = mm(split_rows(value), ones)
+    return (parts[2 * m :] + parts[m : 2 * m]) + parts[:m]
+
+
+def span_matrix(compare):
+    rows, cols = iotas((BLOCK, BLOCK))
+    return (compare(rows, cols) & (rows // SPAN == cols // SPAN)).astype(bf16)
 
 
 def enter_kernel(
@@ -111,16 +121,15 @@
     tok_ref,
     wide_ref,
     time_ref,
-    pre_ref,
-    taps_ref,
-    offset_ref,
+    vectors_ref,
     bias_ref,
     decay_ref,
     gate_o,
     fin_o,
     filt_o,
     act_o,
-    x_o,
+    rows_o,
+    cols_o,
     state_o,
     last_s,
     run_s,
@@ -130,6 +139,8 @@
     pre_s,
     rate_s,
     bias_s,
+    until_s,
+    from_s,
 ):
     seq = pl.program_id(0)
     block = pl.program_id(1)
@@ -137,12 +148,16 @@
 
     @pl.when((seq == 0) & (block == 0))
     def _():
-        spread_taps(taps_s, taps_ref, offset_ref)
-        join_row(pre_s, pre_ref)
+        for k in range(CONV + 1):
+            spread_vectors(taps_s.at[k], vectors_ref, k)
+        join_row(pre_s, vectors_ref, CONV + 1)
         rate_s[...] = rate_columns(decay_ref)
+        until_s[...] = span_matrix(lambda r, c: r <= c)
+        from_s[...] = span_matrix(lambda r, c: r >= c)
         bias_s[...] = column(bias_ref[...], BLOCK)
-        rows_d, cols_d = iotas((D, D))
-        time_s[...] = mm_tn(time_ref[...], (rows_d == cols_d).astype(bf16)).astype(bf16)
+        shards, _, width = time_ref.shape
+        for s in range(shards):
+            time_s[:, s * width : (s + 1) * width] = time_ref[s].astype(f32)
         for i in range(WIDE // 256):
             wide_s[i * 256 : (i + 1) * 256, :] = wide_ref[:, i * 256 : (i + 1) * 256].T
 
@@ -156,7 +171,25 @@
         tok = tok_ref[0].astype(f32)
         scale = lax.rsqrt(jnp.mean(tok * tok, axis=-1, keepdims=True) + EPS)
         normed = (tok * scale * pre_s[...]).astype(bf16)
-        x_o[0] = mm_nt(time_s[...], normed) + bias_s[...]
+        x = mm_nt(time_s[...].astype(bf16), normed) + bias_s[...]
+        steps = jnp.maximum(x, 0.0) + jnp.log1p(jnp.exp(-jnp.abs(x)))
+        scaled = steps * rate_s[:, :1]
+        fcum = exact_mm(scaled[:HEADS], until_s[...])
+        rcum = exact_mm(scaled[HEADS:], from_s[...])
+        least = jnp.log2(jnp.maximum(steps, TINY))
+        cums = jnp.concatenate([fcum, rcum], axis=0)
+        blank = jnp.zeros((SPAN - 48, BLOCK), f32)
+        cols_o[0] = jnp.concatenate([cums - least, blank], axis=0).T
+        rows_o[0, :48, :] = x
+        rows_o[0, 48:96, :] = steps
+        rows_o[0, 96:144, :] = cums
+        rows_o[0, 144:192, :] = jnp.exp2(cums)
+        for sub in range(SUBS):
+            part = slice(sub * SPAN, (sub + 1) * SPAN)
+            last = (sub + 1) * SPAN - 1
+            rows_o[0, 192:216, part] = jnp.exp2(fcum[:, last : last + 1] - fcum[:, part]) * steps[:HEADS, part]
+            first = sub * SPAN
+            rows_o[0, 216:240, part] = jnp.exp2(rcum[:, first : first + 1] - rcum[:, part]) * steps[HEADS:, part]
         place = block * BLOCK + lax.broadcasted_iota(jnp.int32, (1, BLOCK), 1)
         mask = (place < length).astype(f32)
 
@@ -196,11 +229,11 @@
 
         lane = lax.broadcasted_iota(jnp.int32, (1, SPAN), 1)
 
-        def span(sub, _):
-            cols = pl.ds(pl.multiple_of(sub * SPAN, SPAN), SPAN)
-            steps, fcum, rcum = step_sums(x_o[0, :, cols], rate_s[:, :1])
-            tail_f, tail_r = span_tails(steps, fcum, rcum)
-            decay = jnp.exp2(fcum[:, SPAN - 1 :])
+        for sub in range(SUBS):
+            cols = slice(sub * SPAN, (sub + 1) * SPAN)
+            tail_f = rows_o[0, 192:216, cols]
+            tail_r = rows_o[0, 216:240, cols]
+            decay = rows_o[0, 144:168, (sub + 1) * SPAN - 1 : (sub + 1) * SPAN]
             ins_f = act_o[0, INNER : INNER + 64, cols].astype(f32)
             ins_r = act_o[0, INNER + 128 : INNER + 192, cols].astype(f32)
             for h in range(HEADS):
@@ -216,9 +249,6 @@
                 run = run_s[rows, :]
                 state_o[0, sub, rows, :] = jnp.where(lane < 64, run, fresh).astype(bf16)
                 run_s[rows, :] = run * decay[h : h + 1] + fresh
-            return None
-
-        lax.fori_loop(0, SUBS, span, None)
 
 
 def middle_kernel(
@@ -228,11 +258,11 @@
     cot_ref,
     gate_ref,
     act_ref,
-    x_ref,
+    rows_ref,
+    cols_ref,
     state_ref,
     narrow_ref,
     post_ref,
-    decay_ref,
     result_o,
     dgate_o,
     dval_o,
@@ -255,7 +285,6 @@
     slope_s,
     norm_s,
     gain_s,
-    rate_s,
     narrow_s,
     post_s,
 ):
@@ -269,10 +298,7 @@
         narrow_s[...] = jnp.zeros_like(narrow_s)
         post_s[...] = jnp.zeros_like(post_s)
         skip_o[...] = jnp.zeros_like(skip_o)
-        shards, _, width = post_ref.shape
-        for s in range(shards):
-            gain_s[s * width : (s + 1) * width, :] = mm_tn(post_ref[s], jnp.ones((1, SPAN), bf16))
-        rate_s[...] = rate_columns(decay_ref)
+        spread_vectors(gain_s, post_ref, CONV + 2)
 
     @pl.when(step == 0)
     def _():
@@ -307,18 +333,14 @@
         def fold(value):
             return jnp.sum(value.reshape(8, 8, SPAN), axis=0)
 
-        def forward_span(back, _):
-            sub = SUBS - 1 - back
-            cols = pl.ds(pl.multiple_of(sub * SPAN, SPAN), SPAN)
-            steps, fcum, rcum = step_sums(x_ref[0, :, cols], rate_s[:, :1])
-            least = jnp.log2(jnp.maximum(steps, TINY))
-            columns = jnp.concatenate(
-                [fcum - least[:HEADS], rcum - least[HEADS:], jnp.zeros((SPAN - 48, SPAN), f32)],
-                axis=0,
-            ).T
-            out_f = jnp.exp2(fcum)
-            out_r = jnp.exp2(rcum)
-            decay = jnp.exp2(rcum[:, :1])
+        def forward_span(sub):
+            cols = slice(sub * SPAN, (sub + 1) * SPAN)
+            fcum = rows_ref[0, 96:120, cols]
+            rcum = rows_ref[0, 120:144, cols]
+            columns = cols_ref[0, cols, :]
+            out_f = rows_ref[0, 144:168, cols]
+            out_r = rows_ref[0, 168:192, cols]
+            decay = rows_ref[0, 168:192, sub * SPAN : sub * SPAN + 1]
             fi, fo, ri, ro = span_scores(cols)
             ahead_scores = jnp.where(lower, mm_tn(fi, fo), 0.0)
             behind_scores = jnp.where(upper, mm_tn(ri, ro), 0.0)
@@ -372,9 +394,9 @@
             pull = rs * rs * rs * (jnp.sum(dots, axis=0, keepdims=True) * (1.0 / INNER))
             norm_s[:1, cols] = rs
             norm_s[1:2, cols] = pull
-            return None
-
-        lax.fori_loop(0, SUBS, forward_span, None)
+
+        for sub in reversed(range(SUBS)):
+            forward_span(sub)
         rs = norm_s[:1, :]
 
         def norm_rows(i, _):
@@ -394,13 +416,11 @@
             rows = slice(i * 512, (i + 1) * 512)
             narrow_s[rows, :] += mm(gnormed[rows], slope_s[...])
 
-        def backward_span(back, _):
-            sub = SUBS - 1 - back
-            cols = pl.ds(pl.multiple_of(sub * SPAN, SPAN), SPAN)
-            steps, fcum, rcum = step_sums(x_ref[0, :, cols], rate_s[:, :1])
-            out_f = jnp.exp2(fcum)
-            out_r = jnp.exp2(rcum)
-            decay = jnp.exp2(fcum[:, SPAN - 1 :])
+        def backward_span(sub):
+            cols = slice(sub * SPAN, (sub + 1) * SPAN)
+            out_f = rows_ref[0, 144:168, cols]
+            out_r = rows_ref[0, 168:192, cols]
+            decay = rows_ref[0, 144:168, (sub + 1) * SPAN - 1 : (sub + 1) * SPAN]
             fi, fo, ri, ro = span_scores(cols)
             rs = norm_s[:1, cols]
             pull = norm_s[1:2, cols]
@@ -453,9 +473,9 @@
             dio_o[0, 64:128, cols] = dfo + mm(fi, low)
             dio_o[0, 128:192, cols] = mm_nt(ro, high)
             dio_o[0, 192:256, cols] = dro + mm(ri, high)
-            return None
-
-        lax.fori_loop(0, SUBS, backward_span, None)
+
+        for sub in reversed(range(SUBS)):
+            backward_span(sub)
 
     @pl.when((seq == pl.num_programs(0) - 1) & (step == pl.num_programs(1) - 1))
     def _():
@@ -475,7 +495,7 @@
     filt_ref,
     act_ref,
     fin_ref,
-    x_ref,
+    rows_ref,
     dval_ref,
     dio_ref,
     sums_ref,
@@ -496,6 +516,9 @@
     bias_s,
     decay_s,
     rate_s,
+    ends_s,
+    ahead_s,
+    behind_s,
 ):
     seq = pl.program_id(0)
     block = pl.program_id(1)
@@ -507,7 +530,14 @@
         taps_s[...] = jnp.zeros_like(taps_s)
         bias_s[...] = jnp.zeros_like(bias_s)
         decay_s[...] = jnp.zeros_like(decay_s)
-        rate_s[...] = rate_columns(decay_ref)
+        rate_s[...] = rate_columns(decay_ref) * (1.0 / LOG2E)
+        same = span_matrix(lambda r, c: r == r)
+        ahead_s[:BLOCK] = span_matrix(lambda r, c: r >= c)
+        ahead_s[BLOCK : 2 * BLOCK] = span_matrix(lambda r, c: r < c)
+        ahead_s[2 * BLOCK :] = same
+        behind_s[:BLOCK] = span_matrix(lambda r, c: r <= c)
+        behind_s[BLOCK : 2 * BLOCK] = span_matrix(lambda r, c: r > c)
+        behind_s[2 * BLOCK :] = same
 
     @pl.when(block == 0)
     def _():
@@ -516,21 +546,39 @@
 
     @pl.when(block * BLOCK < length)
     def _():
-        rows_i, cols_i = iotas((SPAN, SPAN))
         lane = lax.broadcasted_iota(jnp.int32, (1, SPAN), 1)
 
-        def span(sub, _):
-            cols = pl.ds(pl.multiple_of(sub * SPAN, SPAN), SPAN)
-            x = x_ref[0, :, cols]
-            steps, fcum, rcum = step_sums(x, rate_s[:, :1])
-            tail_f, tail_r = span_tails(steps, fcum, rcum)
-            decay = jnp.exp2(rcum[:, :1])
+        place = block * BLOCK + lax.broadcasted_iota(jnp.int32, (1, BLOCK), 1)
+        mask = (place < length).astype(f32)
+
+        def filter_rows(i):
+            r = slice(i * 32, (i + 1) * 32)
+            filt = filt_ref[0, r, :].astype(f32)
+            sig = sigmoid(filt)
+            dact = dact_s[r, :]
+            if i < INNER // 32:
+                dact = dact * mask
+            dfilt = dact * (sig * (1.0 + filt * (1.0 - sig)))
+            dfilt_o[0, r, :] = dfilt.astype(bf16)
+            offset_s[r, :] += dfilt[:, :SPAN] + dfilt[:, SPAN:]
+            fin = fin_ref[0, r, :]
+            w = jnp.concatenate([last_s[r, :], fin], axis=1)
+            last_s[r, :] = fin[:, SPAN:]
+            product = dfilt * fin.astype(f32)
+            taps_s[3, r, :] += product[:, :SPAN] + product[:, SPAN:]
+            for lag in range(1, CONV):
+                product = dfilt * pltpu.roll(w, lag, 1)[:, SPAN:].astype(f32)
+                taps_s[3 - lag, r, :] += product[:, :SPAN] + product[:, SPAN:]
+
+        def span(sub):
+            cols = slice(sub * SPAN, (sub + 1) * SPAN)
+            tail_f = rows_ref[0, 192:216, cols]
+            tail_r = rows_ref[0, 216:240, cols]
+            decay = rows_ref[0, 168:192, sub * SPAN : sub * SPAN + 1]
             fi = act_ref[0, INNER : INNER + 64, cols].astype(f32)
             ri = act_ref[0, INNER + 128 : INNER + 192, cols].astype(f32)
             dfi = jnp.zeros((64, SPAN), f32)
             dri = jnp.zeros((64, SPAN), f32)
-            ends_f = []
-            ends_r = []
             for h in range(HEADS):
                 rows = slice(h * 64, (h + 1) * 64)
                 weighted = jnp.concatenate(
@@ -543,7 +591,7 @@
                 dstate = dstate_ref[0, sub, rows, :].astype(f32)
                 run = grun_s[rows, :]
                 dfresh = jnp.where(lane < 64, dstate, run).astype(bf16)
-                near_s[h : h + 1, :] = decay[h : h + 1] * jnp.sum(
+                near_s[h : h + 1, cols] = decay[h : h + 1] * jnp.sum(
                     jnp.where(lane < 64, 0.0, run * rstate_ref[0, sub, rows, :].astype(f32)),
                     axis=0,
                     keepdims=True,
@@ -556,63 +604,48 @@
                 part_r = dweighted[64:] * tail_r[h : h + 1]
                 dfi = dfi + part_f
                 dri = dri + part_r
-                ends_f.append(jnp.sum(part_f * fi, axis=0, keepdims=True))
-                ends_r.append(jnp.sum(part_r * ri, axis=0, keepdims=True))
+                ends_s[h : h + 1, cols] = jnp.sum(part_f * fi, axis=0, keepdims=True)
+                ends_s[HEADS + h : HEADS + h + 1, cols] = jnp.sum(
+                    part_r * ri, axis=0, keepdims=True
+                )
+                if sub == SUBS - 1:
+                    filter_rows(2 * h)
+                    filter_rows(2 * h + 1)
             dact_s[INNER : INNER + 64, cols] = dio_ref[0, 0:64, cols] + dfi
             dact_s[INNER + 64 : INNER + 128, cols] = dio_ref[0, 64:128, cols]
             dact_s[INNER + 128 : INNER + 192, cols] = dio_ref[0, 128:192, cols] + dri
             dact_s[INNER + 192 : INNER + 256, cols] = dio_ref[0, 192:256, cols]
-            ends_f = jnp.concatenate(ends_f, axis=0)
-            ends_r = jnp.concatenate(ends_r, axis=0)
-            col_f = sums_ref[0, 2 * HEADS : 3 * HEADS, cols]
-            col_r = sums_ref[0, 3 * HEADS : 4 * HEADS, cols]
-            far_f = jnp.sum(sums_ref[0, 4 * HEADS :, cols], axis=1, keepdims=True)
-            far_r = jnp.sum(near_s[...], axis=1, keepdims=True)
-            dfa = mm(sums_ref[0, :HEADS, cols] - col_f, (rows_i >= cols_i).astype(f32), precise)
-            dra = mm(
-                sums_ref[0, HEADS : 2 * HEADS, cols] - col_r,
-                (rows_i <= cols_i).astype(f32),
-                precise,
-            )
-            dfa = dfa + far_f + mm(ends_f, (rows_i < cols_i).astype(f32), precise)
-            dra = dra + far_r + mm(ends_r, (rows_i > cols_i).astype(f32), precise)
-            sig = jax.nn.sigmoid(x)
-            rate = rate_s[:, :1] * (1.0 / LOG2E)
-            share = sig / jnp.maximum(steps, TINY)
-            span_d = jnp.concatenate([dfa, dra], axis=0)
-            draw = jnp.concatenate([col_f + ends_f, col_r + ends_r], axis=0) * share + span_d * (rate * sig)
-            draw_o[0, :, cols] = draw.astype(bf16)
-            bias_s[...] += draw
-            decay_s[...] += span_d * steps * rate
-            return None
-
-        lax.fori_loop(0, SUBS, span, None)
-        place = block * BLOCK + lax.broadcasted_iota(jnp.int32, (1, BLOCK), 1)
-        mask = (place < length).astype(f32)
-
-        def filter_rows(i, masked):
-            r = pl.ds(pl.multiple_of(i * 32, 32), 32)
-            filt = filt_ref[0, r, :].astype(f32)
-            sig = sigmoid(filt)
-            dact = dact_s[r, :]
-            if masked:
-                dact = dact * mask
-            dfilt = dact * (sig * (1.0 + filt * (1.0 - sig)))
-            dfilt_o[0, r, :] = dfilt.astype(bf16)
-            offset_s[r, :] += dfilt[:, :SPAN] + dfilt[:, SPAN:]
-            fin = fin_ref[0, r, :]
-            w = jnp.concatenate([last_s[r, :], fin], axis=1)
-            last_s[r, :] = fin[:, SPAN:]
-            product = dfilt * fin.astype(f32)
-            taps_s[3, r, :] += product[:, :SPAN] + product[:, SPAN:]
-            for lag in range(1, CONV):
-                product = dfilt * pltpu.roll(w, lag, 1)[:, SPAN:].astype(f32)
-                taps_s[3 - lag, r, :] += product[:, :SPAN] + product[:, SPAN:]
-            return None
-
-        lax.fori_loop(0, INNER // 32, lambda i, _: filter_rows(i, True), None, unroll=8)
-        lax.fori_loop(INNER // 32, CHANNELS // 32, lambda i, _: filter_rows(i, False), None, unroll=8)
-
+
+        for sub in range(SUBS):
+            span(sub)
+        for i in range(INNER // 32, CHANNELS // 32):
+            filter_rows(i)
+        col_f = sums_ref[0, 2 * HEADS : 3 * HEADS, :]
+        col_r = sums_ref[0, 3 * HEADS : 4 * HEADS, :]
+        ends_f = ends_s[:HEADS, :]
+        ends_r = ends_s[HEADS:, :]
+        dfa = exact_mm(
+            jnp.concatenate(
+                [sums_ref[0, :HEADS, :] - col_f, ends_f, sums_ref[0, 4 * HEADS :, :]], axis=1
+            ),
+            ahead_s[...],
+        )
+        dra = exact_mm(
+            jnp.concatenate(
+                [sums_ref[0, HEADS : 2 * HEADS, :] - col_r, ends_r, near_s[...]], axis=1
+            ),
+            behind_s[...],
+        )
+        sig = jax.nn.sigmoid(rows_ref[0, :48, :])
+        steps = rows_ref[0, 48:96, :]
+        rate = rate_s[:, :1]
+        share = sig / jnp.maximum(steps, TINY)
+        passed = jnp.concatenate([dfa, dra], axis=0) * rate
+        draw = jnp.concatenate([col_f + ends_f, col_r + ends_r], axis=0) * share + passed * sig
+        draw_o[0] = draw.astype(bf16)
+        bias_s[...] += draw[:, :SPAN] + draw[:, SPAN:]
+        product = passed * steps
+        decay_s[...] += product[:, :SPAN] + product[:, SPAN:]
     @pl.when((seq == pl.num_programs(0) - 1) & (block == pl.num_programs(1) - 1))
     def _():
         lines_o[...] = jnp.zeros_like(lines_o)
@@ -635,8 +668,7 @@
     draw_ref,
     wide_ref,
     time_ref,
-    pre_ref,
-    taps_ref,
+    vectors_ref,
     lines_ref,
     post_ref,
     slope_o,
@@ -649,6 +681,7 @@
     total_s,
     pre_s,
     lines_s,
+    turned_s,
 ):
     seq = pl.program_id(0)
     block = pl.program_id(1)
@@ -659,8 +692,12 @@
         wide_s[...] = jnp.zeros_like(wide_s)
         time_s[...] = jnp.zeros_like(time_s)
         total_s[...] = jnp.zeros_like(total_s)
-        spread_taps(taps_s, taps_ref, None)
-        join_row(pre_s, pre_ref)
+        for k in range(CONV):
+            spread_vectors(taps_s.at[k], vectors_ref, k)
+        join_row(pre_s, vectors_ref, CONV + 1)
+        shards, _, width = time_ref.shape
+        for s in range(shards):
+            turned_s[:, s * width : (s + 1) * width] = time_ref[s].astype(f32)
 
     @pl.when(block * BLOCK >= length)
     def _():
@@ -672,11 +709,10 @@
         scale = lax.rsqrt(jnp.mean(tok * tok, axis=-1, keepdims=True) + EPS)
         normed = (tok * scale * pre_s[...]).astype(bf16)
         normed_t = normed.T
-        dproj_s[:INNER, :] = dgate_ref[0]
         beyond = (block + 1) * BLOCK < length
 
-        def filter_rows(i, _):
-            r = pl.ds(pl.multiple_of(i * 32, 32), 32)
+        def filter_rows(i):
+            r = slice(i * 32, (i + 1) * 32)
             following = jnp.where(beyond, next_ref[0, r, :].astype(f32), 0.0).astype(bf16)
             now = dfilt_ref[0, r, :]
             w = jnp.concatenate([now, following], axis=1)
@@ -685,16 +721,28 @@
             for lag in range(1, CONV):
                 moved = pltpu.roll(w, BLOCK + SPAN - lag, 1)[:, :BLOCK].astype(f32)
                 acc = acc + twice(3 - lag) * moved
-            dproj_s[pl.ds(pl.multiple_of(INNER + i * 32, 32), 32), :] = acc.astype(bf16)
-            return None
-
-        lax.fori_loop(0, CHANNELS // 32, filter_rows, None, unroll=8)
+            dproj_s[i * 32 : (i + 1) * 32, :] = acc.astype(bf16)
+
+        groups = CHANNELS // 32
+        done = 0
         for i in range(WIDE // 256):
             rows = slice(i * 256, (i + 1) * 256)
-            wide_s[:, rows] += mm_nt(normed_t, dproj_s[rows, :])
+            if i < INNER // 256:
+                right = dgate_ref[0, rows, :]
+            else:
+                right = dproj_s[i * 256 - INNER : (i + 1) * 256 - INNER, :]
+            wide_s[:, rows] += mm_nt(normed_t, right)
+            upto = min(groups, -(-groups * (i + 1) // (INNER // 256)))
+            for j in range(done, upto):
+                filter_rows(j)
+            done = upto
         draw = draw_ref[0]
-        time_s[:, : 2 * HEADS] += mm_nt(normed_t, draw)
-        dnormed = (mm(wide_ref[...], dproj_s[...]) + mm(time_ref[...], draw)).T
+        time_s[...] += mm(draw, normed)
+        dnormed = (
+            mm(wide_ref[:, :INNER], dgate_ref[0])
+            + mm(wide_ref[:, INNER:], dproj_s[...])
+            + mm_tn(turned_s[...].astype(bf16), draw)
+        ).T
         product = dnormed * tok
         total_s[...] += jnp.sum((product * scale).reshape(BLOCK // 8, 8, D), axis=0)
         gain = pre_s[...]
@@ -709,7 +757,12 @@
             own = slice(s * rows, (s + 1) * rows)
             for unit in range(tiles):
                 wide_o[unit, s] = wide_s[own, unit * SPAN : (unit + 1) * SPAN].astype(bf16)
-            small_o[0, s] = time_s[own, :].astype(bf16)
+            lines_s[...] = jnp.zeros_like(lines_s)
+            time_rows = time_s[...]
+            for start in range(0, 2 * HEADS, rows):
+                size = min(rows, 2 * HEADS - start)
+                lines_s[:size, start : start + rows] = time_rows[start : start + size, own]
+            small_o[0, s] = lines_s[...].astype(bf16)
         pre_sum = jnp.sum(total_s[...], axis=0, keepdims=True)
         vectors = [(lines_ref[k : k + 1, :], CHANNELS // shards) for k in range(CONV + 1)]
         vectors += [(pre_sum, rows), (post_ref[...], INNER // shards)]
@@ -732,11 +785,10 @@
 
 
 def layer(
-    tokens, cotangent, lengths, wide, time, narrow, taps, offset, prenorm, postnorm,
-    timestep_bias, decay_log, skip_gain,
+    tokens, cotangent, lengths, wide, time, narrow, vectors, timestep_bias, decay_log, skip_gain
 ):
     count, length = tokens.shape[:2]
-    shards = taps.shape[0]
+    shards = vectors.shape[0]
     rows = D // shards
     blocks = length // BLOCK
     spans = length // SPAN
@@ -761,31 +813,38 @@
             return pl.BlockSpec((1, SUBS, INNER, SPAN), lambda s, c, *_: (s, blocks - 1 - c, 0, 0))
         return pl.BlockSpec((1, SUBS, INNER, SPAN), lambda s, c, *_: (s, c, 0, 0))
 
+    def turned(reverse):
+        if reverse:
+            return pl.BlockSpec((1, BLOCK, SPAN), lambda s, c, *_: (s, blocks - 1 - c, 0))
+        return pl.BlockSpec((1, BLOCK, SPAN), lambda s, c, *_: (s, c, 0))
+
     params = pltpu.CompilerParams(
         dimension_semantics=("arbitrary", "arbitrary"), vmem_limit_bytes=VMEM_LIMIT
     )
     state_shape = sds((count, spans, INNER, SPAN), bf16)
-    gate, fin, filt, act, x, state = pl.pallas_call(
+    gate, fin, filt, act, step_rows, step_cols, state = pl.pallas_call(
         enter_kernel,
         grid_spec=pltpu.PrefetchScalarGridSpec(
             num_scalar_prefetch=1,
             grid=grid,
             in_specs=[
-                tall(False), whole((D, WIDE)), whole((D, 48)), whole(prenorm.shape),
-                whole(taps.shape), whole(offset.shape), whole((1, 48)), whole((1, HEADS)),
+                tall(False), whole((D, WIDE)), whole(time.shape), whole(vectors.shape),
+                whole((1, 48)), whole((1, HEADS)),
             ],
             out_specs=[
-                ahead(INNER), ahead(CHANNELS), ahead(CHANNELS), ahead(CHANNELS), ahead(48), states(False),
+                ahead(INNER), ahead(CHANNELS), ahead(CHANNELS), ahead(CHANNELS), ahead(240), turned(False), states(False),
             ],
             scratch_shapes=[
                 pltpu.VMEM((CHANNELS, SPAN), bf16),
                 pltpu.VMEM((INNER, SPAN), f32),
                 pltpu.VMEM((CONV + 1, CHANNELS, SPAN), f32),
                 pltpu.VMEM((WIDE, D), bf16),
-                pltpu.VMEM((48, D), bf16),
+                pltpu.VMEM((48, D), f32),
                 pltpu.VMEM((1, D), f32),
                 pltpu.VMEM((48, SPAN), f32),
                 pltpu.VMEM((48, BLOCK), f32),
+                pltpu.VMEM((BLOCK, BLOCK), bf16),
+                pltpu.VMEM((BLOCK, BLOCK), bf16),
             ],
         ),
         out_shape=[
@@ -793,12 +852,13 @@
             sds((count, CHANNELS, length), bf16),
             sds((count, CHANNELS, length), bf16),
             sds((count, CHANNELS, length), bf16),
-            sds((count, 48, length), f32),
+            sds((count, 240, length), f32),
+            sds((count, length, SPAN), f32),
             state_shape,
         ],
         compiler_params=params,
         name="enter",
-    )(lengths, tokens, wide, time, prenorm, taps, offset, bias, decay)
+    )(lengths, tokens, wide, time, vectors, bias, decay)
 
     across = 2 * D // SPAN
     result, dgate, dval, dio, sums, dstate, rstate, narrow_grad, post_grad, skip_grad = pl.pallas_call(
@@ -808,8 +868,8 @@
             grid=grid,
             in_specs=[
                 pl.BlockSpec(memory_space=pltpu.SMEM),
-                tall(True), tall(True), back(INNER), back(CHANNELS), back(48), states(True),
-                whole((INNER, D)), whole(postnorm.shape), whole((1, HEADS)),
+                tall(True), tall(True), back(INNER), back(CHANNELS), back(240), turned(True), states(True),
+                whole((INNER, D)), whole(vectors.shape),
             ],
             out_specs=[
                 tall(True), back(INNER), back(INNER), back(256), back(120), states(True), states(True),
@@ -828,7 +888,6 @@
                 pltpu.VMEM((BLOCK, D), bf16),
                 pltpu.VMEM((8, BLOCK), f32),
                 pltpu.VMEM((INNER, SPAN), f32),
-                pltpu.VMEM((48, SPAN), f32),
                 pltpu.VMEM((INNER, D), f32),
                 pltpu.VMEM((INNER, SPAN), f32),
             ],
@@ -847,7 +906,7 @@
         ],
         compiler_params=params,
         name="middle",
-    )(lengths, skip_gain, tokens, cotangent, gate, act, x, state, narrow, postnorm, decay)
+    )(lengths, skip_gain, tokens, cotangent, gate, act, step_rows, step_cols, state, narrow, vectors)
 
     dfilt, draw, lines, heads = pl.pallas_call(
         leave_kernel,
@@ -855,7 +914,7 @@
             num_scalar_prefetch=1,
             grid=grid,
             in_specs=[
-                ahead(CHANNELS), ahead(CHANNELS), ahead(CHANNELS), ahead(48), ahead(INNER), ahead(256), ahead(120),
+                ahead(CHANNELS), ahead(CHANNELS), ahead(CHANNELS), ahead(240), ahead(INNER), ahead(256), ahead(120),
                 states(False), states(False), whole((1, HEADS)), whole((HEADS, SPAN)),
             ],
             out_specs=[
@@ -863,7 +922,7 @@
             ],
             scratch_shapes=[
                 pltpu.VMEM((INNER, SPAN), f32),
-                pltpu.VMEM((HEADS, SPAN), f32),
+                pltpu.VMEM((HEADS, BLOCK), f32),
                 pltpu.VMEM((CHANNELS, BLOCK), f32),
                 pltpu.VMEM((CHANNELS, SPAN), bf16),
                 pltpu.VMEM((CHANNELS, SPAN), f32),
@@ -871,6 +930,9 @@
                 pltpu.VMEM((48, SPAN), f32),
                 pltpu.VMEM((48, SPAN), f32),
                 pltpu.VMEM((48, SPAN), f32),
+                pltpu.VMEM((48, BLOCK), f32),
+                pltpu.VMEM((3 * BLOCK, BLOCK), bf16),
+                pltpu.VMEM((3 * BLOCK, BLOCK), bf16),
             ],
         ),
         out_shape=[
@@ -881,7 +943,7 @@
         ],
         compiler_params=params,
         name="leave",
-    )(lengths, filt, act, fin, x, dval, dio, sums, dstate, rstate, decay, skip_grad)
+    )(lengths, filt, act, fin, step_rows, dval, dio, sums, dstate, rstate, decay, skip_grad)
 
     slope, wide_grad, small_grad = pl.pallas_call(
         widen_kernel,
@@ -895,20 +957,21 @@
                     lambda s, c, *_: (s, 0, jnp.minimum(SUBS * (c + 1), spans - 1)),
                 ),
                 ahead(48),
-                whole((D, WIDE)), whole((D, 48)), whole(prenorm.shape), whole(taps.shape),
+                whole((D, WIDE)), whole(time.shape), whole(vectors.shape),
                 whole((8, CHANNELS)), whole((1, INNER)),
             ],
             out_specs=[
                 tall(False), whole((WIDE // SPAN, shards, rows, SPAN)), whole((2, shards, rows, SPAN)),
             ],
             scratch_shapes=[
-                pltpu.VMEM((WIDE, BLOCK), bf16),
+                pltpu.VMEM((CHANNELS, BLOCK), bf16),
                 pltpu.VMEM((CONV, CHANNELS, SPAN), f32),
                 pltpu.VMEM((D, WIDE), f32),
-                pltpu.VMEM((D, SPAN), f32),
+                pltpu.VMEM((48, D), f32),
                 pltpu.VMEM((8, D), f32),
                 pltpu.VMEM((1, D), f32),
                 pltpu.VMEM((rows, SPAN), f32),
+                pltpu.VMEM((48, D), f32),
             ],
         ),
         out_shape=[
@@ -918,7 +981,7 @@
         ],
         compiler_params=params,
         name="widen",
-    )(lengths, tokens, cotangent, dgate, dfilt, dfilt, draw, wide, time, prenorm, taps, lines, post_grad)
+    )(lengths, tokens, cotangent, dgate, dfilt, dfilt, draw, wide, time, vectors, lines, post_grad)
     return result, slope, wide_grad, narrow_grad, small_grad, heads
 
 
@@ -1219,7 +1282,10 @@
             narrow_o[core * rows : (core + 1) * rows, j * SPAN : (j + 1) * SPAN] = read(
                 core, tiles_wide + j
             )
-    time_o[...] = read(0, tiles_wide + tiles_narrow)[:, : 2 * HEADS]
+    times = read(0, tiles_wide + tiles_narrow)
+    for start in range(0, 2 * HEADS, rows):
+        size = min(rows, 2 * HEADS - start)
+        time_o[start : start + size, :] = times[:size, start : start + rows]
     vectors = read(1, tiles_wide + tiles_narrow)
     line = 0
     outs = [(taps_o, k) for k in range(CONV)] + [(offset_o, 0), (pre_o, 0), (post_o, 0)]
@@ -1236,7 +1302,7 @@
 
 def finish(summed, heads, wide, rows, width):
     shapes = [
-        (rows, WIDE), (rows, 2 * HEADS), (2 * rows, D), (CONV, width), (1, width), (1, rows), (1, 2 * rows),
+        (rows, WIDE), (2 * HEADS, rows), (2 * rows, D), (CONV, width), (1, width), (1, rows), (1, 2 * rows),
         (1, 2 * HEADS), (1, HEADS), (1, HEADS),
     ]
     return pl.pallas_call(
@@ -1247,59 +1313,52 @@
     )(summed, heads)
 
 
-def gather_kernel(lines, cuts, kinds, *refs):
+def gather_kernel(lines, large, kinds, *refs):
     ins, outs = refs[:kinds], refs[kinds : 2 * kinds]
-    send_sem, recv_sem, own_sem = refs[2 * kinds :]
+    send_sem, recv_sem, own_sem, small_send, small_recv = refs[2 * kinds :]
     rep = lax.axis_index("rep")
     shard = lax.axis_index("shard")
-    core = lax.rem(rep, 2)
+    shards = 2 * lines
+    core, x = lax.rem(rep, 2), lax.div(rep, 2)
+    odd = lax.rem(x, 2)
     y, z = lax.rem(shard, 2), lax.div(shard, 2)
-    half = sum(cuts)
     sibling = peer(rep + 1 - 2 * core, shard)
+    across = peer((x + 1 - 2 * odd) * 2 + core, shard)
     partner = peer(rep, shard + 1 - 2 * y)
     has_up, has_down = z < lines - 1, z > 0
     up = peer(rep, jnp.minimum(z + 1, lines - 1) * 2 + y)
     down = peer(rep, jnp.maximum(z - 1, 0) * 2 + y)
-    barrier = pltpu.get_barrier_semaphore()
-
-    def hello(device):
-        pl.semaphore_signal(barrier, inc=1, device_id=device, device_id_type=pl.DeviceIdType.MESH)
-
-    hello(sibling)
-    hello(partner)
-    pl.when(has_up)(lambda: hello(up))
-    pl.when(has_down)(lambda: hello(down))
-    pl.semaphore_wait(barrier, 2 + has_up.astype(jnp.int32) + has_down.astype(jnp.int32))
+    away = [lax.rem(shard + k, shards) for k in range(1, shards)]
+    greet([sibling, across, *[peer(rep, other) for other in away]])
 
     own = [
         pltpu.make_async_copy(src, dst.at[shard], own_sem.at[i])
         for i, (src, dst) in enumerate(zip(ins, outs))
     ]
-    for copy in own:
-        copy.start()
-
-    def place(order, part, ref, index, side):
-        if part:
-            return ref if index is None else ref.at[index]
-        start = pl.multiple_of(side * half + (cuts[0] if order else 0), 128)
-        columns = pl.ds(start, cuts[order])
+
+    def place(group, part, ref, index, side):
+        half = ref.shape[-1] // SPAN // 2
+        thin = max(1, half * 5 // 13)
+        thick = half - 2 * thin
+        start = side * half
+        if group:
+            swap = odd if group == 1 else 1 - odd
+            start = start + thick + swap * thin
+        columns = pl.ds(pl.multiple_of(start * SPAN, SPAN), (thin if group else thick) * SPAN)
         return ref.at[:, columns] if index is None else ref.at[index, :, columns]
 
-    def copies(way, order, index, device, mine=False, side=None):
+    def copies(way, group, index, device, mine=False, side=None):
         side = core if side is None else side
-        parts = range(kinds) if order == 0 and way != 3 else (0,)
-        made = []
-        for part in parts:
-            made.append(
-                remote(
-                    place(order, part, ins[part] if mine else outs[part], None if mine else index, side),
-                    place(order, part, outs[part], index, side),
-                    send_sem.at[way, order, part, index],
-                    recv_sem.at[way, order, part, index],
-                    device,
-                )
+        return [
+            remote(
+                place(group, part, ins[part] if mine else outs[part], None if mine else index, side),
+                place(group, part, outs[part], index, side),
+                send_sem.at[way, group, part, index],
+                recv_sem.at[way, 1 if way == 4 else group, part, index],
+                device,
             )
-        return made
+            for part in range(large)
+        ]
 
     def start(*args, **kw):
         for copy in copies(*args, **kw):
@@ -1318,92 +1377,123 @@
     def index_of(line, side):
         return line * 2 + side
 
-    start(0, 1, shard, partner, mine=True)
-    pl.when(has_up)(lambda: start(1, 0, shard, up, mine=True))
-    pl.when(has_down)(lambda: start(2, 0, shard, down, mine=True))
-    pl.when(has_up)(lambda: start(1, 1, shard, up, mine=True))
-    pl.when(has_down)(lambda: start(2, 1, shard, down, mine=True))
-    start(0, 0, shard, partner, mine=True)
-    arrive(0, 1, other, partner)
-    pl.when(has_up)(lambda: start(1, 1, other, up))
-    pl.when(has_down)(lambda: start(2, 1, other, down))
-    start(3, 1, other, sibling)
-
-    def line_step(k, order, side):
+    for group in (1, 0):
+        pl.when(has_up)(lambda group=group: start(1, group, shard, up, mine=True))
+        pl.when(has_down)(lambda group=group: start(2, group, shard, down, mine=True))
+        start(0, group, shard, partner, mine=True)
+    for copy in own:
+        copy.start()
+    small = []
+    for k, index in enumerate(away):
+        for part in range(large, kinds):
+            copy = remote(
+                ins[part], outs[part].at[shard], small_send.at[part - large, k], small_recv.at[part - large, k],
+                peer(rep, index),
+            )
+            copy.start()
+            small.append(copy)
+
+    def line_step(k, group):
+        def spread(index):
+            start(0, group, index, partner)
+            if group == 1:
+                start(4, 1, index, across)
+            start(3, group, index, sibling)
+
         def from_below():
-            index = index_of(z - k, side)
-            arrive(1, order, index, down)
-            pl.when(has_up)(lambda: start(1, order, index, up))
-            start(3, order, index, sibling)
-            if order == 0:
-                start(0, 0, index, partner)
+            index = index_of(z - k, y)
+            arrive(1, group, index, down)
+            pl.when(has_up)(lambda: start(1, group, index, up))
+            spread(index)
 
         def from_above():
-            index = index_of(z + k, side)
-            arrive(2, order, index, up)
-            pl.when(has_down)(lambda: start(2, order, index, down))
-            start(3, order, index, sibling)
-            if order == 0:
-                start(0, 0, index, partner)
+            index = index_of(z + k, y)
+            arrive(2, group, index, up)
+            pl.when(has_down)(lambda: start(2, group, index, down))
+            spread(index)
 
         pl.when(z - k >= 0)(from_below)
         pl.when(z + k < lines)(from_above)
 
+    def take(group, index):
+        arrive(0, group, index, partner)
+        if group == 1:
+            start(4, 1, index, across)
+        start(3, group, index, sibling)
+
+    def cross(index):
+        arrive(4, 2, index, across)
+        start(3, 2, index, sibling)
+
+    def either(k, action, side):
+        pl.when(z - k >= 0)(lambda: action(index_of(z - k, side)))
+        if k:
+            pl.when(z + k < lines)(lambda: action(index_of(z + k, side)))
+
+    take(1, other)
+    take(0, other)
     for k in range(1, lines):
-        line_step(k, 0, y)
-        line_step(k, 1, y)
-        line_step(k, 1, 1 - y)
-    for k in range(lines):
-
-        def take(index):
-            arrive(0, 0, index, partner)
-            start(3, 0, index, sibling)
-
-        pl.when(z - k >= 0)(lambda k=k: take(index_of(z - k, 1 - y)))
-        if k:
-            pl.when(z + k < lines)(lambda k=k: take(index_of(z + k, 1 - y)))
-    for index in range(2 * lines):
+        line_step(k, 1)
+        line_step(k, 0)
+        if k > 1:
+            either(k - 1, partial(take, 1), 1 - y)
+            either(k - 1, partial(take, 0), 1 - y)
+    either(lines - 1, partial(take, 1), 1 - y)
+    either(lines - 1, partial(take, 0), 1 - y)
+    either(0, cross, 1 - y)
+    for k in range(1, lines):
+        either(k, cross, y)
+        either(k, cross, 1 - y)
+    for index in range(shards):
 
         @pl.when(index != shard)
         def _(index=index):
-            for order in range(2):
-                arrive(3, order, index, sibling, side=1 - core)
-                sent(3, order, index, sibling)
+            for group in range(3):
+                arrive(3, group, index, sibling, side=1 - core)
+                sent(3, group, index, sibling)
+            sent(4, 1, index, across)
 
     for line in range(lines):
-        sent(0, 0, index_of(line, y), partner)
-    sent(0, 1, shard, partner)
-    for line in range(lines):
-        for order, side in ((0, y), (1, y), (1, 1 - y)):
-            index = index_of(line, side)
+        for group in range(2):
+            index = index_of(line, y)
+            sent(0, group, index, partner)
 
             @pl.when((line <= z) & has_up)
-            def _(order=order, index=index):
-                sent(1, order, index, up)
+            def _(group=group, index=index):
+                sent(1, group, index, up)
 
             @pl.when((line >= z) & has_down)
-            def _(order=order, index=index):
-                sent(2, order, index, down)
+            def _(group=group, index=index):
+                sent(2, group, index, down)
 
     for copy in own:
         copy.wait()
-
-
-def gather_weights(arrays, lines):
+    for copy in small:
+        copy.wait_send()
+    for k in range(1, shards):
+        index = lax.rem(shard + shards - k, shards)
+        for part in range(large, kinds):
+            remote(
+                ins[part], outs[part].at[index], small_send.at[part - large, k - 1],
+                small_recv.at[part - large, k - 1], peer(rep, index),
+            ).wait_recv()
+
+
+def gather_weights(arrays, large, lines):
     shards = 2 * lines
-    half = arrays[0].shape[1] // 2
-    first = half * 5 // 8 // 128 * 128
     hbm = pl.BlockSpec(memory_space=pl.ANY)
     kinds = len(arrays)
     return pl.pallas_call(
-        partial(gather_kernel, lines, (first, half - first), kinds),
+        partial(gather_kernel, lines, large, kinds),
         in_specs=[hbm] * kinds,
         out_specs=[hbm] * kinds,
         out_shape=[jax.ShapeDtypeStruct((shards, *a.shape), a.dtype) for a in arrays],
         scratch_shapes=[
-            pltpu.SemaphoreType.DMA((4, 2, kinds, shards)),
-            pltpu.SemaphoreType.DMA((4, 2, kinds, shards)),
+            pltpu.SemaphoreType.DMA((5, 3, large, shards)),
+            pltpu.SemaphoreType.DMA((5, 3, large, shards)),
             pltpu.SemaphoreType.DMA((kinds,)),
+            pltpu.SemaphoreType.DMA((kinds - large, shards - 1)),
+            pltpu.SemaphoreType.DMA((kinds - large, shards - 1)),
         ],
         compiler_params=pltpu.CompilerParams(collective_id=0, has_side_effects=True),
         name="gather",
@@ -1429,18 +1519,15 @@
     wide = lax.axis_size("rep") // 2
     rows = widen_weight.shape[0]
     width = filter_weight.shape[1]
-    widen, timestep, taps, offset, prenorm, postnorm = gather_weights(
-        [
-            widen_weight, timestep_weight, filter_weight,
-            filter_offset[None], prenorm_gain[None], postnorm_gain[None],
-        ],
-        lines,
+    own = jnp.concatenate(
+        [filter_weight.reshape(-1), filter_offset, prenorm_gain, postnorm_gain]
     )
-    narrow_weight, taps = lax.optimization_barrier((narrow_weight, taps))
-    narrow = lax.all_gather(narrow_weight, "shard", axis=0, tiled=True)
+    widen, narrow, timestep, vectors = gather_weights(
+        [widen_weight, narrow_weight, timestep_weight.T, own[None]], 2, lines
+    )
     result, slope, wide_grad, narrow_grad, small_grad, heads = layer(
-        tokens, cotangent, lengths, widen.reshape(D, WIDE), timestep.reshape(D, 2 * HEADS), narrow,
-        taps, offset, prenorm, postnorm, timestep_bias, decay_log, skip_gain,
+        tokens, cotangent, lengths, widen.reshape(D, WIDE), timestep, narrow.reshape(INNER, D),
+        vectors, timestep_bias, decay_log, skip_gain,
     )
     summed, heads = reduce_units(wide_grad, narrow_grad, small_grad, heads, wide, lines)
     (
@@ -1448,7 +1535,7 @@
         bias_out, decay_out, skip_out,
     ) = finish(summed, heads, wide, rows, width)
     return (
-        result, slope, widen_out, timestep_out, narrow_out, filter_out,
+        result, slope, widen_out, timestep_out.T, narrow_out, filter_out,
         *[row.reshape(-1) for row in (offset_out, prenorm_out, postnorm_out, bias_out, decay_out, skip_out)],
     )
 

time: 371 us -> 303 us (0.82)
  Pallas kernels: 334 us -> 297 us
  waiting for transfers between devices: 17.4 us -> 0 us
  between operations: 14.1 us -> 0.82 us
    all_gather x1 -> x0, waiting for transfers between devices: 17.4 us -> none  [local(): narrow = lax.all_gather(narrow_weight, 'shard', axis=0, tiled=True)]
    pallas_call x1, Pallas kernels: 103 us -> 90.7 us  [reduce_units(): pl.pallas_call(partial(reduce_kernel, lines, wide), in_specs=[hbm, hbm, h...]
    pallas_call x1, Pallas kernels: 39.7 us -> 32.2 us  [layer(): pl.pallas_call(widen_kernel, grid_spec=pltpu.PrefetchScalarGridSpec(num_s...]
    pallas_call x1, Pallas kernels: 69.8 us -> 62.5 us  [layer(): pl.pallas_call(middle_kernel, grid_spec=pltpu.PrefetchScalarGridSpec(num_...]
    pallas_call x1, Pallas kernels: 39 us -> 32.5 us  [layer(): pl.pallas_call(leave_kernel, grid_spec=pltpu.PrefetchScalarGridSpec(num_s...]
    pallas_call x1, Pallas kernels: 34.3 us -> 30.2 us  [layer(): pl.pallas_call(enter_kernel, grid_spec=pltpu.PrefetchScalarGridSpec(num_s...]
  transfers between devices with their start and end apart: 1 -> 0, of which waited for: 1 -> 0; matrix products, arithmetic and copies ran while one was open for 0% -> 0% of each run, Pallas kernels for 9% -> 0%
where the time goes in v4:
time: 303 us; the launch traced here: 302 us
  Pallas kernels  297 us (98%)
  local copies, waits for them, and re-layouts  3.46 us (1%)
    pallas_call x1, Pallas kernels, reduce_units(): pl.pallas_call(partial(reduce_kernel, lines, wide), in_specs=[hbm, hbm, h...  90.7 us
    pallas_call x1, Pallas kernels, layer(): pl.pallas_call(middle_kernel, grid_spec=pltpu.PrefetchScalarGridSpec(num_...  62.5 us
    pallas_call x1, Pallas kernels, gather_weights(): pl.pallas_call(partial(gather_kernel, lines, large, kinds), in_specs=[hbm...  46.6 us
    pallas_call x1, Pallas kernels, layer(): pl.pallas_call(leave_kernel, grid_spec=pltpu.PrefetchScalarGridSpec(num_s...  32.5 us
    pallas_call x1, Pallas kernels, layer(): pl.pallas_call(widen_kernel, grid_spec=pltpu.PrefetchScalarGridSpec(num_s...  32.2 us
    pallas_call x1, Pallas kernels, layer(): pl.pallas_call(enter_kernel, grid_spec=pltpu.PrefetchScalarGridSpec(num_s...  30.2 us

profile of v4, /device:TPU:0, one launch (start us, length us, event | category | flops | bytes accessed | tf_op | source)
XLA Modules:
  0.0 301.6 jit_solution(15530142282594596211)
XLA Ops:
  0.6 0.8 reshape.60
  1.4 2.1 concatenate.3
  3.5 0.6 broadcast_in_dim.9.refs_3_
  4.1 46.6 %gather.1 = (bf16[8,96,3328]{2,1,0:T(8,128)(2,1)}, bf16[8,192,768]{2,1,0:T(8,128)(2,1)}, bf16[8,48,96]{2,1,0:T(8,128)(2,1)}, bf16[8,1,1408]{2,1,0:T(2,128)(2,1)}) custom-call(bf16[96,3328]{1,0:T(8,128)(2,1)} %refs_0_.1, bf16[192,768]{1,0:T(8,128)(2,1)} %refs_1_.1, bf16[48,96]{1,0:T(8,128)(2,1)} %bitcast.21, bf16[1,1408]{1,0:T(2,128)(2,1)} %broadcast_in_dim.9.refs_3_), custom_call_target="tpu_custom_call" | custom-call | tf_op jit(solution)/shard_map/gather/pallas_call | solution.py:1486
  50.7 30.2 %enter.1 = (bf16[2,1536,1024]{2,1,0:T(8,128)(2,1)}, bf16[2,1792,1024]{2,1,0:T(8,128)(2,1)}, bf16[2,1792,1024]{2,1,0:T(8,128)(2,1)}, bf16[2,1792,1024]{2,1,0:T(8,...) custom-call(s32[2]{0:T(128)} %len_ref.7, ...), custom_call_target="tpu_custom_call" | custom-call | tf_op jit(solution)/shard_map/enter/pallas_call | solution.py:825
  80.9 62.5 %middle.1 = (bf16[2,1024,768]{2,1,0:T(8,128)(2,1)}, bf16[2,1536,1024]{2,1,0:T(8,128)(2,1)}, bf16[2,1536,1024]{2,1,0:T(8,128)(2,1)}, f32[2,256,1024]{2,1,0:T(8,12...) custom-call(s32[2]{0:T(128)} %len_ref.7, ...), custom_call_target="tpu_custom_call" | custom-call | tf_op jit(solution)/shard_map/middle/pallas_call | solution.py:864
  143.4 32.5 %leave.1 = (bf16[2,1792,1024]{2,1,0:T(8,128)(2,1)}, bf16[2,48,1024]{2,1,0:T(8,128)(2,1)}, f32[8,1792]{1,0:T(8,128)}, f32[8,128]{1,0:T(8,128)}) custom-call(s32[2]{0:T(128)} %len_ref.7, bf16[2,1792,1024]{2,1,0:T(8,128)(2,1)} %get-tuple-element.63.filt_ref, bf16[2,1792,1024]{2,1,0:T(8,128)(2,1)} %get-tuple-element.56.act_ref, ...), custom_call_target="tpu_custom_call" | custom-call | tf_op jit(solution)/shard_map/leave/pallas_call | solution.py:911
  175.9 32.2 %widen.1 = (bf16[2,1024,768]{2,1,0:T(8,128)(2,1)}, bf16[26,8,96,128]{3,2,1,0:T(8,128)(2,1)}, bf16[2,8,96,128]{3,2,1,0:T(8,128)(2,1)}) custom-call(s32[2]{0:T(128)} %len_ref.7, bf16[2,1024,768]{2,1,0:T(8,128)(2,1)} %tok_ref.5, bf16[2,1024,768]{2,1,0:T(8,128)(2,1)} %cot_ref.3, bf16[2,1536,1024]{2,1,0:T(8,128)(2,1)} %get-tuple-element.62.dgate_ref, ...), custom_call_target="tpu_custom_call" | custom-call | tf_op jit(solution)/shard_map/widen/pallas_call | solution.py:948
  208.2 90.7 %reduce.1 = (bf16[2,2,2,5,96,128]{5,4,3,2,1,0:T(8,128)(2,1)}, f32[8,128]{1,0:T(8,128)}) custom-call(bf16[2,13,4,2,96,128]{5,4,3,2,1,0:T(8,128)(2,1)} %bitcast.17, bf16[2,6,4,2,96,128]{5,4,3,2,1,0:T(8,128)(2,1)} %bitcast.19, bf16[2,1,4,2,96,128]{5,4,3,2,1,0:T(8,128)(2,1)} %bitcast.20, f32[8,128]{1,0:T(8,128)} %get-tuple-element.79.heads_ref), custom_call_target="tpu_custom_call" | custom-call | tf_op jit(solution)/shard_map/reduce/pallas_call | solution.py:1226
  298.9 2.6 finish.1
